TPU v7x, 32 devices: a whole 2x2x4 slice. The times are simulated.
32 devices in a mesh: outer: 4 (over x, core), inner: 8 (over z, y).
Axes of the slice: x: 2, y: 2, z: 4, core: 2. Of those that a mesh axis runs over, the one named last changes fastest.
Arguments:
- tokens: bfloat16 [512, 3584], P(('outer', 'inner')), may hold values from -6 to 6
- experts: int32 [512, 8], P(('outer', 'inner')), may hold values from 0 to 31, as said below
- gate_score: int32 [512, 8], P(('outer', 'inner')), may hold values from 1 to 16
- expert_gate: bfloat16 [32, 3584, 1024], P(('outer', 'inner')), may hold values from -0.09375 to 0.09375
- expert_up: bfloat16 [32, 3584, 1024], P(('outer', 'inner')), may hold values from -0.09375 to 0.09375
- expert_down: bfloat16 [32, 1024, 3584], P(('outer', 'inner')), may hold values from -0.1875 to 0.1875
- shared_gate: bfloat16 [3584, 2048], P(None, 'inner'), may hold values from -0.09375 to 0.09375
- shared_up: bfloat16 [3584, 2048], P(None, 'inner'), may hold values from -0.09375 to 0.09375
- shared_down: bfloat16 [2048, 3584], P('inner'), may hold values from -0.125 to 0.125
Outputs:
- moe_out: bfloat16 [512, 3584], P(('outer', 'inner'))
Inputs may be any that keep to these rules, and one draw needn't show every extreme that they name: Each token names 8 different experts, exactly two in each of 4 different groups, where expert e lies in group e // 8. One group, drawn from the seed, is named by every token. The 16 tokens of one device name one expert at most 4 times, and name each expert of that group exactly 4 times.
All inputs are finite; a program needn't handle non-finite values.
Results may differ from a plain program's by a relative error of at most 0.012.
Values may be sent and summed in bfloat16 or wider, within the bound.
No kernel may reach another device: no remote copies, remote signals or barrier semaphores. Data moves between devices by JAX's collectives and lax.ppermute only.
A program may use at most 128 MiB of HBM per device.

v0:
```python
import jax
import jax.numpy as jnp
from jax import lax
from jax.sharding import PartitionSpec as P

TOPK = 8
TOP_GROUPS = 4


def gated_mlp(inputs, gate_matrix, up_matrix, down_matrix):
    gate_part = jnp.dot(inputs, gate_matrix, preferred_element_type=jnp.float32)
    up_part = jnp.dot(inputs, up_matrix, preferred_element_type=jnp.float32)
    hidden = (jax.nn.silu(gate_part) * up_part).astype(jnp.bfloat16)
    return jnp.dot(hidden, down_matrix, preferred_element_type=jnp.float32).astype(jnp.bfloat16)


def gate_weights(gate_score):
    values = gate_score.astype(jnp.float32)
    return 2.5 * values / jnp.sum(values, axis=-1, keepdims=True)


def group_rank(group_ids):
    slot_width = group_ids.shape[-1]
    same_group = group_ids[..., :, None] == group_ids[..., None, :]
    earlier = jnp.arange(slot_width)[None, :] < jnp.arange(slot_width)[:, None]
    return jnp.sum(jnp.logical_and(same_group, earlier), axis=-1)


def combine_pairs(pair_rows, pair_weights):
    values = pair_rows.astype(jnp.float32)
    mixed = (
        pair_weights[..., 0, None] * values[..., 0, :]
        + pair_weights[..., 1, None] * values[..., 1, :]
    )
    return mixed.astype(jnp.bfloat16)


def rank_slots(matches):
    named_mask = jnp.any(matches, axis=-2).astype(jnp.int32)
    earlier = jnp.cumsum(named_mask, axis=-2) - named_mask
    slot_ranks = jnp.sum(jnp.where(matches, earlier[..., None, :], 0), axis=-1)
    return (named_mask, earlier, slot_ranks)


def pair_tables(group_ids, slot_rank, slot_index, weights, group_count):
    wanted = jnp.arange(group_count, dtype=jnp.int32)
    in_group = group_ids[..., None, None, :] == wanted[:, None, None]
    in_place = slot_rank[..., None, None, :] == jnp.arange(2, dtype=jnp.int32)[None, :, None]
    picked = jnp.logical_and(in_group, in_place)
    chosen = jnp.sum(jnp.where(picked, slot_index[..., None, None, :], 0), axis=-1)
    present = jnp.any(picked, axis=-1)
    pair_weights = jnp.sum(jnp.where(picked, weights[..., None, None, :], 0.0), axis=-1)
    return (chosen, present, pair_weights)


def per_device(
    tokens,
    experts,
    gate_score,
    expert_gate,
    expert_up,
    expert_down,
    shared_gate,
    shared_up,
    shared_down,
):
    row_count = tokens.shape[0]
    model_width = tokens.shape[1]
    inner_count = lax.axis_size("inner")
    outer_count = lax.axis_size("outer")
    capacity = TOPK // TOP_GROUPS * row_count // inner_count
    gate_matrix = expert_gate[0]
    up_matrix = expert_up[0]
    down_matrix = expert_down[0]
    segment = lax.all_gather(tokens, "inner", axis=0, tiled=True)
    gate_part = jnp.dot(segment, shared_gate, preferred_element_type=jnp.float32)
    up_part = jnp.dot(segment, shared_up, preferred_element_type=jnp.float32)
    shared_hidden = (jax.nn.silu(gate_part) * up_part).astype(jnp.bfloat16)
    shared = lax.psum_scatter(
        jnp.dot(shared_hidden, shared_down, preferred_element_type=jnp.float32).astype(
            jnp.bfloat16
        ),
        "inner",
        scatter_dimension=0,
        tiled=True,
    ).astype(jnp.float32)
    weights = gate_weights(gate_score)
    group_ids = experts // inner_count
    slot_rank = group_rank(group_ids)
    total_count = inner_count * outer_count
    matches = experts[:, :, None] == jnp.arange(total_count, dtype=jnp.int32)[None, None, :]
    named_mask, earlier, slot_ranks = rank_slots(matches)
    slot_ids = jnp.arange(capacity, dtype=jnp.int32)[None, :, None]
    selector = jnp.logical_and(
        named_mask.T[:, None, :] == 1, earlier.T[:, None, :] == slot_ids
    ).astype(jnp.bfloat16)
    outbound = jnp.einsum(
        "ecr,rd->ecd", selector, tokens, preferred_element_type=jnp.float32
    ).astype(jnp.bfloat16)
    received = lax.all_to_all(outbound, ("outer", "inner"), split_axis=0, concat_axis=0, tiled=True)
    answer = gated_mlp(received.reshape(-1, model_width), gate_matrix, up_matrix, down_matrix)
    returned = lax.all_to_all(
        answer.reshape(received.shape), ("outer", "inner"), split_axis=0, concat_axis=0, tiled=True
    )
    flat_rows = returned.reshape(-1, model_width)
    slot_index = experts * capacity + slot_ranks
    chosen, present, pair_weights = pair_tables(
        group_ids, slot_rank, slot_index, weights, outer_count
    )
    pair_rows = jnp.where(present[..., None], flat_rows[chosen], jnp.zeros((), jnp.bfloat16))
    partial_value = combine_pairs(pair_rows, pair_weights)
    routed = jnp.sum(partial_value.astype(jnp.float32), axis=1)
    return (shared + routed).astype(jnp.bfloat16)


def solution(mesh):
    return jax.shard_map(
        per_device,
        mesh=mesh,
        in_specs=(
            P(("outer", "inner"), None),
            P(("outer", "inner"), None),
            P(("outer", "inner"), None),
            P(("outer", "inner"), None, None),
            P(("outer", "inner"), None, None),
            P(("outer", "inner"), None, None),
            P(None, "inner"),
            P(None, "inner"),
            P("inner", None),
        ),
        out_specs=P(("outer", "inner"), None),
        check_vma=False,
    )
```

profile of v0, /device:TPU:0, one launch (start us, length us, event | category | flops | bytes accessed | tf_op | source)
XLA Modules:
  0.0 144.2 jit_solution(463187441828471023)
XLA Ops:
  6.5 0.9 copy.54
  7.4 0.1 fusion.34
  7.6 1.3 convolution_convert_fusion
  8.9 1.6 %copy.55 = bf16[32,4,3584]{2,1,0:T(4,128)(2,1)} copy(bf16[32,4,3584]{2,0,1:T(8,128)(2,1)S(1)} %convolution_convert_fusion) | data formatting | bytes 1835008 | tf_op jit(solution)/shard_map/convert_element_type | solution.py:99
  10.6 7.4 %all-to-all-start = ((bf16[32,4,3584]{2,1,0:T(4,128)(2,1)}), bf16[32,4,3584]{2,1,0:T(4,128)(2,1)}, u32[]{:S(2)}, u32[]{:S(2)}) async-start(bf16[32,4,3584]{2,1,0:T(4,128)(2,1)} %copy.55), calls=%async_computation.1 | async-start | bytes 1835008 | tf_op jit(solution)/shard_map/all_to_all | solution.py:100
  18.0 0.0 reduce-scatter.2.cloned.1.call-start
  18.1 47.0 %all_gather.3 = bf16[128,3584]{1,0:T(8,128)(2,1)S(1)} all-gather(bf16[16,3584]{1,0:T(8,128)(2,1)S(1)} %copy-done.1), channel_id=1, replica_groups=mesh['outer'=4,'inner'=8] {'inner'}, dimensions={0}, use_global_device_ids=true | all-gather | bytes 1032192 | tf_op jit(solution)/shard_map/all_gather | solution.py:75
  65.0 1.9 %fusion.48 = f32[128,256]{1,0:T(8,128)S(1)} fusion(bf16[128,3584]{1,0:T(8,128)(2,1)S(1)} %all_gather.3, bf16[3584,256]{1,0:T(8,128)(2,1)} %param.15), kind=kOutput, calls=%fused_computation.70 | convolution fusion | flops 234881024 | bytes 2883584 | tf_op jit(solution)/shard_map/dot_general | solution.py:76
  67.0 3.6 %convolution_convert_fusion.1 = bf16[128,3584]{1,0:T(8,128)(2,1)} fusion(bf16[256,3584]{1,0:T(8,128)(2,1)S(1)} %copy-done, bf16[128,3584]{1,0:T(8,128)(2,1)S(1)} %all_gather.3, bf16[3584,256]{1,0:T(8,128)(2,1)} %param.16, f32[128,256]{1,0:T(8,128)S(1)} %fusion.48), kind=kOutput, calls=%fused_computation.9 | convolution fusion | flops 470417408 | bytes 5636096 | tf_op jit(solution)/shard_map/dot_general | solution.py:80
  70.6 0.0 reduce-scatter.2.cloned.1.call-update
  70.6 0.4 select_reduce_fusion
  71.0 0.1 copy.56
  71.1 1.7 %reshape.66 = bf16[128,3584]{1,0:T(8,128)(2,1)S(1)} reshape(bf16[32,4,3584]{2,1,0:T(4,128)(2,1)} %all-to-all-done) | data formatting | bytes 1835008 | tf_op jit(solution)/shard_map/reshape | solution.py:101
  72.8 4.2 %fusion.4 = f32[128,1024]{1,0:T(8,128)S(1)} fusion(bf16[128,3584]{1,0:T(8,128)(2,1)S(1)} %reshape.66, bf16[1,3584,1024]{2,1,0:T(8,128)(2,1)} %param.12), kind=kOutput, calls=%fused_computation.5 | convolution fusion | flops 939524096 | bytes 8781824 | tf_op jit(solution)/shard_map/dot_general | solution.py:11
  77.0 8.3 %fusion.6 = bf16[128,3584]{1,0:T(8,128)(2,1)} fusion(bf16[1,1024,3584]{2,1,0:T(8,128)(2,1)} %param.14, bf16[128,3584]{1,0:T(8,128)(2,1)S(1)} %reshape.66, bf16[1,3584,1024]{2,1,0:T(8,128)(2,1)} %param.13, f32[128,1024]{1,0:T(8,128)S(1)} %fusion.4), kind=kOutput, calls=%fused_computation.7 | convolution fusion | flops 1880293376 | bytes 17039360 | tf_op jit(solution)/shard_map/dot_general | solution.py:14
  85.3 2.5 %reshape.67 = bf16[32,4,3584]{2,1,0:T(4,128)(2,1)} reshape(bf16[128,3584]{1,0:T(8,128)(2,1)} %fusion.6) | data formatting | bytes 1835008 | tf_op jit(solution)/shard_map/reshape | solution.py:103
  87.8 3.8 %all-to-all-start.1 = ((bf16[32,4,3584]{2,1,0:T(4,128)(2,1)}), bf16[32,4,3584]{2,1,0:T(4,128)(2,1)}, u32[]{:S(2)}, u32[]{:S(2)}) async-start(bf16[32,4,3584]{2,1,0:T(4,128)(2,1)} %reshape.67), calls=%async_computation.2 | async-start | bytes 1835008 | tf_op jit(solution)/shard_map/all_to_all | solution.py:102
  91.6 0.1 convert_reduce_fusion.1
  91.8 0.1 copy.58
  91.9 0.1 reshape.71
  92.1 0.1 copy.53
  92.3 0.1 copy.52
  92.4 0.1 copy.60
  92.5 25.0 %all-to-all-done.1 = bf16[32,4,3584]{2,1,0:T(4,128)(2,1)} async-done(((bf16[32,4,3584]{2,1,0:T(4,128)(2,1)}), bf16[32,4,3584]{2,1,0:T(4,128)(2,1)}, u32[]{:S(2)}, u32[]{:S(2)}) %all-to-all-start.1) | async-done | bytes 917536 | tf_op jit(solution)/shard_map/all_to_all | solution.py:102
  117.5 1.7 %reshape.68 = bf16[128,3584]{1,0:T(8,128)(2,1)S(1)} reshape(bf16[32,4,3584]{2,1,0:T(4,128)(2,1)} %all-to-all-done.1) | data formatting | bytes 1835008 | tf_op jit(solution)/shard_map/reshape | solution.py:105
  119.1 2.1 %gather_fusion = bf16[128,3584]{1,0:T(8,128)(2,1)} fusion(bf16[128,3584]{1,0:T(8,128)(2,1)S(1)} %reshape.68, s32[1024]{0:T(1024)S(1)} %pad_clamp_fusion), kind=kCustom, calls=%fused_computation | custom fusion | bytes 1835520 | tf_op jit(solution)/shard_map/gather | solution.py:110
  121.2 2.3 %reshape.70 = bf16[16,4,2,3584]{3,2,1,0:T(2,128)(2,1)S(1)} reshape(bf16[128,3584]{1,0:T(8,128)(2,1)} %gather_fusion) | data formatting | bytes 1835008 | tf_op jit(solution)/shard_map/gather | solution.py:110
  123.6 0.8 fusion.16
  124.4 1.4 fusion.46
  125.8 0.9 convert_reduce_fusion
  126.7 9.1 %reduce-scatter.2.cloned.1.call-done = bf16[16,3584]{1,0:T(8,128)(2,1)} async-done(((bf16[128,3584]{1,0:T(8,128)(2,1)}), bf16[16,3584]{1,0:T(8,128)(2,1)}) %reduce-scatter.2.cloned.1.call-update) | async-done | bytes 114704 | tf_op jit(solution)/shard_map/reduce_scatter | solution.py:79
  135.8 1.6 %add_convert_fusion = bf16[16,3584]{1,0:T(8,128)(2,1)} fusion(f32[16,3584]{1,0:T(8,128)S(1)} %convert_reduce_fusion, bf16[16,3584]{1,0:T(8,128)(2,1)} %reduce-scatter.2.cloned.1.call-done), kind=kLoop, calls=%fused_computation.28 | loop fusion | flops 172032 | bytes 458752 | tf_op jit(solution)/shard_map/convert_element_type | solution.py:113
  (24 shorter events, 0.2 us)
Async XLA Ops:
  6.5 60.4 %copy-start = (bf16[256,3584]{1,0:T(8,128)(2,1)S(1)}, bf16[256,3584]{1,0:T(8,128)(2,1)}, u32[]{:S(2)}) copy-start(bf16[256,3584]{1,0:T(8,128)(2,1)} %param.17) | copy-start | bytes 5505028
  8.9 9.1 %copy-start.1 = (bf16[16,3584]{1,0:T(8,128)(2,1)S(1)}, bf16[16,3584]{1,0:T(8,128)(2,1)}, u32[]{:S(2)}) copy-start(bf16[16,3584]{1,0:T(8,128)(2,1)} %param.9) | copy-start | bytes 344068
  10.6 60.5 %all-to-all-start = ((bf16[32,4,3584]{2,1,0:T(4,128)(2,1)}), bf16[32,4,3584]{2,1,0:T(4,128)(2,1)}, u32[]{:S(2)}, u32[]{:S(2)}) async-start(bf16[32,4,3584]{2,1,0:T(4,128)(2,1)} %copy.55), calls=%async_computation.1 | async-start | bytes 1835008 | tf_op jit(solution)/shard_map/all_to_all | solution.py:100
  18.0 117.8 %reduce-scatter.2.cloned.1.call-start = ((), (), s32[]{:S(2)}) async-start(), calls=%async_computation.3 | async-start | bytes 1032192 | tf_op jit(solution)/shard_map/reduce_scatter | solution.py:79
  67.0 4.1 %copy-start.2 = (s32[16,8]{0,1:T(8,128)S(1)}, s32[16,8]{0,1:T(8,128)}, u32[]{:S(2)}) copy-start(s32[16,8]{0,1:T(8,128)} %param.10) | copy-start | bytes 1540
  85.3 6.9 %copy-start.3 = (s32[16,8]{0,1:T(8,128)S(1)}, s32[16,8]{0,1:T(8,128)}, u32[]{:S(2)}) copy-start(s32[16,8]{0,1:T(8,128)} %param.11) | copy-start | bytes 1540
  87.8 29.6 %all-to-all-start.1 = ((bf16[32,4,3584]{2,1,0:T(4,128)(2,1)}), bf16[32,4,3584]{2,1,0:T(4,128)(2,1)}, u32[]{:S(2)}, u32[]{:S(2)}) async-start(bf16[32,4,3584]{2,1,0:T(4,128)(2,1)} %reshape.67), calls=%async_computation.2 | async-start | bytes 1835008 | tf_op jit(solution)/shard_map/all_to_all | solution.py:102
Sparse Core Ops, SparseCore 0:
  70.7 64.9 reduce-scatter.1
where the time goes:
time: 145 us; the launch traced here: 144 us
  blocking collectives  47 us (32%)
  waiting for transfers between devices  34.1 us (24%)
  matrix products  19.3 us (13%)
  local copies, waits for them, and re-layouts  14.9 us (10%)
  between operations  13.6 us (9%)
  starting transfers between devices  11.2 us (8%)
  other arithmetic  4.04 us (3%)
    all_gather x1, blocking collectives, per_device(): segment = lax.all_gather(tokens, 'inner', axis=0, tiled=True)  47 us
    all_to_all x1, waiting for transfers between devices, per_device(): lax.all_to_all(answer.reshape(received.shape), ('outer', 'inner'), split_...  25 us
    reduce_scatter x1, waiting for transfers between devices, per_device(): lax.psum_scatter(jnp.dot(shared_hidden, shared_down, preferred_element_ty...  9.08 us
    dot_general x1, matrix products, gated_mlp(): jnp.dot(hidden, down_matrix, preferred_element_type=jnp.float32)  8.28 us
    all_to_all x1, starting transfers between devices, per_device(): lax.all_to_all(outbound, ('outer', 'inner'), split_axis=0, concat_axis=0,...  7.4 us
    gather x2, local copies, waits for them, and re-layouts, per_device(): flat_rows[chosen]  4.43 us
    dot_general x1, matrix products, gated_mlp(): gate_part = jnp.dot(inputs, gate_matrix, preferred_element_type=jnp.float32)  4.2 us
    all_to_all x1, starting transfers between devices, per_device(): lax.all_to_all(answer.reshape(received.shape), ('outer', 'inner'), split_...  3.78 us
  transfers between devices with their start and end apart: 3, of which 2 were waited for; matrix products, arithmetic and copies ran while one was open for 23% of the time, Pallas kernels for 0%

commit v1 on v0

v1 whole, which is shorter than its diff:
```python
import functools

import jax
import jax.numpy as jnp
from jax import lax
from jax.experimental import pallas as pl
from jax.experimental.pallas import tpu as pltpu
from jax.sharding import PartitionSpec as P

TOPK = 8
TOP_GROUPS = 4
LANES = 128
DEPTH_Z = 4
IN_CUTS = 2
OUT_CUTS = 2
BOTH = ("outer", "inner")
BF16 = jnp.bfloat16
F32 = jnp.float32
PARAMS = pltpu.CompilerParams(vmem_limit_bytes=48 * 1024 * 1024)


def dot(a, b):
    return jnp.dot(a, b, preferred_element_type=F32)


def dot_first(a, b):
    return lax.dot_general(a, b, (((0,), (0,)), ((), ())), preferred_element_type=F32)


def whole(shape, dtype):
    return jax.ShapeDtypeStruct(shape, dtype)


def prepare_kernel(width, tokens_ref, experts_ref, score_ref, *outs):
    names = jnp.concatenate([experts_ref[...], score_ref[...]], axis=0).astype(F32).astype(BF16)
    slots = names.shape[0]
    row = lax.broadcasted_iota(jnp.int32, (slots, LANES), 0)
    col = lax.broadcasted_iota(jnp.int32, (slots, LANES), 1)
    spread = jnp.where(row == col, 1.0, 0.0).astype(BF16)
    for at, out in enumerate(outs):
        out[:, :width] = tokens_ref[:, at * width:(at + 1) * width]
    outs[0][:, width:] = dot_first(names, spread).astype(BF16)


def route_kernel(width, block_rows, capacity, inner_count, blocks, where_ref, *refs):
    pieces, (place_ref, high_ref, low_ref), outs = refs[:blocks], refs[blocks:blocks + 3], refs[blocks + 3:]
    meta = jnp.concatenate([piece[:, width:] for piece in pieces], axis=0).astype(F32)
    token_count = meta.shape[0]
    outer_at, inner_at = where_ref[0], where_ref[1]
    send_rows = inner_count * capacity
    total = send_rows * len(outs)
    slot = lax.broadcasted_iota(jnp.int32, (1, total), 1)
    part = lax.div(slot, jnp.int32(send_rows))
    expert = ((outer_at ^ part) * inner_count + inner_at).astype(F32)
    scores = meta[:, TOPK:2 * TOPK]
    weights = 2.5 * scores / jnp.sum(scores, axis=1, keepdims=True)
    named = jnp.zeros((token_count, total), F32)
    weight = jnp.zeros((token_count, total), F32)
    for k in range(TOPK):
        match = meta[:, k:k + 1] == expert
        named = jnp.where(match, 1.0, named)
        weight = jnp.where(match, weights[:, k:k + 1], weight)
    row = lax.broadcasted_iota(jnp.int32, (token_count, token_count), 0)
    col = lax.broadcasted_iota(jnp.int32, (token_count, token_count), 1)
    rows_each = jnp.int32(block_rows)
    before = jnp.logical_and(lax.div(row, rows_each) == lax.div(col, rows_each), col < row)
    rank = dot(jnp.where(before, 1.0, 0.0).astype(BF16), named.astype(BF16))
    owner = lax.div(lax.broadcasted_iota(jnp.int32, (token_count, 1), 0), rows_each)
    wanted = (slot - part * send_rows - owner * capacity).astype(F32)
    hit = jnp.logical_and(jnp.logical_and(rank == wanted, rank < float(capacity)), named > 0.5)
    place = jnp.where(hit, 1.0, 0.0).astype(BF16)
    place_ref[...] = place
    weight = jnp.where(hit, weight, 0.0)
    high = weight.astype(BF16)
    high_ref[...] = high
    low_ref[...] = (weight - high.astype(F32)).astype(BF16)
    send_selected(width, place, pieces, outs)


def send_selected(width, place, pieces, outs):
    rows = pieces[0].shape[0]
    chosen = sum(
        dot_first(place[at * rows:(at + 1) * rows], piece[:, :width]) for at, piece in enumerate(pieces)
    ).astype(BF16)
    send_rows = outs[0].shape[0]
    for at, out in enumerate(outs):
        out[...] = chosen[at * send_rows:(at + 1) * send_rows]


def select_kernel(width, blocks, place_ref, *refs):
    send_selected(width, place_ref[...], refs[:blocks], refs[blocks:])


def hidden_kernel(blocks, steps, last, *refs):
    pieces = refs[:blocks]
    gate_ref, up_ref = refs[blocks:blocks + 2]
    rest = refs[blocks + 2:]
    step = pl.program_id(0)
    if last:
        gate_in, up_in = rest[:-3] if len(rest) == 5 else (None, None)
        out_ref, gate_sum, up_sum = rest[-3:]
    else:
        gate_in, up_in = rest[:-2] if len(rest) == 4 else (None, None)
        gate_sum, up_sum = rest[-2:]

    @pl.when(step == 0)
    def _():
        if gate_in is None:
            gate_sum[...] = jnp.zeros_like(gate_sum)
            up_sum[...] = jnp.zeros_like(up_sum)
        else:
            gate_sum[...] = gate_in[...]
            up_sum[...] = up_in[...]

    rows = jnp.concatenate([piece[...] for piece in pieces], axis=0)
    gate_sum[...] += dot(rows, gate_ref[...])
    up_sum[...] += dot(rows, up_ref[...])
    if last:

        @pl.when(step == steps - 1)
        def _():
            gate = gate_sum[...]
            out_ref[...] = (gate / (1.0 + jnp.exp(-gate)) * up_sum[...]).astype(BF16)


def hidden(pieces, gate, up, start, width, sums, last):
    blocks = len(pieces)
    token_count = sum(piece.shape[0] for piece in pieces)
    units = gate.shape[1]
    step_width = width // 2 if width // 2 % LANES == 0 else width
    steps = width // step_width
    first = start // step_width
    sum_spec = pl.BlockSpec((token_count, units), lambda s: (0, 0))
    weight_spec = pl.BlockSpec((step_width, units), lambda s: (first + s, 0))
    in_specs = [pl.BlockSpec((piece.shape[0], step_width), lambda s: (0, s)) for piece in pieces]
    in_specs += [weight_spec, weight_spec] + [sum_spec] * len(sums)
    scratch = [pltpu.VMEM((token_count, units), F32)] * 2 if last else []
    if last:
        out_shape, out_specs = whole((token_count, units), BF16), sum_spec
    else:
        out_shape, out_specs = [whole((token_count, units), F32)] * 2, [sum_spec] * 2
    return pl.pallas_call(
        functools.partial(hidden_kernel, blocks, steps, last),
        grid=(steps,),
        in_specs=in_specs,
        out_specs=out_specs,
        out_shape=out_shape,
        scratch_shapes=scratch,
        compiler_params=PARAMS,
    )(*pieces, gate, up, *sums)


def down_kernel(hidden_ref, down_ref, *outs):
    answer = dot(hidden_ref[...], down_ref[...]).astype(BF16)
    rows = outs[0].shape[0]
    for at, out in enumerate(outs):
        out[...] = answer[at * rows:(at + 1) * rows]


def down(rows, matrix, start, width, blocks):
    step_width = width // 2 if width // 2 % LANES == 0 else width
    first = start // step_width
    row_count, units = rows.shape
    each = row_count // blocks
    return pl.pallas_call(
        down_kernel,
        grid=(width // step_width,),
        in_specs=[
            pl.BlockSpec((row_count, units), lambda s: (0, 0)),
            pl.BlockSpec((units, step_width), lambda s: (0, first + s)),
        ],
        out_specs=[pl.BlockSpec((each, step_width), lambda s: (0, s))] * blocks,
        out_shape=[whole((each, width), BF16)] * blocks,
        compiler_params=PARAMS,
    )(rows, matrix)


def combine_kernel(blocks, hidden_ref, down_ref, high_ref, low_ref, *refs):
    answers, keep_ref, outs = refs[:blocks], refs[blocks], refs[blocks + 1:]
    rows = jnp.concatenate([answer[...] for answer in answers], axis=0)
    total = dot(hidden_ref[...], down_ref[...]) + dot(high_ref[...], rows) + dot(low_ref[...], rows)
    each = keep_ref.shape[0]
    keep_ref[...] = total[:each]
    for at, out in enumerate(outs):
        out[...] = total[(at + 1) * each:(at + 2) * each].astype(BF16)


def combine(shared_hidden, shared_down, high, low, answers, start, width, sends):
    token_count, units = shared_hidden.shape
    each = token_count // (sends + 1)
    full = lambda array: pl.BlockSpec(array.shape, lambda s: (0, 0))
    at = start // width
    return pl.pallas_call(
        functools.partial(combine_kernel, len(answers)),
        grid=(1,),
        in_specs=[full(shared_hidden), pl.BlockSpec((units, width), lambda s: (0, at)), full(high), full(low)]
        + [full(answer) for answer in answers],
        out_specs=[pl.BlockSpec((each, width), lambda s: (0, 0))] * (sends + 1),
        out_shape=[whole((each, width), F32)] + [whole((each, width), BF16)] * sends,
        compiler_params=PARAMS,
    )(shared_hidden, shared_down, high, low, *answers)


def add_kernel(blocks, kept_ref, *refs):
    arrived, outs = refs[:blocks], refs[blocks:]
    total = kept_ref[...]
    for block in arrived:
        total = total + block[...].astype(F32)
    each = outs[0].shape[0]
    for at, out in enumerate(outs):
        out[...] = total[at * each:(at + 1) * each].astype(out.dtype)


def finish_kernel(blocks, width, *refs):
    out_ref = refs[-1]
    for at in range((len(refs) - 1) // blocks):
        group = refs[at * blocks:(at + 1) * blocks]
        total = group[0][...]
        for block in group[1:]:
            total = total + block[...].astype(F32)
        out_ref[:, at * width:(at + 1) * width] = total.astype(BF16)


def call(kernel, out_shape, *args, in_specs=None):
    extra = {} if in_specs is None else {"in_specs": in_specs}
    return pl.pallas_call(kernel, out_shape=out_shape, compiler_params=PARAMS, **extra)(*args)


def per_device(
    tokens,
    experts,
    gate_score,
    expert_gate,
    expert_up,
    expert_down,
    shared_gate,
    shared_up,
    shared_down,
):
    rows, model_width = tokens.shape
    inner_count = lax.axis_size("inner")
    outer_count = lax.axis_size("outer")
    depth_y = inner_count // DEPTH_Z
    capacity = TOPK // TOP_GROUPS * rows // inner_count
    send_rows = inner_count * capacity
    device_count = inner_count * outer_count
    where = jnp.stack([lax.axis_index("outer"), lax.axis_index("inner")]).astype(jnp.int32)

    def swap(array, distance):
        return lax.ppermute(array, BOTH, [(at, at ^ distance) for at in range(device_count)])

    def along_z(k):
        return k * depth_y

    def along_outer(k):
        return k * inner_count

    in_width = model_width // IN_CUTS
    out_width = model_width // OUT_CUTS

    sent = call(
        functools.partial(prepare_kernel, in_width),
        [whole((rows, in_width + (LANES if at == 0 else 0)), BF16) for at in range(IN_CUTS)],
        tokens,
        experts.T,
        gate_score.T,
    )
    columns = []
    for piece in sent:
        columns.append(jnp.concatenate([piece] + [swap(piece, along_z(k)) for k in range(1, DEPTH_Z)], axis=0))
    segments = []
    for column in columns:
        segments.append([column] + [swap(column, k) for k in range(1, depth_y)])

    token_count = rows * inner_count
    table = (token_count, device_count * capacity)
    arrived = []
    sums = []
    for at, segment in enumerate(segments):
        send_shapes = [whole((send_rows, in_width), BF16)] * outer_count
        if at == 0:
            place, high, low, *blocks = call(
                functools.partial(route_kernel, in_width, rows, capacity, inner_count, depth_y),
                [whole(table, BF16)] * 3 + send_shapes,
                where,
                *segment,
                in_specs=[pl.BlockSpec(memory_space=pltpu.SMEM)]
                + [pl.BlockSpec(memory_space=pltpu.VMEM)] * depth_y,
            )
        else:
            blocks = call(
                functools.partial(select_kernel, in_width, depth_y), send_shapes, place, *segment
            )
        arrived.append([blocks[0]] + [swap(blocks[k], along_outer(k)) for k in range(1, outer_count)])
    shared_sums = []
    for at, segment in enumerate(segments):
        shared_sums = hidden(
            segment, shared_gate, shared_up, at * in_width, in_width, shared_sums, at == IN_CUTS - 1
        )
    shared_hidden = shared_sums
    for at, blocks in enumerate(arrived):
        sums = hidden(
            blocks, expert_gate[0], expert_up[0], at * in_width, in_width, sums, at == IN_CUTS - 1
        )
    expert_hidden = sums

    finals = []
    for at in range(OUT_CUTS):
        start = at * out_width
        blocks = down(expert_hidden, expert_down[0], start, out_width, outer_count)
        answers = [blocks[0]] + [swap(blocks[k], along_outer(k)) for k in range(1, outer_count)]
        kept, *leaving = combine(
            shared_hidden, shared_down, high, low, answers, start, out_width, depth_y - 1
        )
        coming = [swap(block, k + 1) for k, block in enumerate(leaving)]
        kept, *leaving = call(
            functools.partial(add_kernel, depth_y - 1),
            [whole((rows, out_width), F32)] + [whole((rows, out_width), BF16)] * (DEPTH_Z - 1),
            kept,
            *coming,
        )
        finals += [kept] + [swap(block, along_z(k + 1)) for k, block in enumerate(leaving)]
    return call(
        functools.partial(finish_kernel, DEPTH_Z, out_width), whole((rows, model_width), BF16), *finals
    )


def solution(mesh):
    return jax.shard_map(
        per_device,
        mesh=mesh,
        in_specs=(
            P(("outer", "inner"), None),
            P(("outer", "inner"), None),
            P(("outer", "inner"), None),
            P(("outer", "inner"), None, None),
            P(("outer", "inner"), None, None),
            P(("outer", "inner"), None, None),
            P(None, "inner"),
            P(None, "inner"),
            P("inner", None),
        ),
        out_specs=P(("outer", "inner"), None),
        check_vma=False,
    )
```

time: 145 us -> 79.7 us (0.55)
  blocking collectives: 47 us -> 0 us
  starting transfers between devices: 11.2 us -> 33.3 us
  matrix products: 19.3 us -> 0 us
  Pallas kernels: 0 us -> 18.8 us
  between operations: 13.6 us -> 0.21 us
  local copies, waits for them, and re-layouts: 14.9 us -> 2.35 us
  waiting for transfers between devices: 34.1 us -> 24.7 us
  other arithmetic: 4.04 us -> 0.07 us
    all_gather x1 -> x0, blocking collectives: 47 us -> none  [per_device(): segment = lax.all_gather(tokens, 'inner', axis=0, tiled=True)]
    ppermute x0 -> x28, starting transfers between devices: none -> 33.3 us  [swap(): lax.ppermute(array, BOTH, [(at, at ^ distance) for at in range(device_cou...]
    all_to_all x2 -> x0, waiting for transfers between devices: 25 us -> none  [the longest x1 25 us: per_device(): lax.all_to_all(answer.reshape(received.shape), ('outer', 'inner'), split_...]
    ppermute x0 -> x28, waiting for transfers between devices: none -> 24.7 us  [swap(): lax.ppermute(array, BOTH, [(at, at ^ distance) for at in range(device_cou...]
    dot_general x5 -> x0, matrix products: 19.3 us -> none  [the longest x1 8.28 us: gated_mlp(): jnp.dot(hidden, down_matrix, preferred_element_type=jnp.float32)]
    pallas_call x0 -> x14, Pallas kernels: none -> 18.8 us  [the longest x4 9.69 us: hidden(): pl.pallas_call(functools.partial(hidden_kernel, blocks, steps, last), gri...]
    all_to_all x2 -> x0, starting transfers between devices: 11.2 us -> none  [the longest x1 7.4 us: per_device(): lax.all_to_all(outbound, ('outer', 'inner'), split_axis=0, concat_axis=0,...]
    reduce_scatter x1 -> x0, waiting for transfers between devices: 9.08 us -> none  [per_device(): lax.psum_scatter(jnp.dot(shared_hidden, shared_down, preferred_element_ty...]
  transfers between devices with their start and end apart: 3 -> 28, of which waited for: 2 -> 15; matrix products, arithmetic and copies ran while one was open for 23% -> 0% of each run, Pallas kernels for 0% -> 14%
where the time goes in v1:
time: 79.7 us; the launch traced here: 79.5 us
  starting transfers between devices  33.3 us (42%)
  waiting for transfers between devices  24.7 us (31%)
  Pallas kernels  18.8 us (24%)
  local copies, waits for them, and re-layouts  2.35 us (3%)
    ppermute x28, starting transfers between devices, swap(): lax.ppermute(array, BOTH, [(at, at ^ distance) for at in range(device_cou...  33.3 us
    ppermute x28, waiting for transfers between devices, swap(): lax.ppermute(array, BOTH, [(at, at ^ distance) for at in range(device_cou...  24.7 us
    pallas_call x4, Pallas kernels, hidden(): pl.pallas_call(functools.partial(hidden_kernel, blocks, steps, last), gri...  9.69 us
    pallas_call x2, Pallas kernels, down(): pl.pallas_call(down_kernel, grid=(width // step_width,), in_specs=[pl.Blo...  5.38 us
    pallas_call x6, Pallas kernels, call(): pl.pallas_call(kernel, out_shape=out_shape, compiler_params=PARAMS, **extra)  2.75 us
    unnamed x18, local copies, waits for them, and re-layouts  2.33 us
  transfers between devices with their start and end apart: 28, of which 15 were waited for; matrix products, arithmetic and copies ran while one was open for 0% of the time, Pallas kernels for 14%

profile of v1, /device:TPU:0, one launch (start us, length us, event | category | flops | bytes accessed | tf_op | source)
XLA Modules:
  0.0 79.5 jit_solution(9676758275858191169)
XLA Ops:
  0.0 0.9 %copy-done.3 = bf16[16,3584]{1,0:T(8,128)(2,1)S(1)} copy-done((bf16[16,3584]{1,0:T(8,128)(2,1)S(1)}, bf16[16,3584]{1,0:T(8,128)(2,1)}, u32[]{:S(2)}) %copy-start.3) | copy-done | bytes 114712
  2.4 5.0 %collective-permute-start.2 = (bf16[16,1792]{1,0:T(8,128)(2,1)S(1)}, bf16[16,1792]{1,0:T(8,128)(2,1)S(1)}, u32[]{:S(2)}, u32[]{:S(2)}) collective-permute-start(bf16[16,1792]{1,0:T(8,128)(2,1)S(1)} %get-tuple-element.42), channel_id=1, source_target_pairs={{0,6},{1,7},{2,4},{3,5},{4,2},{5,3},{6,0},{7,1},{8,14},{9,15},{10,... | collective-permute-start | bytes 172040 | tf_op jit(solution)/shard_map/ppermute | solution.py:250
  8.1 3.8 %collective-permute-start.6 = (bf16[16,1920]{1,0:T(8,128)(2,1)S(1)}, bf16[16,1920]{1,0:T(8,128)(2,1)S(1)}, u32[]{:S(2)}, u32[]{:S(2)}) collective-permute-start(bf16[16,1920]{1,0:T(8,128)(2,1)S(1)} %get-tuple-element.43), channel_id=1, source_target_pairs={{0,6},{1,7},{2,4},{3,5},{4,2},{5,3},{6,0},{7,1},{8,14},{9,15},{10,... | collective-permute-start | bytes 184328 | tf_op jit(solution)/shard_map/ppermute | solution.py:250
  11.9 1.9 %collective-permute-start.4 = (bf16[16,1920]{1,0:T(8,128)(2,1)S(1)}, bf16[16,1920]{1,0:T(8,128)(2,1)S(1)}, u32[]{:S(2)}, u32[]{:S(2)}) collective-permute-start(bf16[16,1920]{1,0:T(8,128)(2,1)S(1)} %get-tuple-element.43), channel_id=1, source_target_pairs={{0,2},{1,3},{2,0},{3,1},{4,6},{5,7},{6,4},{7,5},{8,10},{9,11},{10,... | collective-permute-start | bytes 184328 | tf_op jit(solution)/shard_map/ppermute | solution.py:250
  13.8 2.2 %collective-permute-done.1 = bf16[16,1792]{1,0:T(8,128)(2,1)S(1)} collective-permute-done((bf16[16,1792]{1,0:T(8,128)(2,1)S(1)}, bf16[16,1792]{1,0:T(8,128)(2,1)S(1)}, u32[]{:S(2)}, u32[]{:S(2)}) %collective-permute-start.1) | collective-permute-done | bytes 57376 | tf_op jit(solution)/shard_map/ppermute | solution.py:250
  16.0 0.9 %collective-permute-done.4 = bf16[16,1920]{1,0:T(8,128)(2,1)S(1)} collective-permute-done((bf16[16,1920]{1,0:T(8,128)(2,1)S(1)}, bf16[16,1920]{1,0:T(8,128)(2,1)S(1)}, u32[]{:S(2)}, u32[]{:S(2)}) %collective-permute-start.4) | collective-permute-done | bytes 61472 | tf_op jit(solution)/shard_map/ppermute | solution.py:250
  17.8 1.6 %collective-permute-start.7 = (bf16[64,1920]{1,0:T(8,128)(2,1)S(1)}, bf16[64,1920]{1,0:T(8,128)(2,1)S(1)}, u32[]{:S(2)}, u32[]{:S(2)}) collective-permute-start(bf16[64,1920]{1,0:T(8,128)(2,1)S(1)} %constant_dynamic-update-slice_fusion.4.refs_0_), channel_id=1, source_target_pairs={{0,1},{1,0},{2,3},{3,2},{4,5},{5,4},{6,7},{7,6},{8,9},{9,8},{10,11... | collective-permute-start | bytes 737288 | tf_op jit(solution)/shard_map/ppermute | solution.py:250
  20.0 6.7 %collective-permute-done.7.refs_1_ = bf16[64,1920]{1,0:T(8,128)(2,1)S(1)} collective-permute-done((bf16[64,1920]{1,0:T(8,128)(2,1)S(1)}, bf16[64,1920]{1,0:T(8,128)(2,1)S(1)}, u32[]{:S(2)}, u32[]{:S(2)}) %collective-permute-start.7) | collective-permute-done | bytes 245792 | tf_op jit(solution)/shard_map/ppermute | solution.py:250
  26.8 1.4 %shard_map.94 = (bf16[128,128]{1,0:T(8,128)(2,1)S(1)}, bf16[128,128]{1,0:T(8,128)(2,1)S(1)}, bf16[128,128]{1,0:T(8,128)(2,1)S(1)}, bf16[32,1792]{1,0:T(8,128)(2,...) custom-call(s32[2]{0:T(128)S(1)} %pad_add_fusion.where_ref, ...), custom_call_target="tpu_custom_call" | custom-call | tf_op jit(solution)/shard_map/pallas_call | solution.py:226
  28.2 1.6 %collective-permute-start.12 = (bf16[32,1792]{1,0:T(8,128)(2,1)S(1)}, bf16[32,1792]{1,0:T(8,128)(2,1)S(1)}, u32[]{:S(2)}, u32[]{:S(2)}) collective-permute-start(bf16[32,1792]{1,0:T(8,128)(2,1)S(1)} %get-tuple-element.55), channel_id=1, source_target_pairs={{0,16},{1,17},{2,18},{3,19},{4,20},{5,21},{6,22},{7,23},{8,24},{9,... | collective-permute-start | bytes 344072 | tf_op jit(solution)/shard_map/ppermute | solution.py:250
  30.9 1.5 %collective-permute-start.9 = (bf16[32,1792]{1,0:T(8,128)(2,1)S(1)}, bf16[32,1792]{1,0:T(8,128)(2,1)S(1)}, u32[]{:S(2)}, u32[]{:S(2)}) collective-permute-start(bf16[32,1792]{1,0:T(8,128)(2,1)S(1)} %get-tuple-element.51), channel_id=1, source_target_pairs={{0,16},{1,17},{2,18},{3,19},{4,20},{5,21},{6,22},{7,23},{8,24},{9,... | collective-permute-start | bytes 344072 | tf_op jit(solution)/shard_map/ppermute | solution.py:250
  32.4 1.8 %collective-permute-done.12.refs_2_ = bf16[32,1792]{1,0:T(8,128)(2,1)S(1)} collective-permute-done((bf16[32,1792]{1,0:T(8,128)(2,1)S(1)}, bf16[32,1792]{1,0:T(8,128)(2,1)S(1)}, u32[]{:S(2)}, u32[]{:S(2)}) %collective-permute-start.12) | collective-permute-done | bytes 114720 | tf_op jit(solution)/shard_map/ppermute | solution.py:250
  34.2 1.6 %collective-permute-done.13.refs_3_ = bf16[32,1792]{1,0:T(8,128)(2,1)S(1)} collective-permute-done((bf16[32,1792]{1,0:T(8,128)(2,1)S(1)}, bf16[32,1792]{1,0:T(8,128)(2,1)S(1)}, u32[]{:S(2)}, u32[]{:S(2)}) %collective-permute-start.13) | collective-permute-done | bytes 114720 | tf_op jit(solution)/shard_map/ppermute | solution.py:250
  35.8 3.9 %shard_map.96 = (f32[128,1024]{1,0:T(8,128)S(1)}, f32[128,1024]{1,0:T(8,128)S(1)}) custom-call(bf16[32,1792]{1,0:T(8,128)(2,1)S(1)} %get-tuple-element.53.refs_0_, bf16[32,1792]{1,0:T(8,128)(2,1)S(1)} %collective-permute-done.11.refs_1_, bf16[32,1792]{1,0:T(8,128)(2,1)S(1)} %collective-permute-done.12.refs_2_, ...), custom_call_target="tpu_custom_call" | custom-call | tf_op jit(solution)/shard_map/pallas_call | solution.py:142
  39.8 0.9 %collective-permute-done.10.refs_3_ = bf16[32,1792]{1,0:T(8,128)(2,1)S(1)} collective-permute-done((bf16[32,1792]{1,0:T(8,128)(2,1)S(1)}, bf16[32,1792]{1,0:T(8,128)(2,1)S(1)}, u32[]{:S(2)}, u32[]{:S(2)}) %collective-permute-start.10) | collective-permute-done | bytes 114720 | tf_op jit(solution)/shard_map/ppermute | solution.py:250
  40.7 4.1 %shard_map.97.hidden_ref = bf16[128,1024]{1,0:T(8,128)(2,1)S(1)} custom-call(bf16[32,1792]{1,0:T(8,128)(2,1)S(1)} %get-tuple-element.49.refs_0_, bf16[32,1792]{1,0:T(8,128)(2,1)S(1)} %collective-permute-done.8.refs_1_, bf16[32,1792]{1,0:T(8,128)(2,1)S(1)} %collective-permute-done.9.refs_2_, bf16[32,1792]{1,0:T(8,128)(2,1)S(1)} %collective-permute-done.10.refs_3_, ...), custom_call_target="tpu_custom_call" | custom-call | tf_op jit(solution)/shard_map/pallas_call | solution.py:142
  44.8 2.7 %shard_map.101 = (bf16[32,1792]{1,0:T(8,128)(2,1)S(1)}, bf16[32,1792]{1,0:T(8,128)(2,1)S(1)}, bf16[32,1792]{1,0:T(8,128)(2,1)S(1)}, bf16[32,1792]{1,0:T(8,128)(2,1)S(1)}) custom-call(bf16[128,1024]{1,0:T(8,128)(2,1)S(1)} %shard_map.97.hidden_ref, bf16[1024,3584]{1,0:T(8,128)(2,1)} %bitcast.13), custom_call_target="tpu_custom_call" | custom-call | tf_op jit(solution)/shard_map/pallas_call | solution.py:165
  47.9 1.5 %collective-permute-start.22 = (bf16[32,1792]{1,0:T(8,128)(2,1)S(1)}, bf16[32,1792]{1,0:T(8,128)(2,1)S(1)}, u32[]{:S(2)}, u32[]{:S(2)}) collective-permute-start(bf16[32,1792]{1,0:T(8,128)(2,1)S(1)} %get-tuple-element.71), channel_id=1, source_target_pairs={{0,16},{1,17},{2,18},{3,19},{4,20},{5,21},{6,22},{7,23},{8,24},{9,... | collective-permute-start | bytes 344072 | tf_op jit(solution)/shard_map/ppermute | solution.py:250
  49.5 2.7 %shard_map.98 = (bf16[32,1792]{1,0:T(8,128)(2,1)S(1)}, bf16[32,1792]{1,0:T(8,128)(2,1)S(1)}, bf16[32,1792]{1,0:T(8,128)(2,1)S(1)}, bf16[32,1792]{1,0:T(8,128)(2,1)S(1)}) custom-call(bf16[128,1024]{1,0:T(8,128)(2,1)S(1)} %shard_map.97.hidden_ref, bf16[1024,3584]{1,0:T(8,128)(2,1)} %bitcast.14), custom_call_target="tpu_custom_call" | custom-call | tf_op jit(solution)/shard_map/pallas_call | solution.py:165
  52.6 1.5 %collective-permute-start.15 = (bf16[32,1792]{1,0:T(8,128)(2,1)S(1)}, bf16[32,1792]{1,0:T(8,128)(2,1)S(1)}, u32[]{:S(2)}, u32[]{:S(2)}) collective-permute-start(bf16[32,1792]{1,0:T(8,128)(2,1)S(1)} %get-tuple-element.61), channel_id=1, source_target_pairs={{0,16},{1,17},{2,18},{3,19},{4,20},{5,21},{6,22},{7,23},{8,24},{9,... | collective-permute-start | bytes 344072 | tf_op jit(solution)/shard_map/ppermute | solution.py:250
  54.2 0.9 %shard_map.92 = (f32[128,256]{1,0:T(8,128)S(1)}, f32[128,256]{1,0:T(8,128)S(1)}) custom-call(bf16[64,1920]{1,0:T(8,128)(2,1)S(1)} %constant_dynamic-update-slice_fusion.4.refs_0_, bf16[64,1920]{1,0:T(8,128)(2,1)S(1)} %collective-permute-done.7.refs_1_, bf16[3584,256]{1,0:T(8,128)(2,1)S(1)} %copy-done.1, bf16[3584,256]{1,0:T(8,128)(2,1)S(1)} %copy-done.2), custom_call_target="tpu_custom_call" | custom-call | tf_op jit(solution)/shard_map/pallas_call | solution.py:142
  56.4 1.6 %collective-permute-start.24 = (bf16[64,1792]{1,0:T(8,128)(2,1)S(1)}, bf16[64,1792]{1,0:T(8,128)(2,1)S(1)}, u32[]{:S(2)}, u32[]{:S(2)}) collective-permute-start(bf16[64,1792]{1,0:T(8,128)(2,1)S(1)} %get-tuple-element.74), channel_id=1, source_target_pairs={{0,1},{1,0},{2,3},{3,2},{4,5},{5,4},{6,7},{7,6},{8,9},{9,8},{10,11... | collective-permute-start | bytes 688136 | tf_op jit(solution)/shard_map/ppermute | solution.py:250
  58.6 1.3 %collective-permute-done.16.refs_3_ = bf16[32,1792]{1,0:T(8,128)(2,1)S(1)} collective-permute-done((bf16[32,1792]{1,0:T(8,128)(2,1)S(1)}, bf16[32,1792]{1,0:T(8,128)(2,1)S(1)}, u32[]{:S(2)}, u32[]{:S(2)}) %collective-permute-start.16) | collective-permute-done | bytes 114720 | tf_op jit(solution)/shard_map/ppermute | solution.py:250
  60.5 1.6 %collective-permute-start.17 = (bf16[64,1792]{1,0:T(8,128)(2,1)S(1)}, bf16[64,1792]{1,0:T(8,128)(2,1)S(1)}, u32[]{:S(2)}, u32[]{:S(2)}) collective-permute-start(bf16[64,1792]{1,0:T(8,128)(2,1)S(1)} %get-tuple-element.64), channel_id=1, source_target_pairs={{0,1},{1,0},{2,3},{3,2},{4,5},{5,4},{6,7},{7,6},{8,9},{9,8},{10,11... | collective-permute-start | bytes 688136 | tf_op jit(solution)/shard_map/ppermute | solution.py:250
  62.0 2.8 %collective-permute-done.24.refs_0_ = bf16[64,1792]{1,0:T(8,128)(2,1)S(1)} collective-permute-done((bf16[64,1792]{1,0:T(8,128)(2,1)S(1)}, bf16[64,1792]{1,0:T(8,128)(2,1)S(1)}, u32[]{:S(2)}, u32[]{:S(2)}) %collective-permute-start.24) | collective-permute-done | bytes 229408 | tf_op jit(solution)/shard_map/ppermute | solution.py:250
  65.2 2.9 %collective-permute-start.26 = (bf16[16,1792]{1,0:T(8,128)(2,1)S(1)}, bf16[16,1792]{1,0:T(8,128)(2,1)S(1)}, u32[]{:S(2)}, u32[]{:S(2)}) collective-permute-start(bf16[16,1792]{1,0:T(8,128)(2,1)S(1)} %get-tuple-element.77), channel_id=1, source_target_pairs={{0,4},{1,5},{2,6},{3,7},{4,0},{5,1},{6,2},{7,3},{8,12},{9,13},{10,... | collective-permute-start | bytes 172040 | tf_op jit(solution)/shard_map/ppermute | solution.py:250
  68.1 1.2 %collective-permute-start.27 = (bf16[16,1792]{1,0:T(8,128)(2,1)S(1)}, bf16[16,1792]{1,0:T(8,128)(2,1)S(1)}, u32[]{:S(2)}, u32[]{:S(2)}) collective-permute-start(bf16[16,1792]{1,0:T(8,128)(2,1)S(1)} %get-tuple-element.78), channel_id=1, source_target_pairs={{0,6},{1,7},{2,4},{3,5},{4,2},{5,3},{6,0},{7,1},{8,14},{9,15},{10,... | collective-permute-start | bytes 172040 | tf_op jit(solution)/shard_map/ppermute | solution.py:250
  69.9 2.9 %collective-permute-start.19 = (bf16[16,1792]{1,0:T(8,128)(2,1)S(1)}, bf16[16,1792]{1,0:T(8,128)(2,1)S(1)}, u32[]{:S(2)}, u32[]{:S(2)}) collective-permute-start(bf16[16,1792]{1,0:T(8,128)(2,1)S(1)} %get-tuple-element.67), channel_id=1, source_target_pairs={{0,4},{1,5},{2,6},{3,7},{4,0},{5,1},{6,2},{7,3},{8,12},{9,13},{10,... | collective-permute-start | bytes 172040 | tf_op jit(solution)/shard_map/ppermute | solution.py:250
  72.8 1.2 %collective-permute-start.20 = (bf16[16,1792]{1,0:T(8,128)(2,1)S(1)}, bf16[16,1792]{1,0:T(8,128)(2,1)S(1)}, u32[]{:S(2)}, u32[]{:S(2)}) collective-permute-start(bf16[16,1792]{1,0:T(8,128)(2,1)S(1)} %get-tuple-element.68), channel_id=1, source_target_pairs={{0,6},{1,7},{2,4},{3,5},{4,2},{5,3},{6,0},{7,1},{8,14},{9,15},{10,... | collective-permute-start | bytes 172040 | tf_op jit(solution)/shard_map/ppermute | solution.py:250
  74.3 0.9 %collective-permute-done.18.refs_1_ = bf16[16,1792]{1,0:T(8,128)(2,1)S(1)} collective-permute-done((bf16[16,1792]{1,0:T(8,128)(2,1)S(1)}, bf16[16,1792]{1,0:T(8,128)(2,1)S(1)}, u32[]{:S(2)}, u32[]{:S(2)}) %collective-permute-start.18) | collective-permute-done | bytes 57376 | tf_op jit(solution)/shard_map/ppermute | solution.py:250
  75.2 2.1 %collective-permute-done.19.refs_2_ = bf16[16,1792]{1,0:T(8,128)(2,1)S(1)} collective-permute-done((bf16[16,1792]{1,0:T(8,128)(2,1)S(1)}, bf16[16,1792]{1,0:T(8,128)(2,1)S(1)}, u32[]{:S(2)}, u32[]{:S(2)}) %collective-permute-start.19) | collective-permute-done | bytes 57376 | tf_op jit(solution)/shard_map/ppermute | solution.py:250
  77.3 1.5 %collective-permute-done.20.refs_3_ = bf16[16,1792]{1,0:T(8,128)(2,1)S(1)} collective-permute-done((bf16[16,1792]{1,0:T(8,128)(2,1)S(1)}, bf16[16,1792]{1,0:T(8,128)(2,1)S(1)}, u32[]{:S(2)}, u32[]{:S(2)}) %collective-permute-start.20) | collective-permute-done | bytes 57376 | tf_op jit(solution)/shard_map/ppermute | solution.py:250
  (59 shorter events, 10.3 us)
Async XLA Ops:
  0.0 0.9 %copy-start.3 = (bf16[16,3584]{1,0:T(8,128)(2,1)S(1)}, bf16[16,3584]{1,0:T(8,128)(2,1)}, u32[]{:S(2)}) copy-start(bf16[16,3584]{1,0:T(8,128)(2,1)} %tokens_ref.1) | copy-start | bytes 344068
  2.4 16.9 %collective-permute-start.2 = (bf16[16,1792]{1,0:T(8,128)(2,1)S(1)}, bf16[16,1792]{1,0:T(8,128)(2,1)S(1)}, u32[]{:S(2)}, u32[]{:S(2)}) collective-permute-start(bf16[16,1792]{1,0:T(8,128)(2,1)S(1)} %get-tuple-element.42), channel_id=1, source_target_pairs={{0,6},{1,7},{2,4},{3,5},{4,2},{5,3},{6,0},{7,1},{8,14},{9,15},{10,... | collective-permute-start | bytes 172040 | tf_op jit(solution)/shard_map/ppermute | solution.py:250
  7.5 8.5 %collective-permute-start.1 = (bf16[16,1792]{1,0:T(8,128)(2,1)S(1)}, bf16[16,1792]{1,0:T(8,128)(2,1)S(1)}, u32[]{:S(2)}, u32[]{:S(2)}) collective-permute-start(bf16[16,1792]{1,0:T(8,128)(2,1)S(1)} %get-tuple-element.42), channel_id=1, source_target_pairs={{0,4},{1,5},{2,6},{3,7},{4,0},{5,1},{6,2},{7,3},{8,12},{9,13},{10,... | collective-permute-start | bytes 172040 | tf_op jit(solution)/shard_map/ppermute | solution.py:250
  7.5 4.4 %collective-permute-start = (bf16[16,1792]{1,0:T(8,128)(2,1)S(1)}, bf16[16,1792]{1,0:T(8,128)(2,1)S(1)}, u32[]{:S(2)}, u32[]{:S(2)}) collective-permute-start(bf16[16,1792]{1,0:T(8,128)(2,1)S(1)} %get-tuple-element.42), channel_id=1, source_target_pairs={{0,2},{1,3},{2,0},{3,1},{4,6},{5,7},{6,4},{7,5},{8,10},{9,11},{10,... | collective-permute-start | bytes 172040 | tf_op jit(solution)/shard_map/ppermute | solution.py:250
  8.1 9.7 %collective-permute-start.6 = (bf16[16,1920]{1,0:T(8,128)(2,1)S(1)}, bf16[16,1920]{1,0:T(8,128)(2,1)S(1)}, u32[]{:S(2)}, u32[]{:S(2)}) collective-permute-start(bf16[16,1920]{1,0:T(8,128)(2,1)S(1)} %get-tuple-element.43), channel_id=1, source_target_pairs={{0,6},{1,7},{2,4},{3,5},{4,2},{5,3},{6,0},{7,1},{8,14},{9,15},{10,... | collective-permute-start | bytes 184328 | tf_op jit(solution)/shard_map/ppermute | solution.py:250
  11.9 5.9 %collective-permute-start.5 = (bf16[16,1920]{1,0:T(8,128)(2,1)S(1)}, bf16[16,1920]{1,0:T(8,128)(2,1)S(1)}, u32[]{:S(2)}, u32[]{:S(2)}) collective-permute-start(bf16[16,1920]{1,0:T(8,128)(2,1)S(1)} %get-tuple-element.43), channel_id=1, source_target_pairs={{0,4},{1,5},{2,6},{3,7},{4,0},{5,1},{6,2},{7,3},{8,12},{9,13},{10,... | collective-permute-start | bytes 184328 | tf_op jit(solution)/shard_map/ppermute | solution.py:250
  11.9 5.0 %collective-permute-start.4 = (bf16[16,1920]{1,0:T(8,128)(2,1)S(1)}, bf16[16,1920]{1,0:T(8,128)(2,1)S(1)}, u32[]{:S(2)}, u32[]{:S(2)}) collective-permute-start(bf16[16,1920]{1,0:T(8,128)(2,1)S(1)} %get-tuple-element.43), channel_id=1, source_target_pairs={{0,2},{1,3},{2,0},{3,1},{4,6},{5,7},{6,4},{7,5},{8,10},{9,11},{10,... | collective-permute-start | bytes 184328 | tf_op jit(solution)/shard_map/ppermute | solution.py:250
  17.8 9.0 %collective-permute-start.7 = (bf16[64,1920]{1,0:T(8,128)(2,1)S(1)}, bf16[64,1920]{1,0:T(8,128)(2,1)S(1)}, u32[]{:S(2)}, u32[]{:S(2)}) collective-permute-start(bf16[64,1920]{1,0:T(8,128)(2,1)S(1)} %constant_dynamic-update-slice_fusion.4.refs_0_), channel_id=1, source_target_pairs={{0,1},{1,0},{2,3},{3,2},{4,5},{5,4},{6,7},{7,6},{8,9},{9,8},{10,11... | collective-permute-start | bytes 737288 | tf_op jit(solution)/shard_map/ppermute | solution.py:250
  19.4 10.7 %collective-permute-start.3 = (bf16[64,1792]{1,0:T(8,128)(2,1)S(1)}, bf16[64,1792]{1,0:T(8,128)(2,1)S(1)}, u32[]{:S(2)}, u32[]{:S(2)}) collective-permute-start(bf16[64,1792]{1,0:T(8,128)(2,1)S(1)} %constant_dynamic-update-slice_fusion.refs_0_), channel_id=1, source_target_pairs={{0,1},{1,0},{2,3},{3,2},{4,5},{5,4},{6,7},{7,6},{8,9},{9,8},{10,11... | collective-permute-start | bytes 688136 | tf_op jit(solution)/shard_map/ppermute | solution.py:250
  28.1 4.3 %collective-permute-start.11 = (bf16[32,1792]{1,0:T(8,128)(2,1)S(1)}, bf16[32,1792]{1,0:T(8,128)(2,1)S(1)}, u32[]{:S(2)}, u32[]{:S(2)}) collective-permute-start(bf16[32,1792]{1,0:T(8,128)(2,1)S(1)} %get-tuple-element.54), channel_id=1, source_target_pairs={{0,8},{1,9},{2,10},{3,11},{4,12},{5,13},{6,14},{7,15},{8,0},{9,1},... | collective-permute-start | bytes 344072 | tf_op jit(solution)/shard_map/ppermute | solution.py:250
  28.2 6.0 %collective-permute-start.12 = (bf16[32,1792]{1,0:T(8,128)(2,1)S(1)}, bf16[32,1792]{1,0:T(8,128)(2,1)S(1)}, u32[]{:S(2)}, u32[]{:S(2)}) collective-permute-start(bf16[32,1792]{1,0:T(8,128)(2,1)S(1)} %get-tuple-element.55), channel_id=1, source_target_pairs={{0,16},{1,17},{2,18},{3,19},{4,20},{5,21},{6,22},{7,23},{8,24},{9,... | collective-permute-start | bytes 344072 | tf_op jit(solution)/shard_map/ppermute | solution.py:250
  29.8 6.0 %collective-permute-start.13 = (bf16[32,1792]{1,0:T(8,128)(2,1)S(1)}, bf16[32,1792]{1,0:T(8,128)(2,1)S(1)}, u32[]{:S(2)}, u32[]{:S(2)}) collective-permute-start(bf16[32,1792]{1,0:T(8,128)(2,1)S(1)} %get-tuple-element.56), channel_id=1, source_target_pairs={{0,24},{1,25},{2,26},{3,27},{4,28},{5,29},{6,30},{7,31},{8,16},{9,... | collective-permute-start | bytes 344072 | tf_op jit(solution)/shard_map/ppermute | solution.py:250
  30.5 9.2 %collective-permute-start.8 = (bf16[32,1792]{1,0:T(8,128)(2,1)S(1)}, bf16[32,1792]{1,0:T(8,128)(2,1)S(1)}, u32[]{:S(2)}, u32[]{:S(2)}) collective-permute-start(bf16[32,1792]{1,0:T(8,128)(2,1)S(1)} %get-tuple-element.50), channel_id=1, source_target_pairs={{0,8},{1,9},{2,10},{3,11},{4,12},{5,13},{6,14},{7,15},{8,0},{9,1},... | collective-permute-start | bytes 344072 | tf_op jit(solution)/shard_map/ppermute | solution.py:250
  30.9 8.8 %collective-permute-start.9 = (bf16[32,1792]{1,0:T(8,128)(2,1)S(1)}, bf16[32,1792]{1,0:T(8,128)(2,1)S(1)}, u32[]{:S(2)}, u32[]{:S(2)}) collective-permute-start(bf16[32,1792]{1,0:T(8,128)(2,1)S(1)} %get-tuple-element.51), channel_id=1, source_target_pairs={{0,16},{1,17},{2,18},{3,19},{4,20},{5,21},{6,22},{7,23},{8,24},{9,... | collective-permute-start | bytes 344072 | tf_op jit(solution)/shard_map/ppermute | solution.py:250
  32.4 8.3 %collective-permute-start.10 = (bf16[32,1792]{1,0:T(8,128)(2,1)S(1)}, bf16[32,1792]{1,0:T(8,128)(2,1)S(1)}, u32[]{:S(2)}, u32[]{:S(2)}) collective-permute-start(bf16[32,1792]{1,0:T(8,128)(2,1)S(1)} %get-tuple-element.52), channel_id=1, source_target_pairs={{0,24},{1,25},{2,26},{3,27},{4,28},{5,29},{6,30},{7,31},{8,16},{9,... | collective-permute-start | bytes 344072 | tf_op jit(solution)/shard_map/ppermute | solution.py:250
  44.8 9.4 %copy-start.1 = (bf16[3584,256]{1,0:T(8,128)(2,1)S(1)}, bf16[3584,256]{1,0:T(8,128)(2,1)}, u32[]{:S(2)}) copy-start(bf16[3584,256]{1,0:T(8,128)(2,1)} %refs_2_.3) | copy-start | bytes 5505028
  44.8 9.4 %copy-start.2 = (bf16[3584,256]{1,0:T(8,128)(2,1)S(1)}, bf16[3584,256]{1,0:T(8,128)(2,1)}, u32[]{:S(2)}) copy-start(bf16[3584,256]{1,0:T(8,128)(2,1)} %refs_3_.3) | copy-start | bytes 5505028
  47.5 6.6 %collective-permute-start.21 = (bf16[32,1792]{1,0:T(8,128)(2,1)S(1)}, bf16[32,1792]{1,0:T(8,128)(2,1)S(1)}, u32[]{:S(2)}, u32[]{:S(2)}) collective-permute-start(bf16[32,1792]{1,0:T(8,128)(2,1)S(1)} %get-tuple-element.70), channel_id=1, source_target_pairs={{0,8},{1,9},{2,10},{3,11},{4,12},{5,13},{6,14},{7,15},{8,0},{9,1},... | collective-permute-start | bytes 344072 | tf_op jit(solution)/shard_map/ppermute | solution.py:250
  47.9 8.0 %collective-permute-start.22 = (bf16[32,1792]{1,0:T(8,128)(2,1)S(1)}, bf16[32,1792]{1,0:T(8,128)(2,1)S(1)}, u32[]{:S(2)}, u32[]{:S(2)}) collective-permute-start(bf16[32,1792]{1,0:T(8,128)(2,1)S(1)} %get-tuple-element.71), channel_id=1, source_target_pairs={{0,16},{1,17},{2,18},{3,19},{4,20},{5,21},{6,22},{7,23},{8,24},{9,... | collective-permute-start | bytes 344072 | tf_op jit(solution)/shard_map/ppermute | solution.py:250
  49.4 6.5 %copy-start = (bf16[256,3584]{1,0:T(8,128)(2,1)S(1)}, bf16[256,3584]{1,0:T(8,128)(2,1)}, u32[]{:S(2)}) copy-start(bf16[256,3584]{1,0:T(8,128)(2,1)} %down_ref.3) | copy-start | bytes 5505028
  49.4 6.5 %collective-permute-start.23 = (bf16[32,1792]{1,0:T(8,128)(2,1)S(1)}, bf16[32,1792]{1,0:T(8,128)(2,1)S(1)}, u32[]{:S(2)}, u32[]{:S(2)}) collective-permute-start(bf16[32,1792]{1,0:T(8,128)(2,1)S(1)} %get-tuple-element.72), channel_id=1, source_target_pairs={{0,24},{1,25},{2,26},{3,27},{4,28},{5,29},{6,30},{7,31},{8,16},{9,... | collective-permute-start | bytes 344072 | tf_op jit(solution)/shard_map/ppermute | solution.py:250
  52.1 5.8 %collective-permute-start.14 = (bf16[32,1792]{1,0:T(8,128)(2,1)S(1)}, bf16[32,1792]{1,0:T(8,128)(2,1)S(1)}, u32[]{:S(2)}, u32[]{:S(2)}) collective-permute-start(bf16[32,1792]{1,0:T(8,128)(2,1)S(1)} %get-tuple-element.60), channel_id=1, source_target_pairs={{0,8},{1,9},{2,10},{3,11},{4,12},{5,13},{6,14},{7,15},{8,0},{9,1},... | collective-permute-start | bytes 344072 | tf_op jit(solution)/shard_map/ppermute | solution.py:250
  52.6 6.0 %collective-permute-start.15 = (bf16[32,1792]{1,0:T(8,128)(2,1)S(1)}, bf16[32,1792]{1,0:T(8,128)(2,1)S(1)}, u32[]{:S(2)}, u32[]{:S(2)}) collective-permute-start(bf16[32,1792]{1,0:T(8,128)(2,1)S(1)} %get-tuple-element.61), channel_id=1, source_target_pairs={{0,16},{1,17},{2,18},{3,19},{4,20},{5,21},{6,22},{7,23},{8,24},{9,... | collective-permute-start | bytes 344072 | tf_op jit(solution)/shard_map/ppermute | solution.py:250
  54.1 5.8 %collective-permute-start.16 = (bf16[32,1792]{1,0:T(8,128)(2,1)S(1)}, bf16[32,1792]{1,0:T(8,128)(2,1)S(1)}, u32[]{:S(2)}, u32[]{:S(2)}) collective-permute-start(bf16[32,1792]{1,0:T(8,128)(2,1)S(1)} %get-tuple-element.62), channel_id=1, source_target_pairs={{0,24},{1,25},{2,26},{3,27},{4,28},{5,29},{6,30},{7,31},{8,16},{9,... | collective-permute-start | bytes 344072 | tf_op jit(solution)/shard_map/ppermute | solution.py:250
  56.4 8.4 %collective-permute-start.24 = (bf16[64,1792]{1,0:T(8,128)(2,1)S(1)}, bf16[64,1792]{1,0:T(8,128)(2,1)S(1)}, u32[]{:S(2)}, u32[]{:S(2)}) collective-permute-start(bf16[64,1792]{1,0:T(8,128)(2,1)S(1)} %get-tuple-element.74), channel_id=1, source_target_pairs={{0,1},{1,0},{2,3},{3,2},{4,5},{5,4},{6,7},{7,6},{8,9},{9,8},{10,11... | collective-permute-start | bytes 688136 | tf_op jit(solution)/shard_map/ppermute | solution.py:250
  60.5 9.0 %collective-permute-start.17 = (bf16[64,1792]{1,0:T(8,128)(2,1)S(1)}, bf16[64,1792]{1,0:T(8,128)(2,1)S(1)}, u32[]{:S(2)}, u32[]{:S(2)}) collective-permute-start(bf16[64,1792]{1,0:T(8,128)(2,1)S(1)} %get-tuple-element.64), channel_id=1, source_target_pairs={{0,1},{1,0},{2,3},{3,2},{4,5},{5,4},{6,7},{7,6},{8,9},{9,8},{10,11... | collective-permute-start | bytes 688136 | tf_op jit(solution)/shard_map/ppermute | solution.py:250
  64.9 7.9 %collective-permute-start.25 = (bf16[16,1792]{1,0:T(8,128)(2,1)S(1)}, bf16[16,1792]{1,0:T(8,128)(2,1)S(1)}, u32[]{:S(2)}, u32[]{:S(2)}) collective-permute-start(bf16[16,1792]{1,0:T(8,128)(2,1)S(1)} %get-tuple-element.76), channel_id=1, source_target_pairs={{0,2},{1,3},{2,0},{3,1},{4,6},{5,7},{6,4},{7,5},{8,10},{9,11},{10,... | collective-permute-start | bytes 172040 | tf_op jit(solution)/shard_map/ppermute | solution.py:250
  65.2 8.8 %collective-permute-start.26 = (bf16[16,1792]{1,0:T(8,128)(2,1)S(1)}, bf16[16,1792]{1,0:T(8,128)(2,1)S(1)}, u32[]{:S(2)}, u32[]{:S(2)}) collective-permute-start(bf16[16,1792]{1,0:T(8,128)(2,1)S(1)} %get-tuple-element.77), channel_id=1, source_target_pairs={{0,4},{1,5},{2,6},{3,7},{4,0},{5,1},{6,2},{7,3},{8,12},{9,13},{10,... | collective-permute-start | bytes 172040 | tf_op jit(solution)/shard_map/ppermute | solution.py:250
  68.1 6.2 %collective-permute-start.27 = (bf16[16,1792]{1,0:T(8,128)(2,1)S(1)}, bf16[16,1792]{1,0:T(8,128)(2,1)S(1)}, u32[]{:S(2)}, u32[]{:S(2)}) collective-permute-start(bf16[16,1792]{1,0:T(8,128)(2,1)S(1)} %get-tuple-element.78), channel_id=1, source_target_pairs={{0,6},{1,7},{2,4},{3,5},{4,2},{5,3},{6,0},{7,1},{8,14},{9,15},{10,... | collective-permute-start | bytes 172040 | tf_op jit(solution)/shard_map/ppermute | solution.py:250
  69.5 5.7 %collective-permute-start.18 = (bf16[16,1792]{1,0:T(8,128)(2,1)S(1)}, bf16[16,1792]{1,0:T(8,128)(2,1)S(1)}, u32[]{:S(2)}, u32[]{:S(2)}) collective-permute-start(bf16[16,1792]{1,0:T(8,128)(2,1)S(1)} %get-tuple-element.66), channel_id=1, source_target_pairs={{0,2},{1,3},{2,0},{3,1},{4,6},{5,7},{6,4},{7,5},{8,10},{9,11},{10,... | collective-permute-start | bytes 172040 | tf_op jit(solution)/shard_map/ppermute | solution.py:250
  69.9 7.4 %collective-permute-start.19 = (bf16[16,1792]{1,0:T(8,128)(2,1)S(1)}, bf16[16,1792]{1,0:T(8,128)(2,1)S(1)}, u32[]{:S(2)}, u32[]{:S(2)}) collective-permute-start(bf16[16,1792]{1,0:T(8,128)(2,1)S(1)} %get-tuple-element.67), channel_id=1, source_target_pairs={{0,4},{1,5},{2,6},{3,7},{4,0},{5,1},{6,2},{7,3},{8,12},{9,13},{10,... | collective-permute-start | bytes 172040 | tf_op jit(solution)/shard_map/ppermute | solution.py:250
  72.8 6.0 %collective-permute-start.20 = (bf16[16,1792]{1,0:T(8,128)(2,1)S(1)}, bf16[16,1792]{1,0:T(8,128)(2,1)S(1)}, u32[]{:S(2)}, u32[]{:S(2)}) collective-permute-start(bf16[16,1792]{1,0:T(8,128)(2,1)S(1)} %get-tuple-element.68), channel_id=1, source_target_pairs={{0,6},{1,7},{2,4},{3,5},{4,2},{5,3},{6,0},{7,1},{8,14},{9,15},{10,... | collective-permute-start | bytes 172040 | tf_op jit(solution)/shard_map/ppermute | solution.py:250
  (2 other events, 1.4 us)

commit v2 on v0

v2 whole, which is shorter than its diff:
```python
import functools

import jax
import jax.numpy as jnp
from jax import lax
from jax.experimental import pallas as pl
from jax.experimental.pallas import tpu as pltpu
from jax.sharding import PartitionSpec as P

TOPK = 8
TOP_GROUPS = 4
LANES = 128
CORES = 2
DEPTH_Z = 4
OUT_CUTS = 2
BOTH = ("outer", "inner")
BF16 = jnp.bfloat16
F32 = jnp.float32
PARAMS = pltpu.CompilerParams(vmem_limit_bytes=16 * 1024 * 1024)
IN_VMEM = pl.BlockSpec(memory_space=pltpu.VMEM)
IN_SMEM = pl.BlockSpec(memory_space=pltpu.SMEM)
ANYWHERE = pl.BlockSpec(memory_space=pl.ANY)


def dot(a, b):
    return jnp.dot(a, b, preferred_element_type=F32)


def dot_first(a, b):
    return lax.dot_general(a, b, (((0,), (0,)), ((), ())), preferred_element_type=F32)


def whole(shape, dtype):
    return jax.ShapeDtypeStruct(shape, dtype)


def call(kernel, out_shape, *args, **more):
    return pl.pallas_call(kernel, out_shape=out_shape, compiler_params=PARAMS, **more)(*args)


def prefetch_kernel(*refs):
    count = (len(refs) - 2) // 2
    token_ref, sem = refs[-2:]
    copies = [
        pltpu.make_async_copy(refs[at], refs[count + at], sem.at[at]) for at in range(count)
    ]
    for copy in copies:
        copy.start()
    token_ref[...] = jnp.zeros_like(token_ref)
    for copy in copies:
        copy.wait()


def far(array):
    return pltpu.with_memory_space_constraint(array, pltpu.HBM)


def after(array, *others):
    return lax.optimization_barrier((array, *others))[0]


def prefetch(*arrays):
    arrays = [far(array) for array in arrays]
    return call(
        prefetch_kernel,
        [pltpu.VMEM(array.shape, array.dtype) for array in arrays] + [pltpu.VMEM((8, LANES), F32)],
        *arrays,
        in_specs=[ANYWHERE] * len(arrays),
        out_specs=[IN_VMEM] * (len(arrays) + 1),
        scratch_shapes=[pltpu.SemaphoreType.DMA((len(arrays),))],
    )


def prepare_kernel(tokens_ref, experts_ref, score_ref, out_ref, experts, scores, sem):
    width = tokens_ref.shape[1]
    copies = [
        pltpu.make_async_copy(experts_ref, experts, sem.at[0]),
        pltpu.make_async_copy(score_ref, scores, sem.at[1]),
        pltpu.make_async_copy(tokens_ref, out_ref.at[:, pl.ds(0, width)], sem.at[2]),
    ]
    for copy in copies:
        copy.start()
    copies[0].wait()
    copies[1].wait()
    names = jnp.concatenate([experts[...], scores[...]], axis=0).astype(F32).astype(BF16)
    slots = names.shape[0]
    row = lax.broadcasted_iota(jnp.int32, (slots, LANES), 0)
    col = lax.broadcasted_iota(jnp.int32, (slots, LANES), 1)
    spread = jnp.where(row == col, 1.0, 0.0).astype(BF16)
    out_ref[:, width:] = dot_first(names, spread).astype(BF16)
    copies[2].wait()


def prepare(tokens, experts, gate_score):
    rows, width = tokens.shape
    return call(
        prepare_kernel,
        pltpu.VMEM((rows, width + LANES), BF16),
        far(tokens),
        far(experts.T),
        far(gate_score.T),
        in_specs=[ANYWHERE] * 3,
        out_specs=IN_VMEM,
        scratch_shapes=[pltpu.VMEM((TOPK, rows), jnp.int32)] * 2 + [pltpu.SemaphoreType.DMA((3,))],
    )


def routing(meta, block_rows, capacity, group_count, expert_of):
    token_count = meta.shape[0]
    send_rows = token_count // block_rows * capacity
    total = send_rows * group_count
    slot = lax.broadcasted_iota(jnp.int32, (1, total), 1)
    group = lax.div(slot, jnp.int32(send_rows))
    expert = expert_of(group).astype(F32)
    scores = meta[:, TOPK:2 * TOPK]
    weights = 2.5 * scores / jnp.sum(scores, axis=1, keepdims=True)
    named = jnp.zeros((token_count, total), F32)
    weight = jnp.zeros((token_count, total), F32)
    for k in range(TOPK):
        match = meta[:, k:k + 1] == expert
        named = jnp.where(match, 1.0, named)
        weight = jnp.where(match, weights[:, k:k + 1], weight)
    row = lax.broadcasted_iota(jnp.int32, (token_count, token_count), 0)
    col = lax.broadcasted_iota(jnp.int32, (token_count, token_count), 1)
    rows_each = jnp.int32(block_rows)
    before = jnp.logical_and(lax.div(row, rows_each) == lax.div(col, rows_each), col < row)
    rank = dot(jnp.where(before, 1.0, 0.0).astype(BF16), named.astype(BF16))
    owner = lax.div(lax.broadcasted_iota(jnp.int32, (token_count, 1), 0), rows_each)
    wanted = (slot - group * send_rows - owner * capacity).astype(F32)
    hit = jnp.logical_and(jnp.logical_and(rank == wanted, rank < float(capacity)), named > 0.5)
    return hit, weight


def select_kernel(width, block_rows, capacity, inner_count, chips_x, blocks, where_ref, *refs):
    pieces, outs = refs[:blocks], refs[blocks + 1:]
    outer_at, inner_at = where_ref[0], where_ref[1]

    def expert_of(group):
        along_y = lax.div(group, jnp.int32(chips_x))
        along_x = group - along_y * chips_x
        return (outer_at ^ (along_x * CORES)) * inner_count + (inner_at ^ along_y)

    meta = jnp.concatenate([piece[:, width:] for piece in pieces], axis=0).astype(F32)
    hit, _ = routing(meta, block_rows, capacity, len(outs), expert_of)
    rows = jnp.concatenate([piece[:, :width] for piece in pieces], axis=0)
    chosen = dot_first(jnp.where(hit, 1.0, 0.0).astype(BF16), rows).astype(BF16)
    each = outs[0].shape[0]
    for at, out in enumerate(outs):
        out[...] = chosen[at * each:(at + 1) * each]


def hidden_kernel(width, blocks, *refs):
    pieces = refs[:blocks]
    gate_ref, up_ref, out_ref = refs[blocks:]
    rows = jnp.concatenate([piece[:, :width] for piece in pieces], axis=0)
    gate = dot(rows, gate_ref[...])
    up = dot(rows, up_ref[...])
    out_ref[...] = (gate / (1.0 + jnp.exp(-gate)) * up).astype(BF16)


def hidden(pieces, gate, up):
    shape = (sum(piece.shape[0] for piece in pieces), gate.shape[1])
    return call(
        functools.partial(hidden_kernel, gate.shape[0], len(pieces)),
        whole(shape, BF16),
        *pieces,
        gate,
        up,
    )


def down_kernel(start, width, chips_x, depth_y, hidden_ref, down_ref, *outs):
    answer = dot(hidden_ref[...], down_ref[:, start:start + width])
    part = outs[0].shape[0] // depth_y
    for at, out in enumerate(outs):
        along_x, core = at // CORES, at % CORES
        firsts = [((y * chips_x + along_x) * CORES + core) * part for y in range(depth_y)]
        out[...] = jnp.concatenate([answer[first:first + part] for first in firsts], axis=0).astype(BF16)


def down(rows, matrix, start, width, outer_count, depth_y):
    return call(
        functools.partial(down_kernel, start, width, outer_count // CORES, depth_y),
        [whole((rows.shape[0] // outer_count, width), BF16)] * outer_count,
        rows,
        matrix,
    )


def table_kernel(width, block_rows, capacity, inner_count, group_count, blocks, where_ref, *refs):
    pieces, (high_ref, low_ref) = refs[:blocks], refs[blocks:]
    outer_at, inner_at = where_ref[0], where_ref[1]
    meta = jnp.concatenate([piece[:, width:] for piece in pieces], axis=0).astype(F32)
    hit, weight = routing(
        meta, block_rows, capacity, group_count, lambda group: (outer_at ^ group) * inner_count + inner_at
    )
    weight = jnp.where(hit, weight, 0.0)
    high = weight.astype(BF16)
    high_ref[...] = high
    low_ref[...] = (weight - high.astype(F32)).astype(BF16)


def combine_kernel(blocks, start, width, hidden_ref, down_ref, high_ref, low_ref, *refs):
    answers, keep_ref, outs = refs[:blocks], refs[blocks], refs[blocks + 1:]
    rows = jnp.concatenate([answer[...] for answer in answers], axis=0)
    total = dot(hidden_ref[...], down_ref[:, start:start + width])
    total = total + dot(high_ref[...], rows) + dot(low_ref[...], rows)
    each = keep_ref.shape[0]
    keep_ref[...] = total[:each]
    for at, out in enumerate(outs):
        out[...] = total[(at + 1) * each:(at + 2) * each].astype(BF16)


def combine(shared_hidden, shared_down, high, low, answers, start, width, sends):
    each = shared_hidden.shape[0] // (sends + 1)
    return call(
        functools.partial(combine_kernel, len(answers), start, width),
        [whole((each, width), F32)] + [whole((each, width), BF16)] * sends,
        shared_hidden,
        shared_down,
        high,
        low,
        *answers,
    )


def add_kernel(blocks, kept_ref, *refs):
    arrived, outs = refs[:blocks], refs[blocks:]
    total = kept_ref[...]
    for block in arrived:
        total = total + block[...].astype(F32)
    each = outs[0].shape[0]
    for at, out in enumerate(outs):
        out[...] = total[at * each:(at + 1) * each].astype(out.dtype)


def finish_kernel(blocks, width, *refs):
    out_ref = refs[-1]
    for at in range((len(refs) - 1) // blocks):
        group = refs[at * blocks:(at + 1) * blocks]
        total = group[0][...]
        for block in group[1:]:
            total = total + block[...].astype(F32)
        out_ref[:, at * width:(at + 1) * width] = total.astype(BF16)


def per_device(
    tokens,
    experts,
    gate_score,
    expert_gate,
    expert_up,
    expert_down,
    shared_gate,
    shared_up,
    shared_down,
):
    rows, model_width = tokens.shape
    inner_count = lax.axis_size("inner")
    outer_count = lax.axis_size("outer")
    depth_y = inner_count // DEPTH_Z
    chips_x = outer_count // CORES
    capacity = TOPK // TOP_GROUPS * rows // inner_count
    device_count = inner_count * outer_count
    where = jnp.stack([lax.axis_index("outer"), lax.axis_index("inner")]).astype(jnp.int32)

    def swap(array, distance):
        return lax.ppermute(array, BOTH, [(at, at ^ distance) for at in range(device_count)])

    def along_z(k):
        return k * depth_y

    def along_outer(k):
        return k * inner_count

    sent = prepare(tokens, experts, gate_score)
    *expert_weights, loaded = prefetch(expert_gate[0], expert_up[0], expert_down[0])
    column = [sent] + [swap(sent, along_z(k)) for k in range(1, DEPTH_Z)]
    *column, loaded = lax.optimization_barrier((*column, loaded))
    at_hand = column + [swap(block, along_outer(1)) for block in column]

    groups = depth_y * chips_x
    blocks = call(
        functools.partial(
            select_kernel, model_width, rows, capacity, inner_count, chips_x, len(at_hand)
        ),
        [whole((CORES * DEPTH_Z * capacity, model_width), BF16)] * groups,
        where,
        *at_hand,
        loaded,
        in_specs=[IN_SMEM] + [IN_VMEM] * len(at_hand) + [ANYWHERE],
    )
    arrived = [blocks[0]]
    for at in range(1, groups):
        along_y, along_x = at // chips_x, at % chips_x
        arrived.append(swap(blocks[at], along_y + along_outer(along_x * CORES)))
    expert_hidden = hidden(arrived, *expert_weights[:2])

    *shared_weights, _ = prefetch(shared_gate, shared_up, shared_down)
    dense = after(jnp.concatenate(column, axis=0), *arrived)
    segment = [dense] + [swap(dense, k) for k in range(1, depth_y)]
    high, low = call(
        functools.partial(
            table_kernel, model_width, rows, capacity, inner_count, outer_count, len(segment)
        ),
        [whole((rows * inner_count, device_count * capacity), BF16)] * 2,
        where,
        *segment,
        in_specs=[IN_SMEM] + [IN_VMEM] * len(segment),
    )
    shared_hidden = hidden(segment, *shared_weights[:2])

    out_width = model_width // OUT_CUTS
    finals = []
    for at in range(OUT_CUTS):
        start = at * out_width
        blocks = down(expert_hidden, expert_weights[2], start, out_width, outer_count, depth_y)
        answers = [blocks[0]] + [swap(blocks[k], along_outer(k)) for k in range(1, outer_count)]
        kept, *leaving = combine(
            shared_hidden, shared_weights[2], high, low, answers, start, out_width, depth_y - 1
        )
        coming = [swap(block, k + 1) for k, block in enumerate(leaving)]
        kept, *leaving = call(
            functools.partial(add_kernel, depth_y - 1),
            [whole((rows, out_width), F32)] + [whole((rows, out_width), BF16)] * (DEPTH_Z - 1),
            kept,
            *coming,
        )
        finals += [kept] + [swap(block, along_z(k + 1)) for k, block in enumerate(leaving)]
    return call(
        functools.partial(finish_kernel, DEPTH_Z, out_width), whole((rows, model_width), BF16), *finals
    )


def solution(mesh):
    return jax.shard_map(
        per_device,
        mesh=mesh,
        in_specs=(
            P(("outer", "inner"), None),
            P(("outer", "inner"), None),
            P(("outer", "inner"), None),
            P(("outer", "inner"), None, None),
            P(("outer", "inner"), None, None),
            P(("outer", "inner"), None, None),
            P(None, "inner"),
            P(None, "inner"),
            P("inner", None),
        ),
        out_specs=P(("outer", "inner"), None),
        check_vma=False,
    )
```

time: 145 us -> 85.3 us (0.59)
  blocking collectives: 47 us -> 0 us
  Pallas kernels: 0 us -> 19.7 us
  matrix products: 19.3 us -> 0 us
  starting transfers between devices: 11.2 us -> 25.7 us
  between operations: 13.6 us -> 0.19 us
  waiting for transfers between devices: 34.1 us -> 24.3 us
  other arithmetic: 4.04 us -> 0.11 us
    all_gather x1 -> x0, blocking collectives: 47 us -> none  [per_device(): segment = lax.all_gather(tokens, 'inner', axis=0, tiled=True)]
    ppermute x0 -> x25, starting transfers between devices: none -> 25.7 us  [swap(): lax.ppermute(array, BOTH, [(at, at ^ distance) for at in range(device_cou...]
    all_to_all x2 -> x0, waiting for transfers between devices: 25 us -> none  [the longest x1 25 us: per_device(): lax.all_to_all(answer.reshape(received.shape), ('outer', 'inner'), split_...]
    ppermute x0 -> x25, waiting for transfers between devices: none -> 24.3 us  [swap(): lax.ppermute(array, BOTH, [(at, at ^ distance) for at in range(device_cou...]
    pallas_call x0 -> x14, Pallas kernels: none -> 19.7 us  [call(): pl.pallas_call(kernel, out_shape=out_shape, compiler_params=PARAMS, **more)]
    dot_general x5 -> x0, matrix products: 19.3 us -> none  [the longest x1 8.28 us: gated_mlp(): jnp.dot(hidden, down_matrix, preferred_element_type=jnp.float32)]
    unnamed x9 -> x14, local copies, waits for them, and re-layouts: 0.91 us -> 15 us
    all_to_all x2 -> x0, starting transfers between devices: 11.2 us -> none  [the longest x1 7.4 us: per_device(): lax.all_to_all(outbound, ('outer', 'inner'), split_axis=0, concat_axis=0,...]
  transfers between devices with their start and end apart: 3 -> 25, of which waited for: 2 -> 13; matrix products, arithmetic and copies ran while one was open for 23% -> 0% of each run, Pallas kernels for 0% -> 20%
where the time goes in v2:
time: 85.3 us; the launch traced here: 85.1 us
  starting transfers between devices  25.7 us (30%)
  waiting for transfers between devices  24.3 us (28%)
  Pallas kernels  19.7 us (23%)
  local copies, waits for them, and re-layouts  15 us (18%)
    ppermute x25, starting transfers between devices, swap(): lax.ppermute(array, BOTH, [(at, at ^ distance) for at in range(device_cou...  25.7 us
    ppermute x25, waiting for transfers between devices, swap(): lax.ppermute(array, BOTH, [(at, at ^ distance) for at in range(device_cou...  24.3 us
    pallas_call x14, Pallas kernels, call(): pl.pallas_call(kernel, out_shape=out_shape, compiler_params=PARAMS, **more)  19.7 us
    unnamed x14, local copies, waits for them, and re-layouts  15 us
  transfers between devices with their start and end apart: 25, of which 13 were waited for; matrix products, arithmetic and copies ran while one was open for 0% of the time, Pallas kernels for 20%

profile of v2, /device:TPU:0, one launch (start us, length us, event | category | flops | bytes accessed | tf_op | source)
XLA Modules:
  0.0 85.1 jit_solution(11316519078716414922)
XLA Ops:
  0.0 1.0 %shard_map.91.refs_0_ = bf16[16,3712]{1,0:T(8,128)(2,1)S(1)} custom-call(bf16[16,3584]{1,0:T(8,128)(2,1)} %tokens_ref.1, s32[8,16]{1,0:T(8,128)} %bitcast.12, s32[8,16]{1,0:T(8,128)} %bitcast.13), custom_call_target="tpu_custom_call" | custom-call | tf_op jit(solution)/shard_map/pallas_call | solution.py:38
  1.0 3.1 %collective-permute-start = (bf16[16,3712]{1,0:T(8,128)(2,1)S(1)}, bf16[16,3712]{1,0:T(8,128)(2,1)S(1)}, u32[]{:S(2)}, u32[]{:S(2)}) collective-permute-start(bf16[16,3712]{1,0:T(8,128)(2,1)S(1)} %shard_map.91.refs_0_), channel_id=1, source_target_pairs={{0,2},{1,3},{2,0},{3,1},{4,6},{5,7},{6,4},{7,5},{8,10},{9,11},{10,... | collective-permute-start | bytes 356360 | tf_op jit(solution)/shard_map/ppermute | solution.py:268
  4.1 2.6 %collective-permute-start.1 = (bf16[16,3712]{1,0:T(8,128)(2,1)S(1)}, bf16[16,3712]{1,0:T(8,128)(2,1)S(1)}, u32[]{:S(2)}, u32[]{:S(2)}) collective-permute-start(bf16[16,3712]{1,0:T(8,128)(2,1)S(1)} %shard_map.91.refs_0_), channel_id=1, source_target_pairs={{0,4},{1,5},{2,6},{3,7},{4,0},{5,1},{6,2},{7,3},{8,12},{9,13},{10,... | collective-permute-start | bytes 356360 | tf_op jit(solution)/shard_map/ppermute | solution.py:268
  6.6 7.3 %shard_map.92 = (bf16[3584,1024]{1,0:T(8,128)(2,1)S(1)}, bf16[3584,1024]{1,0:T(8,128)(2,1)S(1)}, bf16[1024,3584]{1,0:T(8,128)(2,1)S(1)}, f32[8,128]{1,0:T(8,128)S(1)}) custom-call(bf16[3584,1024]{1,0:T(8,128)(2,1)} %bitcast.9, bf16[3584,1024]{1,0:T(8,128)(2,1)} %bitcast.10, bf16[1024,3584]{1,0:T(8,128)(2,1)} %bitcast.11), custom_call_target="tpu_custom_call" | custom-call | tf_op jit(solution)/shard_map/pallas_call | solution.py:38
  13.9 2.9 %copy-done = bf16[1024,3584]{1,0:T(8,128)(2,1)} copy-done((bf16[1024,3584]{1,0:T(8,128)(2,1)}, bf16[1024,3584]{1,0:T(8,128)(2,1)S(1)}, u32[]{:S(2)}) %copy-start) | copy-done | bytes 7340056
  16.8 3.0 %copy-done.1 = bf16[3584,1024]{1,0:T(8,128)(2,1)} copy-done((bf16[3584,1024]{1,0:T(8,128)(2,1)}, bf16[3584,1024]{1,0:T(8,128)(2,1)S(1)}, u32[]{:S(2)}) %copy-start.1) | copy-done | bytes 7340056
  19.9 2.9 %copy-done.3 = bf16[3584,1024]{1,0:T(8,128)(2,1)} copy-done((bf16[3584,1024]{1,0:T(8,128)(2,1)}, bf16[3584,1024]{1,0:T(8,128)(2,1)S(1)}, u32[]{:S(2)}) %copy-start.3) | copy-done | bytes 7340056
  24.9 1.3 %shard_map.93 = (bf16[32,3584]{1,0:T(8,128)(2,1)S(1)}, bf16[32,3584]{1,0:T(8,128)(2,1)S(1)}, bf16[32,3584]{1,0:T(8,128)(2,1)S(1)}, bf16[32,3584]{1,0:T(8,128)(2,1)S(1)}) custom-call(s32[2]{0:T(128)S(1)} %pad_add_fusion.where_ref, bf16[16,3712]{1,0:T(8,128)(2,1)S(1)} %shard_map.91.refs_0_, bf16[16,3712]{1,0:T(8,128)(2,1)S(1)} %collective-permute-done.refs_1_, ...), custom_call_target="tpu_custom_call" | custom-call | tf_op jit(solution)/shard_map/pallas_call | solution.py:38
  26.2 1.8 %collective-permute-start.7 = (bf16[32,3584]{1,0:T(8,128)(2,1)S(1)}, bf16[32,3584]{1,0:T(8,128)(2,1)S(1)}, u32[]{:S(2)}, u32[]{:S(2)}) collective-permute-start(bf16[32,3584]{1,0:T(8,128)(2,1)S(1)} %get-tuple-element.51), channel_id=1, source_target_pairs={{0,16},{1,17},{2,18},{3,19},{4,20},{5,21},{6,22},{7,23},{8,24},{9,... | collective-permute-start | bytes 688136 | tf_op jit(solution)/shard_map/ppermute | solution.py:268
  27.9 1.5 %collective-permute-start.8 = (bf16[32,3584]{1,0:T(8,128)(2,1)S(1)}, bf16[32,3584]{1,0:T(8,128)(2,1)S(1)}, u32[]{:S(2)}, u32[]{:S(2)}) collective-permute-start(bf16[32,3584]{1,0:T(8,128)(2,1)S(1)} %get-tuple-element.52), channel_id=1, source_target_pairs={{0,1},{1,0},{2,3},{3,2},{4,5},{5,4},{6,7},{7,6},{8,9},{9,8},{10,11... | collective-permute-start | bytes 688136 | tf_op jit(solution)/shard_map/ppermute | solution.py:268
  29.8 4.9 %collective-permute-done.7.refs_1_ = bf16[32,3584]{1,0:T(8,128)(2,1)S(1)} collective-permute-done((bf16[32,3584]{1,0:T(8,128)(2,1)S(1)}, bf16[32,3584]{1,0:T(8,128)(2,1)S(1)}, u32[]{:S(2)}, u32[]{:S(2)}) %collective-permute-start.7) | collective-permute-done | bytes 229408 | tf_op jit(solution)/shard_map/ppermute | solution.py:268
  34.7 5.8 %collective-permute-done.8.refs_2_ = bf16[32,3584]{1,0:T(8,128)(2,1)S(1)} collective-permute-done((bf16[32,3584]{1,0:T(8,128)(2,1)S(1)}, bf16[32,3584]{1,0:T(8,128)(2,1)S(1)}, u32[]{:S(2)}, u32[]{:S(2)}) %collective-permute-start.8) | collective-permute-done | bytes 229408 | tf_op jit(solution)/shard_map/ppermute | solution.py:268
  40.4 1.5 %collective-permute-start.10 = (bf16[64,3712]{1,0:T(8,128)(2,1)S(1)}, bf16[64,3712]{1,0:T(8,128)(2,1)S(1)}, u32[]{:S(2)}, u32[]{:S(2)}) collective-permute-start(bf16[64,3712]{1,0:T(8,128)(2,1)S(1)} %pad_maximum_fusion.refs_0_), channel_id=1, source_target_pairs={{0,1},{1,0},{2,3},{3,2},{4,5},{5,4},{6,7},{7,6},{8,9},{9,8},{10,11... | collective-permute-start | bytes 1425416 | tf_op jit(solution)/shard_map/ppermute | solution.py:268
  42.0 3.1 %copy-done.2 = bf16[3584,1024]{1,0:T(8,128)(2,1)S(1)} copy-done((bf16[3584,1024]{1,0:T(8,128)(2,1)S(1)}, bf16[3584,1024]{1,0:T(8,128)(2,1)}, u32[]{:S(2)}) %copy-start.2) | copy-done | bytes 7340056
  45.0 3.1 %copy-done.4 = bf16[3584,1024]{1,0:T(8,128)(2,1)S(1)} copy-done((bf16[3584,1024]{1,0:T(8,128)(2,1)S(1)}, bf16[3584,1024]{1,0:T(8,128)(2,1)}, u32[]{:S(2)}) %copy-start.4) | copy-done | bytes 7340056
  48.1 2.1 %shard_map.97.hidden_ref = bf16[128,1024]{1,0:T(8,128)(2,1)S(1)} custom-call(bf16[32,3584]{1,0:T(8,128)(2,1)S(1)} %get-tuple-element.50.refs_0_, bf16[32,3584]{1,0:T(8,128)(2,1)S(1)} %collective-permute-done.7.refs_1_, bf16[32,3584]{1,0:T(8,128)(2,1)S(1)} %collective-permute-done.8.refs_2_, bf16[32,3584]{1,0:T(8,128)(2,1)S(1)} %collective-permute-done.9.refs_3_, ...), custom_call_target="tpu_custom_call" | custom-call | tf_op jit(solution)/shard_map/pallas_call | solution.py:38
  51.6 1.3 %collective-permute-start.20 = (bf16[32,1792]{1,0:T(8,128)(2,1)S(1)}, bf16[32,1792]{1,0:T(8,128)(2,1)S(1)}, u32[]{:S(2)}, u32[]{:S(2)}) collective-permute-start(bf16[32,1792]{1,0:T(8,128)(2,1)S(1)} %get-tuple-element.76), channel_id=1, source_target_pairs={{0,24},{1,25},{2,26},{3,27},{4,28},{5,29},{6,30},{7,31},{8,16},{9,... | collective-permute-start | bytes 344072 | tf_op jit(solution)/shard_map/ppermute | solution.py:268
  52.8 0.7 shard_map.98
  54.4 1.0 %collective-permute-start.13 = (bf16[32,1792]{1,0:T(8,128)(2,1)S(1)}, bf16[32,1792]{1,0:T(8,128)(2,1)S(1)}, u32[]{:S(2)}, u32[]{:S(2)}) collective-permute-start(bf16[32,1792]{1,0:T(8,128)(2,1)S(1)} %get-tuple-element.66), channel_id=1, source_target_pairs={{0,24},{1,25},{2,26},{3,27},{4,28},{5,29},{6,30},{7,31},{8,16},{9,... | collective-permute-start | bytes 344072 | tf_op jit(solution)/shard_map/ppermute | solution.py:268
  55.4 3.2 %shard_map.94 = (bf16[3584,256]{1,0:T(8,128)(2,1)S(1)}, bf16[3584,256]{1,0:T(8,128)(2,1)S(1)}, bf16[256,3584]{1,0:T(8,128)(2,1)S(1)}, f32[8,128]{1,0:T(8,128)}) custom-call(bf16[3584,256]{1,0:T(8,128)(2,1)} %refs_0_.1, bf16[3584,256]{1,0:T(8,128)(2,1)} %refs_1_.1, bf16[256,3584]{1,0:T(8,128)(2,1)} %refs_2_.1), custom_call_target="tpu_custom_call" | custom-call | tf_op jit(solution)/shard_map/pallas_call | solution.py:38
  58.7 1.1 %shard_map.96 = (bf16[128,128]{1,0:T(8,128)(2,1)S(1)}, bf16[128,128]{1,0:T(8,128)(2,1)S(1)}) custom-call(s32[2]{0:T(128)S(1)} %pad_add_fusion.where_ref, bf16[64,3712]{1,0:T(8,128)(2,1)S(1)} %pad_maximum_fusion.refs_0_, bf16[64,3712]{1,0:T(8,128)(2,1)S(1)} %collective-permute-done.10.refs_1_), custom_call_target="tpu_custom_call" | custom-call | tf_op jit(solution)/shard_map/pallas_call | solution.py:38
  59.7 0.7 shard_map.95.hidden_ref
  61.9 1.6 %collective-permute-done.13.refs_3_ = bf16[32,1792]{1,0:T(8,128)(2,1)S(1)} collective-permute-done((bf16[32,1792]{1,0:T(8,128)(2,1)S(1)}, bf16[32,1792]{1,0:T(8,128)(2,1)S(1)}, u32[]{:S(2)}, u32[]{:S(2)}) %collective-permute-start.13) | collective-permute-done | bytes 114720 | tf_op jit(solution)/shard_map/ppermute | solution.py:268
  64.5 4.9 %collective-permute-done.21.refs_0_ = bf16[64,1792]{1,0:T(8,128)(2,1)S(1)} collective-permute-done((bf16[64,1792]{1,0:T(8,128)(2,1)S(1)}, bf16[64,1792]{1,0:T(8,128)(2,1)S(1)}, u32[]{:S(2)}, u32[]{:S(2)}) %collective-permute-start.21) | collective-permute-done | bytes 229408 | tf_op jit(solution)/shard_map/ppermute | solution.py:268
  69.5 0.8 collective-permute-start.22
  70.3 3.5 %collective-permute-start.23 = (bf16[16,1792]{1,0:T(8,128)(2,1)S(1)}, bf16[16,1792]{1,0:T(8,128)(2,1)S(1)}, u32[]{:S(2)}, u32[]{:S(2)}) collective-permute-start(bf16[16,1792]{1,0:T(8,128)(2,1)S(1)} %get-tuple-element.81), channel_id=1, source_target_pairs={{0,4},{1,5},{2,6},{3,7},{4,0},{5,1},{6,2},{7,3},{8,12},{9,13},{10,... | collective-permute-start | bytes 172040 | tf_op jit(solution)/shard_map/ppermute | solution.py:268
  74.1 0.7 collective-permute-start.15
  74.9 3.5 %collective-permute-start.16 = (bf16[16,1792]{1,0:T(8,128)(2,1)S(1)}, bf16[16,1792]{1,0:T(8,128)(2,1)S(1)}, u32[]{:S(2)}, u32[]{:S(2)}) collective-permute-start(bf16[16,1792]{1,0:T(8,128)(2,1)S(1)} %get-tuple-element.71), channel_id=1, source_target_pairs={{0,4},{1,5},{2,6},{3,7},{4,0},{5,1},{6,2},{7,3},{8,12},{9,13},{10,... | collective-permute-start | bytes 172040 | tf_op jit(solution)/shard_map/ppermute | solution.py:268
  78.6 1.8 %collective-permute-done.24.refs_7_ = bf16[16,1792]{1,0:T(8,128)(2,1)S(1)} collective-permute-done((bf16[16,1792]{1,0:T(8,128)(2,1)S(1)}, bf16[16,1792]{1,0:T(8,128)(2,1)S(1)}, u32[]{:S(2)}, u32[]{:S(2)}) %collective-permute-start.24) | collective-permute-done | bytes 57376 | tf_op jit(solution)/shard_map/ppermute | solution.py:268
  80.4 2.5 %collective-permute-done.16.refs_2_ = bf16[16,1792]{1,0:T(8,128)(2,1)S(1)} collective-permute-done((bf16[16,1792]{1,0:T(8,128)(2,1)S(1)}, bf16[16,1792]{1,0:T(8,128)(2,1)S(1)}, u32[]{:S(2)}, u32[]{:S(2)}) %collective-permute-start.16) | collective-permute-done | bytes 57376 | tf_op jit(solution)/shard_map/ppermute | solution.py:268
  82.9 1.5 %collective-permute-done.17.refs_3_ = bf16[16,1792]{1,0:T(8,128)(2,1)S(1)} collective-permute-done((bf16[16,1792]{1,0:T(8,128)(2,1)S(1)}, bf16[16,1792]{1,0:T(8,128)(2,1)S(1)}, u32[]{:S(2)}, u32[]{:S(2)}) %collective-permute-start.17) | collective-permute-done | bytes 57376 | tf_op jit(solution)/shard_map/ppermute | solution.py:268
  84.3 0.7 shard_map.104
  (49 shorter events, 7.8 us)
Async XLA Ops:
  1.0 21.8 %collective-permute-start = (bf16[16,3712]{1,0:T(8,128)(2,1)S(1)}, bf16[16,3712]{1,0:T(8,128)(2,1)S(1)}, u32[]{:S(2)}, u32[]{:S(2)}) collective-permute-start(bf16[16,3712]{1,0:T(8,128)(2,1)S(1)} %shard_map.91.refs_0_), channel_id=1, source_target_pairs={{0,2},{1,3},{2,0},{3,1},{4,6},{5,7},{6,4},{7,5},{8,10},{9,11},{10,... | collective-permute-start | bytes 356360 | tf_op jit(solution)/shard_map/ppermute | solution.py:268
  4.1 18.7 %collective-permute-start.1 = (bf16[16,3712]{1,0:T(8,128)(2,1)S(1)}, bf16[16,3712]{1,0:T(8,128)(2,1)S(1)}, u32[]{:S(2)}, u32[]{:S(2)}) collective-permute-start(bf16[16,3712]{1,0:T(8,128)(2,1)S(1)} %shard_map.91.refs_0_), channel_id=1, source_target_pairs={{0,4},{1,5},{2,6},{3,7},{4,0},{5,1},{6,2},{7,3},{8,12},{9,13},{10,... | collective-permute-start | bytes 356360 | tf_op jit(solution)/shard_map/ppermute | solution.py:268
  6.6 16.2 %collective-permute-start.2 = (bf16[16,3712]{1,0:T(8,128)(2,1)S(1)}, bf16[16,3712]{1,0:T(8,128)(2,1)S(1)}, u32[]{:S(2)}, u32[]{:S(2)}) collective-permute-start(bf16[16,3712]{1,0:T(8,128)(2,1)S(1)} %shard_map.91.refs_0_), channel_id=1, source_target_pairs={{0,6},{1,7},{2,4},{3,5},{4,2},{5,3},{6,0},{7,1},{8,14},{9,15},{10,... | collective-permute-start | bytes 356360 | tf_op jit(solution)/shard_map/ppermute | solution.py:268
  13.9 2.9 %copy-start = (bf16[1024,3584]{1,0:T(8,128)(2,1)}, bf16[1024,3584]{1,0:T(8,128)(2,1)S(1)}, u32[]{:S(2)}) copy-start(bf16[1024,3584]{1,0:T(8,128)(2,1)S(1)} %get-tuple-element.62.down_ref) | copy-start | bytes 22020100
  16.8 3.0 %copy-start.1 = (bf16[3584,1024]{1,0:T(8,128)(2,1)}, bf16[3584,1024]{1,0:T(8,128)(2,1)S(1)}, u32[]{:S(2)}) copy-start(bf16[3584,1024]{1,0:T(8,128)(2,1)S(1)} %get-tuple-element.60.refs_4_) | copy-start | bytes 22020100
  19.9 2.9 %copy-start.3 = (bf16[3584,1024]{1,0:T(8,128)(2,1)}, bf16[3584,1024]{1,0:T(8,128)(2,1)S(1)}, u32[]{:S(2)}) copy-start(bf16[3584,1024]{1,0:T(8,128)(2,1)S(1)} %get-tuple-element.61.refs_5_) | copy-start | bytes 22020100
  22.8 1.4 %collective-permute-start.3 = (bf16[16,3712]{1,0:T(8,128)(2,1)S(1)}, bf16[16,3712]{1,0:T(8,128)(2,1)S(1)}, u32[]{:S(2)}, u32[]{:S(2)}) collective-permute-start(bf16[16,3712]{1,0:T(8,128)(2,1)S(1)} %shard_map.91.refs_0_), channel_id=1, source_target_pairs={{0,8},{1,9},{2,10},{3,11},{4,12},{5,13},{6,14},{7,15},{8,0},{9,1},... | collective-permute-start | bytes 356360 | tf_op jit(solution)/shard_map/ppermute | solution.py:268
  22.9 1.5 %collective-permute-start.4 = (bf16[16,3712]{1,0:T(8,128)(2,1)S(1)}, bf16[16,3712]{1,0:T(8,128)(2,1)S(1)}, u32[]{:S(2)}, u32[]{:S(2)}) collective-permute-start(bf16[16,3712]{1,0:T(8,128)(2,1)S(1)} %collective-permute-done.refs_1_), channel_id=1, source_target_pairs={{0,8},{1,9},{2,10},{3,11},{4,12},{5,13},{6,14},{7,15},{8,0},{9,1},... | collective-permute-start | bytes 356360 | tf_op jit(solution)/shard_map/ppermute | solution.py:268
  23.4 1.3 %collective-permute-start.5 = (bf16[16,3712]{1,0:T(8,128)(2,1)S(1)}, bf16[16,3712]{1,0:T(8,128)(2,1)S(1)}, u32[]{:S(2)}, u32[]{:S(2)}) collective-permute-start(bf16[16,3712]{1,0:T(8,128)(2,1)S(1)} %collective-permute-done.1.refs_2_), channel_id=1, source_target_pairs={{0,8},{1,9},{2,10},{3,11},{4,12},{5,13},{6,14},{7,15},{8,0},{9,1},... | collective-permute-start | bytes 356360 | tf_op jit(solution)/shard_map/ppermute | solution.py:268
  23.5 1.4 %collective-permute-start.6 = (bf16[16,3712]{1,0:T(8,128)(2,1)S(1)}, bf16[16,3712]{1,0:T(8,128)(2,1)S(1)}, u32[]{:S(2)}, u32[]{:S(2)}) collective-permute-start(bf16[16,3712]{1,0:T(8,128)(2,1)S(1)} %collective-permute-done.2.refs_3_), channel_id=1, source_target_pairs={{0,8},{1,9},{2,10},{3,11},{4,12},{5,13},{6,14},{7,15},{8,0},{9,1},... | collective-permute-start | bytes 356360 | tf_op jit(solution)/shard_map/ppermute | solution.py:268
  26.2 8.5 %collective-permute-start.7 = (bf16[32,3584]{1,0:T(8,128)(2,1)S(1)}, bf16[32,3584]{1,0:T(8,128)(2,1)S(1)}, u32[]{:S(2)}, u32[]{:S(2)}) collective-permute-start(bf16[32,3584]{1,0:T(8,128)(2,1)S(1)} %get-tuple-element.51), channel_id=1, source_target_pairs={{0,16},{1,17},{2,18},{3,19},{4,20},{5,21},{6,22},{7,23},{8,24},{9,... | collective-permute-start | bytes 688136 | tf_op jit(solution)/shard_map/ppermute | solution.py:268
  27.9 12.5 %collective-permute-start.8 = (bf16[32,3584]{1,0:T(8,128)(2,1)S(1)}, bf16[32,3584]{1,0:T(8,128)(2,1)S(1)}, u32[]{:S(2)}, u32[]{:S(2)}) collective-permute-start(bf16[32,3584]{1,0:T(8,128)(2,1)S(1)} %get-tuple-element.52), channel_id=1, source_target_pairs={{0,1},{1,0},{2,3},{3,2},{4,5},{5,4},{6,7},{7,6},{8,9},{9,8},{10,11... | collective-permute-start | bytes 688136 | tf_op jit(solution)/shard_map/ppermute | solution.py:268
  29.5 11.0 %collective-permute-start.9 = (bf16[32,3584]{1,0:T(8,128)(2,1)S(1)}, bf16[32,3584]{1,0:T(8,128)(2,1)S(1)}, u32[]{:S(2)}, u32[]{:S(2)}) collective-permute-start(bf16[32,3584]{1,0:T(8,128)(2,1)S(1)} %get-tuple-element.53), channel_id=1, source_target_pairs={{0,17},{1,16},{2,19},{3,18},{4,21},{5,20},{6,23},{7,22},{8,25},{9,... | collective-permute-start | bytes 688136 | tf_op jit(solution)/shard_map/ppermute | solution.py:268
  29.7 20.5 %slice-start = ((s8[7340032]{0:T(1024)(128)(4,1)}), s8[4194304]{0:T(1024)(128)(4,1)S(1)}, s32[]{:S(2)}) async-start(s8[7340032]{0:T(1024)(128)(4,1)} %bitcast.7), calls=%async_computation | async-start | bytes 8388608
  40.4 14.0 %collective-permute-start.10 = (bf16[64,3712]{1,0:T(8,128)(2,1)S(1)}, bf16[64,3712]{1,0:T(8,128)(2,1)S(1)}, u32[]{:S(2)}, u32[]{:S(2)}) collective-permute-start(bf16[64,3712]{1,0:T(8,128)(2,1)S(1)} %pad_maximum_fusion.refs_0_), channel_id=1, source_target_pairs={{0,1},{1,0},{2,3},{3,2},{4,5},{5,4},{6,7},{7,6},{8,9},{9,8},{10,11... | collective-permute-start | bytes 1425416 | tf_op jit(solution)/shard_map/ppermute | solution.py:268
  42.0 3.1 %copy-start.2 = (bf16[3584,1024]{1,0:T(8,128)(2,1)S(1)}, bf16[3584,1024]{1,0:T(8,128)(2,1)}, u32[]{:S(2)}) copy-start(bf16[3584,1024]{1,0:T(8,128)(2,1)} %copy-done.1) | copy-start | bytes 22020100
  45.0 3.1 %copy-start.4 = (bf16[3584,1024]{1,0:T(8,128)(2,1)S(1)}, bf16[3584,1024]{1,0:T(8,128)(2,1)}, u32[]{:S(2)}) copy-start(bf16[3584,1024]{1,0:T(8,128)(2,1)} %copy-done.3) | copy-start | bytes 22020100
  48.1 2.1 %slice-start.1 = ((s8[7340032]{0:T(1024)(128)(4,1)}), s8[3145728]{0:T(1024)(128)(4,1)S(1)}, s32[]{:S(2)}) async-start(s8[7340032]{0:T(1024)(128)(4,1)} %bitcast.7), calls=%async_computation.1 | async-start | bytes 6291456
  50.9 3.0 %collective-permute-start.18 = (bf16[32,1792]{1,0:T(8,128)(2,1)S(1)}, bf16[32,1792]{1,0:T(8,128)(2,1)S(1)}, u32[]{:S(2)}, u32[]{:S(2)}) collective-permute-start(bf16[32,1792]{1,0:T(8,128)(2,1)S(1)} %get-tuple-element.74), channel_id=1, source_target_pairs={{0,8},{1,9},{2,10},{3,11},{4,12},{5,13},{6,14},{7,15},{8,0},{9,1},... | collective-permute-start | bytes 344072 | tf_op jit(solution)/shard_map/ppermute | solution.py:268
  51.0 9.5 %collective-permute-start.19 = (bf16[32,1792]{1,0:T(8,128)(2,1)S(1)}, bf16[32,1792]{1,0:T(8,128)(2,1)S(1)}, u32[]{:S(2)}, u32[]{:S(2)}) collective-permute-start(bf16[32,1792]{1,0:T(8,128)(2,1)S(1)} %get-tuple-element.75), channel_id=1, source_target_pairs={{0,16},{1,17},{2,18},{3,19},{4,20},{5,21},{6,22},{7,23},{8,24},{9,... | collective-permute-start | bytes 344072 | tf_op jit(solution)/shard_map/ppermute | solution.py:268
  51.6 8.9 %collective-permute-start.20 = (bf16[32,1792]{1,0:T(8,128)(2,1)S(1)}, bf16[32,1792]{1,0:T(8,128)(2,1)S(1)}, u32[]{:S(2)}, u32[]{:S(2)}) collective-permute-start(bf16[32,1792]{1,0:T(8,128)(2,1)S(1)} %get-tuple-element.76), channel_id=1, source_target_pairs={{0,24},{1,25},{2,26},{3,27},{4,28},{5,29},{6,30},{7,31},{8,16},{9,... | collective-permute-start | bytes 344072 | tf_op jit(solution)/shard_map/ppermute | solution.py:268
  53.5 8.0 %collective-permute-start.11 = (bf16[32,1792]{1,0:T(8,128)(2,1)S(1)}, bf16[32,1792]{1,0:T(8,128)(2,1)S(1)}, u32[]{:S(2)}, u32[]{:S(2)}) collective-permute-start(bf16[32,1792]{1,0:T(8,128)(2,1)S(1)} %get-tuple-element.64), channel_id=1, source_target_pairs={{0,8},{1,9},{2,10},{3,11},{4,12},{5,13},{6,14},{7,15},{8,0},{9,1},... | collective-permute-start | bytes 344072 | tf_op jit(solution)/shard_map/ppermute | solution.py:268
  53.9 8.0 %collective-permute-start.12 = (bf16[32,1792]{1,0:T(8,128)(2,1)S(1)}, bf16[32,1792]{1,0:T(8,128)(2,1)S(1)}, u32[]{:S(2)}, u32[]{:S(2)}) collective-permute-start(bf16[32,1792]{1,0:T(8,128)(2,1)S(1)} %get-tuple-element.65), channel_id=1, source_target_pairs={{0,16},{1,17},{2,18},{3,19},{4,20},{5,21},{6,22},{7,23},{8,24},{9,... | collective-permute-start | bytes 344072 | tf_op jit(solution)/shard_map/ppermute | solution.py:268
  54.4 9.0 %collective-permute-start.13 = (bf16[32,1792]{1,0:T(8,128)(2,1)S(1)}, bf16[32,1792]{1,0:T(8,128)(2,1)S(1)}, u32[]{:S(2)}, u32[]{:S(2)}) collective-permute-start(bf16[32,1792]{1,0:T(8,128)(2,1)S(1)} %get-tuple-element.66), channel_id=1, source_target_pairs={{0,24},{1,25},{2,26},{3,27},{4,28},{5,29},{6,30},{7,31},{8,16},{9,... | collective-permute-start | bytes 344072 | tf_op jit(solution)/shard_map/ppermute | solution.py:268
  61.0 8.4 %collective-permute-start.21 = (bf16[64,1792]{1,0:T(8,128)(2,1)S(1)}, bf16[64,1792]{1,0:T(8,128)(2,1)S(1)}, u32[]{:S(2)}, u32[]{:S(2)}) collective-permute-start(bf16[64,1792]{1,0:T(8,128)(2,1)S(1)} %get-tuple-element.78), channel_id=1, source_target_pairs={{0,1},{1,0},{2,3},{3,2},{4,5},{5,4},{6,7},{7,6},{8,9},{9,8},{10,11... | collective-permute-start | bytes 688136 | tf_op jit(solution)/shard_map/ppermute | solution.py:268
  64.0 10.1 %collective-permute-start.14 = (bf16[64,1792]{1,0:T(8,128)(2,1)S(1)}, bf16[64,1792]{1,0:T(8,128)(2,1)S(1)}, u32[]{:S(2)}, u32[]{:S(2)}) collective-permute-start(bf16[64,1792]{1,0:T(8,128)(2,1)S(1)} %get-tuple-element.68), channel_id=1, source_target_pairs={{0,1},{1,0},{2,3},{3,2},{4,5},{5,4},{6,7},{7,6},{8,9},{9,8},{10,11... | collective-permute-start | bytes 688136 | tf_op jit(solution)/shard_map/ppermute | solution.py:268
  69.5 8.9 %collective-permute-start.22 = (bf16[16,1792]{1,0:T(8,128)(2,1)S(1)}, bf16[16,1792]{1,0:T(8,128)(2,1)S(1)}, u32[]{:S(2)}, u32[]{:S(2)}) collective-permute-start(bf16[16,1792]{1,0:T(8,128)(2,1)S(1)} %get-tuple-element.80), channel_id=1, source_target_pairs={{0,2},{1,3},{2,0},{3,1},{4,6},{5,7},{6,4},{7,5},{8,10},{9,11},{10,... | collective-permute-start | bytes 172040 | tf_op jit(solution)/shard_map/ppermute | solution.py:268
  70.3 8.3 %collective-permute-start.23 = (bf16[16,1792]{1,0:T(8,128)(2,1)S(1)}, bf16[16,1792]{1,0:T(8,128)(2,1)S(1)}, u32[]{:S(2)}, u32[]{:S(2)}) collective-permute-start(bf16[16,1792]{1,0:T(8,128)(2,1)S(1)} %get-tuple-element.81), channel_id=1, source_target_pairs={{0,4},{1,5},{2,6},{3,7},{4,0},{5,1},{6,2},{7,3},{8,12},{9,13},{10,... | collective-permute-start | bytes 172040 | tf_op jit(solution)/shard_map/ppermute | solution.py:268
  73.8 6.6 %collective-permute-start.24 = (bf16[16,1792]{1,0:T(8,128)(2,1)S(1)}, bf16[16,1792]{1,0:T(8,128)(2,1)S(1)}, u32[]{:S(2)}, u32[]{:S(2)}) collective-permute-start(bf16[16,1792]{1,0:T(8,128)(2,1)S(1)} %get-tuple-element.82), channel_id=1, source_target_pairs={{0,6},{1,7},{2,4},{3,5},{4,2},{5,3},{6,0},{7,1},{8,14},{9,15},{10,... | collective-permute-start | bytes 172040 | tf_op jit(solution)/shard_map/ppermute | solution.py:268
  74.1 6.2 %collective-permute-start.15 = (bf16[16,1792]{1,0:T(8,128)(2,1)S(1)}, bf16[16,1792]{1,0:T(8,128)(2,1)S(1)}, u32[]{:S(2)}, u32[]{:S(2)}) collective-permute-start(bf16[16,1792]{1,0:T(8,128)(2,1)S(1)} %get-tuple-element.70), channel_id=1, source_target_pairs={{0,2},{1,3},{2,0},{3,1},{4,6},{5,7},{6,4},{7,5},{8,10},{9,11},{10,... | collective-permute-start | bytes 172040 | tf_op jit(solution)/shard_map/ppermute | solution.py:268
  74.9 8.0 %collective-permute-start.16 = (bf16[16,1792]{1,0:T(8,128)(2,1)S(1)}, bf16[16,1792]{1,0:T(8,128)(2,1)S(1)}, u32[]{:S(2)}, u32[]{:S(2)}) collective-permute-start(bf16[16,1792]{1,0:T(8,128)(2,1)S(1)} %get-tuple-element.71), channel_id=1, source_target_pairs={{0,4},{1,5},{2,6},{3,7},{4,0},{5,1},{6,2},{7,3},{8,12},{9,13},{10,... | collective-permute-start | bytes 172040 | tf_op jit(solution)/shard_map/ppermute | solution.py:268
  78.4 6.0 %collective-permute-start.17 = (bf16[16,1792]{1,0:T(8,128)(2,1)S(1)}, bf16[16,1792]{1,0:T(8,128)(2,1)S(1)}, u32[]{:S(2)}, u32[]{:S(2)}) collective-permute-start(bf16[16,1792]{1,0:T(8,128)(2,1)S(1)} %get-tuple-element.72), channel_id=1, source_target_pairs={{0,6},{1,7},{2,4},{3,5},{4,2},{5,3},{6,0},{7,1},{8,14},{9,15},{10,... | collective-permute-start | bytes 172040 | tf_op jit(solution)/shard_map/ppermute | solution.py:268

commit v3 on v2

--- a/solution.py
+++ b/solution.py
@@ -18,7 +18,6 @@
 F32 = jnp.float32
 PARAMS = pltpu.CompilerParams(vmem_limit_bytes=16 * 1024 * 1024)
 IN_VMEM = pl.BlockSpec(memory_space=pltpu.VMEM)
-IN_SMEM = pl.BlockSpec(memory_space=pltpu.SMEM)
 ANYWHERE = pl.BlockSpec(memory_space=pl.ANY)
 
 
@@ -53,6 +52,10 @@
 
 def far(array):
     return pltpu.with_memory_space_constraint(array, pltpu.HBM)
+
+
+def near(array):
+    return pltpu.with_memory_space_constraint(array, pltpu.VMEM)
 
 
 def after(array, *others):
@@ -131,9 +134,9 @@
     return hit, weight
 
 
-def select_kernel(width, block_rows, capacity, inner_count, chips_x, blocks, where_ref, *refs):
+def select_kernel(width, block_rows, capacity, inner_count, chips_x, blocks, *refs):
     pieces, outs = refs[:blocks], refs[blocks + 1:]
-    outer_at, inner_at = where_ref[0], where_ref[1]
+    outer_at, inner_at = lax.axis_index("outer"), lax.axis_index("inner")
 
     def expert_of(group):
         along_y = lax.div(group, jnp.int32(chips_x))
@@ -151,21 +154,23 @@
 
 def hidden_kernel(width, blocks, *refs):
     pieces = refs[:blocks]
-    gate_ref, up_ref, out_ref = refs[blocks:]
+    gate_ref, up_ref, _, out_ref = refs[blocks:]
     rows = jnp.concatenate([piece[:, :width] for piece in pieces], axis=0)
     gate = dot(rows, gate_ref[...])
     up = dot(rows, up_ref[...])
     out_ref[...] = (gate / (1.0 + jnp.exp(-gate)) * up).astype(BF16)
 
 
-def hidden(pieces, gate, up):
+def hidden(pieces, gate, up, loaded):
     shape = (sum(piece.shape[0] for piece in pieces), gate.shape[1])
     return call(
         functools.partial(hidden_kernel, gate.shape[0], len(pieces)),
         whole(shape, BF16),
         *pieces,
-        gate,
-        up,
+        near(gate),
+        near(up),
+        loaded,
+        in_specs=[IN_VMEM] * (len(pieces) + 2) + [ANYWHERE],
     )
 
 
@@ -183,13 +188,13 @@
         functools.partial(down_kernel, start, width, outer_count // CORES, depth_y),
         [whole((rows.shape[0] // outer_count, width), BF16)] * outer_count,
         rows,
-        matrix,
-    )
-
-
-def table_kernel(width, block_rows, capacity, inner_count, group_count, blocks, where_ref, *refs):
+        near(matrix),
+    )
+
+
+def table_kernel(width, block_rows, capacity, inner_count, group_count, blocks, *refs):
     pieces, (high_ref, low_ref) = refs[:blocks], refs[blocks:]
-    outer_at, inner_at = where_ref[0], where_ref[1]
+    outer_at, inner_at = lax.axis_index("outer"), lax.axis_index("inner")
     meta = jnp.concatenate([piece[:, width:] for piece in pieces], axis=0).astype(F32)
     hit, weight = routing(
         meta, block_rows, capacity, group_count, lambda group: (outer_at ^ group) * inner_count + inner_at
@@ -217,7 +222,7 @@
         functools.partial(combine_kernel, len(answers), start, width),
         [whole((each, width), F32)] + [whole((each, width), BF16)] * sends,
         shared_hidden,
-        shared_down,
+        near(shared_down),
         high,
         low,
         *answers,
@@ -262,7 +267,6 @@
     chips_x = outer_count // CORES
     capacity = TOPK // TOP_GROUPS * rows // inner_count
     device_count = inner_count * outer_count
-    where = jnp.stack([lax.axis_index("outer"), lax.axis_index("inner")]).astype(jnp.int32)
 
     def swap(array, distance):
         return lax.ppermute(array, BOTH, [(at, at ^ distance) for at in range(device_count)])
@@ -274,10 +278,17 @@
         return k * inner_count
 
     sent = prepare(tokens, experts, gate_score)
+    column = [sent] + [None] * (DEPTH_Z - 1)
+    for k in reversed(range(1, DEPTH_Z)):
+        column[k] = swap(sent, along_z(k))
+    beside = [swap(sent, k) for k in range(1, depth_y)]
+    other = [swap(sent, along_outer(1))]
     *expert_weights, loaded = prefetch(expert_gate[0], expert_up[0], expert_down[0])
-    column = [sent] + [swap(sent, along_z(k)) for k in range(1, DEPTH_Z)]
-    *column, loaded = lax.optimization_barrier((*column, loaded))
-    at_hand = column + [swap(block, along_outer(1)) for block in column]
+    *beside, loaded = lax.optimization_barrier((*beside, loaded))
+    for k in range(1, DEPTH_Z):
+        column[k], loaded = lax.optimization_barrier((column[k], loaded))
+        other.append(swap(column[k], along_outer(1)))
+    at_hand = column + other
 
     groups = depth_y * chips_x
     blocks = call(
@@ -285,37 +296,42 @@
             select_kernel, model_width, rows, capacity, inner_count, chips_x, len(at_hand)
         ),
         [whole((CORES * DEPTH_Z * capacity, model_width), BF16)] * groups,
-        where,
         *at_hand,
         loaded,
-        in_specs=[IN_SMEM] + [IN_VMEM] * len(at_hand) + [ANYWHERE],
-    )
-    arrived = [blocks[0]]
-    for at in range(1, groups):
+        in_specs=[IN_VMEM] * len(at_hand) + [ANYWHERE],
+        out_specs=[IN_VMEM] * groups,
+    )
+    arrived = [blocks[0]] + [None] * (groups - 1)
+    for at in reversed(range(1, groups)):
         along_y, along_x = at // chips_x, at % chips_x
-        arrived.append(swap(blocks[at], along_y + along_outer(along_x * CORES)))
-    expert_hidden = hidden(arrived, *expert_weights[:2])
-
-    *shared_weights, _ = prefetch(shared_gate, shared_up, shared_down)
-    dense = after(jnp.concatenate(column, axis=0), *arrived)
-    segment = [dense] + [swap(dense, k) for k in range(1, depth_y)]
+        arrived[at] = swap(blocks[at], along_y + along_outer(along_x * CORES))
+
+    segment = list(column)
+    for block in beside:
+        block = after(block, *blocks)
+        segment.append(block)
+        segment += [swap(block, along_z(k)) for k in range(1, DEPTH_Z)]
+    *shared_weights, loaded = prefetch(shared_gate, shared_up, shared_down)
+    *arrived, loaded = lax.optimization_barrier((*arrived, loaded))
+    expert_hidden = hidden(arrived, *expert_weights[:2], loaded)
     high, low = call(
         functools.partial(
             table_kernel, model_width, rows, capacity, inner_count, outer_count, len(segment)
         ),
         [whole((rows * inner_count, device_count * capacity), BF16)] * 2,
-        where,
         *segment,
-        in_specs=[IN_SMEM] + [IN_VMEM] * len(segment),
-    )
-    shared_hidden = hidden(segment, *shared_weights[:2])
+        in_specs=[IN_VMEM] * len(segment),
+    )
+    shared_hidden = hidden(segment, *shared_weights[:2], loaded)
 
     out_width = model_width // OUT_CUTS
     finals = []
     for at in range(OUT_CUTS):
         start = at * out_width
         blocks = down(expert_hidden, expert_weights[2], start, out_width, outer_count, depth_y)
-        answers = [blocks[0]] + [swap(blocks[k], along_outer(k)) for k in range(1, outer_count)]
+        answers = [blocks[0]] + [None] * (outer_count - 1)
+        for k in reversed(range(1, outer_count)):
+            answers[k] = swap(blocks[k], along_outer(k))
         kept, *leaving = combine(
             shared_hidden, shared_weights[2], high, low, answers, start, out_width, depth_y - 1
         )
@@ -326,7 +342,8 @@
             kept,
             *coming,
         )
-        finals += [kept] + [swap(block, along_z(k + 1)) for k, block in enumerate(leaving)]
+        coming = [swap(leaving[k - 1], along_z(k)) for k in reversed(range(1, DEPTH_Z))]
+        finals += [kept] + coming
     return call(
         functools.partial(finish_kernel, DEPTH_Z, out_width), whole((rows, model_width), BF16), *finals
     )

time: 85.3 us -> 67.5 us (0.79)
  local copies, waits for them, and re-layouts: 15 us -> 0 us
  waiting for transfers between devices: 24.3 us -> 18.3 us
  starting transfers between devices: 25.7 us -> 30.9 us
  Pallas kernels: 19.7 us -> 18.1 us
    unnamed x14 -> x0, local copies, waits for them, and re-layouts: 15 us -> none
    ppermute x25 -> x28, waiting for transfers between devices: 24.3 us -> 18.3 us  [swap(): lax.ppermute(array, BOTH, [(at, at ^ distance) for at in range(device_cou...]
    ppermute x25 -> x28, starting transfers between devices: 25.7 us -> 30.9 us  [swap(): lax.ppermute(array, BOTH, [(at, at ^ distance) for at in range(device_cou...]
    pallas_call x14, Pallas kernels: 19.7 us -> 18.1 us  [call(): pl.pallas_call(kernel, out_shape=out_shape, compiler_params=PARAMS, **more)]
  transfers between devices with their start and end apart: 25 -> 28, of which waited for: 13 -> 14; matrix products, arithmetic and copies ran while one was open for 0% -> 0% of each run, Pallas kernels for 20% -> 23%
where the time goes in v3:
time: 67.5 us; the launch traced here: 67.4 us
  starting transfers between devices  30.9 us (46%)
  waiting for transfers between devices  18.3 us (27%)
  Pallas kernels  18.1 us (27%)
    ppermute x28, starting transfers between devices, swap(): lax.ppermute(array, BOTH, [(at, at ^ distance) for at in range(device_cou...  30.9 us
    ppermute x28, waiting for transfers between devices, swap(): lax.ppermute(array, BOTH, [(at, at ^ distance) for at in range(device_cou...  18.3 us
    pallas_call x14, Pallas kernels, call(): pl.pallas_call(kernel, out_shape=out_shape, compiler_params=PARAMS, **more)  18.1 us
  transfers between devices with their start and end apart: 28, of which 14 were waited for; matrix products, arithmetic and copies ran while one was open for 0% of the time, Pallas kernels for 23%

profile of v3, /device:TPU:0, one launch (start us, length us, event | category | flops | bytes accessed | tf_op | source)
XLA Modules:
  0.0 67.4 jit_solution(17447097126867199970)
XLA Ops:
  0.0 1.0 %shard_map.91.refs_0_ = bf16[16,3712]{1,0:T(8,128)(2,1)S(1)} custom-call(bf16[16,3584]{1,0:T(8,128)(2,1)} %tokens_ref.1, s32[8,16]{1,0:T(8,128)} %bitcast.8, s32[8,16]{1,0:T(8,128)} %bitcast.9), custom_call_target="tpu_custom_call" | custom-call | tf_op jit(solution)/shard_map/pallas_call | solution.py:37
  1.0 3.0 %collective-permute-start.1 = (bf16[16,3712]{1,0:T(8,128)(2,1)S(1)}, bf16[16,3712]{1,0:T(8,128)(2,1)S(1)}, u32[]{:S(2)}, u32[]{:S(2)}) collective-permute-start(bf16[16,3712]{1,0:T(8,128)(2,1)S(1)} %shard_map.91.refs_0_), channel_id=1, source_target_pairs={{0,1},{1,0},{2,3},{3,2},{4,5},{5,4},{6,7},{7,6},{8,9},{9,8},{10,11... | collective-permute-start | bytes 356360 | tf_op jit(solution)/shard_map/ppermute | solution.py:272
  4.0 1.6 %collective-permute-start = (bf16[16,3712]{1,0:T(8,128)(2,1)S(1)}, bf16[16,3712]{1,0:T(8,128)(2,1)S(1)}, u32[]{:S(2)}, u32[]{:S(2)}) collective-permute-start(bf16[16,3712]{1,0:T(8,128)(2,1)S(1)} %shard_map.91.refs_0_), channel_id=1, source_target_pairs={{0,2},{1,3},{2,0},{3,1},{4,6},{5,7},{6,4},{7,5},{8,10},{9,11},{10,... | collective-permute-start | bytes 356360 | tf_op jit(solution)/shard_map/ppermute | solution.py:272
  5.6 2.6 %collective-permute-start.2 = (bf16[16,3712]{1,0:T(8,128)(2,1)S(1)}, bf16[16,3712]{1,0:T(8,128)(2,1)S(1)}, u32[]{:S(2)}, u32[]{:S(2)}) collective-permute-start(bf16[16,3712]{1,0:T(8,128)(2,1)S(1)} %shard_map.91.refs_0_), channel_id=1, source_target_pairs={{0,4},{1,5},{2,6},{3,7},{4,0},{5,1},{6,2},{7,3},{8,12},{9,13},{10,... | collective-permute-start | bytes 356360 | tf_op jit(solution)/shard_map/ppermute | solution.py:272
  8.4 7.3 %shard_map.92 = (bf16[3584,1024]{1,0:T(8,128)(2,1)S(1)}, bf16[3584,1024]{1,0:T(8,128)(2,1)S(1)}, bf16[1024,3584]{1,0:T(8,128)(2,1)S(1)}, f32[8,128]{1,0:T(8,128)S(1)}) custom-call(bf16[3584,1024]{1,0:T(8,128)(2,1)} %bitcast.5, bf16[3584,1024]{1,0:T(8,128)(2,1)} %bitcast.6, bf16[1024,3584]{1,0:T(8,128)(2,1)} %bitcast.7), custom_call_target="tpu_custom_call" | custom-call | tf_op jit(solution)/shard_map/pallas_call | solution.py:37
  15.7 1.6 %collective-permute-done.2.refs_2_ = bf16[16,3712]{1,0:T(8,128)(2,1)S(1)} collective-permute-done((bf16[16,3712]{1,0:T(8,128)(2,1)S(1)}, bf16[16,3712]{1,0:T(8,128)(2,1)S(1)}, u32[]{:S(2)}, u32[]{:S(2)}) %collective-permute-start.2) | collective-permute-done | bytes 118816 | tf_op jit(solution)/shard_map/ppermute | solution.py:272
  17.8 0.8 %collective-permute-done.5.refs_5_ = bf16[16,3712]{1,0:T(8,128)(2,1)S(1)} collective-permute-done((bf16[16,3712]{1,0:T(8,128)(2,1)S(1)}, bf16[16,3712]{1,0:T(8,128)(2,1)S(1)}, u32[]{:S(2)}, u32[]{:S(2)}) %collective-permute-start.5) | collective-permute-done | bytes 118816 | tf_op jit(solution)/shard_map/ppermute | solution.py:272
  19.1 0.7 %shard_map.93 = (bf16[32,3584]{1,0:T(8,128)(2,1)S(1)}, bf16[32,3584]{1,0:T(8,128)(2,1)S(1)}, bf16[32,3584]{1,0:T(8,128)(2,1)S(1)}, bf16[32,3584]{1,0:T(8,128)(2,1)S(1)}) custom-call(bf16[16,3712]{1,0:T(8,128)(2,1)S(1)} %shard_map.91.refs_0_, bf16[16,3712]{1,0:T(8,128)(2,1)S(1)} %collective-permute-done.refs_1_, ...), custom_call_target="tpu_custom_call" | custom-call | tf_op jit(solution)/shard_map/pallas_call | solution.py:37
  19.9 1.6 %collective-permute-start.11 = (bf16[32,3584]{1,0:T(8,128)(2,1)S(1)}, bf16[32,3584]{1,0:T(8,128)(2,1)S(1)}, u32[]{:S(2)}, u32[]{:S(2)}) collective-permute-start(bf16[32,3584]{1,0:T(8,128)(2,1)S(1)} %get-tuple-element.63), channel_id=1, source_target_pairs={{0,16},{1,17},{2,18},{3,19},{4,20},{5,21},{6,22},{7,23},{8,24},{9,... | collective-permute-start | bytes 688136 | tf_op jit(solution)/shard_map/ppermute | solution.py:272
  22.0 1.5 %collective-permute-start.13 = (bf16[32,3584]{1,0:T(8,128)(2,1)S(1)}, bf16[32,3584]{1,0:T(8,128)(2,1)S(1)}, u32[]{:S(2)}, u32[]{:S(2)}) collective-permute-start(bf16[32,3584]{1,0:T(8,128)(2,1)S(1)} %get-tuple-element.65), channel_id=1, source_target_pairs={{0,17},{1,16},{2,19},{3,18},{4,21},{5,20},{6,23},{7,22},{8,25},{9,... | collective-permute-start | bytes 688136 | tf_op jit(solution)/shard_map/ppermute | solution.py:272
  23.4 1.8 %collective-permute-start.8 = (bf16[16,3712]{1,0:T(8,128)(2,1)S(1)}, bf16[16,3712]{1,0:T(8,128)(2,1)S(1)}, u32[]{:S(2)}, u32[]{:S(2)}) collective-permute-start(bf16[16,3712]{1,0:T(8,128)(2,1)S(1)} %collective-permute-done.1.refs_4_), channel_id=1, source_target_pairs={{0,2},{1,3},{2,0},{3,1},{4,6},{5,7},{6,4},{7,5},{8,10},{9,11},{10,... | collective-permute-start | bytes 356360 | tf_op jit(solution)/shard_map/ppermute | solution.py:272
  25.3 1.2 %collective-permute-start.9 = (bf16[16,3712]{1,0:T(8,128)(2,1)S(1)}, bf16[16,3712]{1,0:T(8,128)(2,1)S(1)}, u32[]{:S(2)}, u32[]{:S(2)}) collective-permute-start(bf16[16,3712]{1,0:T(8,128)(2,1)S(1)} %collective-permute-done.1.refs_4_), channel_id=1, source_target_pairs={{0,4},{1,5},{2,6},{3,7},{4,0},{5,1},{6,2},{7,3},{8,12},{9,13},{10,... | collective-permute-start | bytes 356360 | tf_op jit(solution)/shard_map/ppermute | solution.py:272
  26.5 1.9 %collective-permute-done.11.refs_1_ = bf16[32,3584]{1,0:T(8,128)(2,1)S(1)} collective-permute-done((bf16[32,3584]{1,0:T(8,128)(2,1)S(1)}, bf16[32,3584]{1,0:T(8,128)(2,1)S(1)}, u32[]{:S(2)}, u32[]{:S(2)}) %collective-permute-start.11) | collective-permute-done | bytes 229408 | tf_op jit(solution)/shard_map/ppermute | solution.py:272
  28.4 2.5 %collective-permute-start.10 = (bf16[16,3712]{1,0:T(8,128)(2,1)S(1)}, bf16[16,3712]{1,0:T(8,128)(2,1)S(1)}, u32[]{:S(2)}, u32[]{:S(2)}) collective-permute-start(bf16[16,3712]{1,0:T(8,128)(2,1)S(1)} %collective-permute-done.1.refs_4_), channel_id=1, source_target_pairs={{0,6},{1,7},{2,4},{3,5},{4,2},{5,3},{6,0},{7,1},{8,14},{9,15},{10,... | collective-permute-start | bytes 356360 | tf_op jit(solution)/shard_map/ppermute | solution.py:272
  30.9 2.6 %shard_map.94 = (bf16[3584,256]{1,0:T(8,128)(2,1)S(1)}, bf16[3584,256]{1,0:T(8,128)(2,1)S(1)}, bf16[256,3584]{1,0:T(8,128)(2,1)S(1)}, f32[8,128]{1,0:T(8,128)S(1)}) custom-call(bf16[3584,256]{1,0:T(8,128)(2,1)} %refs_0_.1, bf16[3584,256]{1,0:T(8,128)(2,1)} %refs_1_.1, bf16[256,3584]{1,0:T(8,128)(2,1)} %refs_2_.1), custom_call_target="tpu_custom_call" | custom-call | tf_op jit(solution)/shard_map/pallas_call | solution.py:37
  33.8 2.1 %shard_map.97.hidden_ref = bf16[128,1024]{1,0:T(8,128)(2,1)S(1)} custom-call(bf16[32,3584]{1,0:T(8,128)(2,1)S(1)} %get-tuple-element.74.refs_0_, bf16[32,3584]{1,0:T(8,128)(2,1)S(1)} %collective-permute-done.11.refs_1_, bf16[32,3584]{1,0:T(8,128)(2,1)S(1)} %collective-permute-done.12.refs_2_, bf16[32,3584]{1,0:T(8,128)(2,1)S(1)} %collective-permute-done.13.refs_3_, ...), custom_call_target="tpu_custom_call" | custom-call | tf_op jit(solution)/shard_map/pallas_call | solution.py:37
  36.6 1.3 %collective-permute-start.15 = (bf16[32,1792]{1,0:T(8,128)(2,1)S(1)}, bf16[32,1792]{1,0:T(8,128)(2,1)S(1)}, u32[]{:S(2)}, u32[]{:S(2)}) collective-permute-start(bf16[32,1792]{1,0:T(8,128)(2,1)S(1)} %get-tuple-element.83), channel_id=1, source_target_pairs={{0,16},{1,17},{2,18},{3,19},{4,20},{5,21},{6,22},{7,23},{8,24},{9,... | collective-permute-start | bytes 344072 | tf_op jit(solution)/shard_map/ppermute | solution.py:272
  39.6 1.3 %collective-permute-start.22 = (bf16[32,1792]{1,0:T(8,128)(2,1)S(1)}, bf16[32,1792]{1,0:T(8,128)(2,1)S(1)}, u32[]{:S(2)}, u32[]{:S(2)}) collective-permute-start(bf16[32,1792]{1,0:T(8,128)(2,1)S(1)} %get-tuple-element.93), channel_id=1, source_target_pairs={{0,16},{1,17},{2,18},{3,19},{4,20},{5,21},{6,22},{7,23},{8,24},{9,... | collective-permute-start | bytes 344072 | tf_op jit(solution)/shard_map/ppermute | solution.py:272
  41.6 0.7 %shard_map.95.hidden_ref = bf16[128,256]{1,0:T(8,128)(2,1)S(1)} custom-call(bf16[16,3712]{1,0:T(8,128)(2,1)S(1)} %shard_map.91.refs_0_, bf16[16,3712]{1,0:T(8,128)(2,1)S(1)} %collective-permute-done.refs_1_, bf16[16,3712]{1,0:T(8,128)(2,1)S(1)} %collective-permute-done.2.refs_2_, bf16[16,3712]{1,0:T(8,128)(2,1)S(1)} %collective-permute-done.3.refs_3_, ...), custom_call_target="tpu_custom_call" | custom-call | tf_op jit(solution)/shard_map/pallas_call | solution.py:37
  42.6 1.6 %collective-permute-done.16.refs_3_ = bf16[32,1792]{1,0:T(8,128)(2,1)S(1)} collective-permute-done((bf16[32,1792]{1,0:T(8,128)(2,1)S(1)}, bf16[32,1792]{1,0:T(8,128)(2,1)S(1)}, u32[]{:S(2)}, u32[]{:S(2)}) %collective-permute-start.16) | collective-permute-done | bytes 114720 | tf_op jit(solution)/shard_map/ppermute | solution.py:272
  45.3 2.3 %collective-permute-done.22.refs_2_ = bf16[32,1792]{1,0:T(8,128)(2,1)S(1)} collective-permute-done((bf16[32,1792]{1,0:T(8,128)(2,1)S(1)}, bf16[32,1792]{1,0:T(8,128)(2,1)S(1)}, u32[]{:S(2)}, u32[]{:S(2)}) %collective-permute-start.22) | collective-permute-done | bytes 114720 | tf_op jit(solution)/shard_map/ppermute | solution.py:272
  47.5 1.6 %collective-permute-done.23.refs_3_ = bf16[32,1792]{1,0:T(8,128)(2,1)S(1)} collective-permute-done((bf16[32,1792]{1,0:T(8,128)(2,1)S(1)}, bf16[32,1792]{1,0:T(8,128)(2,1)S(1)}, u32[]{:S(2)}, u32[]{:S(2)}) %collective-permute-start.23) | collective-permute-done | bytes 114720 | tf_op jit(solution)/shard_map/ppermute | solution.py:272
  50.2 2.9 %collective-permute-done.17.refs_0_ = bf16[64,1792]{1,0:T(8,128)(2,1)S(1)} collective-permute-done((bf16[64,1792]{1,0:T(8,128)(2,1)S(1)}, bf16[64,1792]{1,0:T(8,128)(2,1)S(1)}, u32[]{:S(2)}, u32[]{:S(2)}) %collective-permute-start.17) | collective-permute-done | bytes 229408 | tf_op jit(solution)/shard_map/ppermute | solution.py:272
  53.1 2.5 %collective-permute-start.18 = (bf16[16,1792]{1,0:T(8,128)(2,1)S(1)}, bf16[16,1792]{1,0:T(8,128)(2,1)S(1)}, u32[]{:S(2)}, u32[]{:S(2)}) collective-permute-start(bf16[16,1792]{1,0:T(8,128)(2,1)S(1)} %get-tuple-element.88), channel_id=1, source_target_pairs={{0,6},{1,7},{2,4},{3,5},{4,2},{5,3},{6,0},{7,1},{8,14},{9,15},{10,... | collective-permute-start | bytes 172040 | tf_op jit(solution)/shard_map/ppermute | solution.py:272
  55.7 0.8 %collective-permute-start.19 = (bf16[16,1792]{1,0:T(8,128)(2,1)S(1)}, bf16[16,1792]{1,0:T(8,128)(2,1)S(1)}, u32[]{:S(2)}, u32[]{:S(2)}) collective-permute-start(bf16[16,1792]{1,0:T(8,128)(2,1)S(1)} %get-tuple-element.89), channel_id=1, source_target_pairs={{0,4},{1,5},{2,6},{3,7},{4,0},{5,1},{6,2},{7,3},{8,12},{9,13},{10,... | collective-permute-start | bytes 172040 | tf_op jit(solution)/shard_map/ppermute | solution.py:272
  56.5 1.1 %collective-permute-start.20 = (bf16[16,1792]{1,0:T(8,128)(2,1)S(1)}, bf16[16,1792]{1,0:T(8,128)(2,1)S(1)}, u32[]{:S(2)}, u32[]{:S(2)}) collective-permute-start(bf16[16,1792]{1,0:T(8,128)(2,1)S(1)} %get-tuple-element.90), channel_id=1, source_target_pairs={{0,2},{1,3},{2,0},{3,1},{4,6},{5,7},{6,4},{7,5},{8,10},{9,11},{10,... | collective-permute-start | bytes 172040 | tf_op jit(solution)/shard_map/ppermute | solution.py:272
  58.0 2.5 %collective-permute-start.25 = (bf16[16,1792]{1,0:T(8,128)(2,1)S(1)}, bf16[16,1792]{1,0:T(8,128)(2,1)S(1)}, u32[]{:S(2)}, u32[]{:S(2)}) collective-permute-start(bf16[16,1792]{1,0:T(8,128)(2,1)S(1)} %get-tuple-element.98), channel_id=1, source_target_pairs={{0,6},{1,7},{2,4},{3,5},{4,2},{5,3},{6,0},{7,1},{8,14},{9,15},{10,... | collective-permute-start | bytes 172040 | tf_op jit(solution)/shard_map/ppermute | solution.py:272
  60.5 0.8 %collective-permute-start.26 = (bf16[16,1792]{1,0:T(8,128)(2,1)S(1)}, bf16[16,1792]{1,0:T(8,128)(2,1)S(1)}, u32[]{:S(2)}, u32[]{:S(2)}) collective-permute-start(bf16[16,1792]{1,0:T(8,128)(2,1)S(1)} %get-tuple-element.99), channel_id=1, source_target_pairs={{0,4},{1,5},{2,6},{3,7},{4,0},{5,1},{6,2},{7,3},{8,12},{9,13},{10,... | collective-permute-start | bytes 172040 | tf_op jit(solution)/shard_map/ppermute | solution.py:272
  61.3 1.1 %collective-permute-start.27 = (bf16[16,1792]{1,0:T(8,128)(2,1)S(1)}, bf16[16,1792]{1,0:T(8,128)(2,1)S(1)}, u32[]{:S(2)}, u32[]{:S(2)}) collective-permute-start(bf16[16,1792]{1,0:T(8,128)(2,1)S(1)} %get-tuple-element.100), channel_id=1, source_target_pairs={{0,2},{1,3},{2,0},{3,1},{4,6},{5,7},{6,4},{7,5},{8,10},{9,11},{10,... | collective-permute-start | bytes 172040 | tf_op jit(solution)/shard_map/ppermute | solution.py:272
  62.4 1.7 %collective-permute-done.25.refs_5_ = bf16[16,1792]{1,0:T(8,128)(2,1)S(1)} collective-permute-done((bf16[16,1792]{1,0:T(8,128)(2,1)S(1)}, bf16[16,1792]{1,0:T(8,128)(2,1)S(1)}, u32[]{:S(2)}, u32[]{:S(2)}) %collective-permute-start.25) | collective-permute-done | bytes 57376 | tf_op jit(solution)/shard_map/ppermute | solution.py:272
  64.1 2.5 %collective-permute-done.26.refs_6_ = bf16[16,1792]{1,0:T(8,128)(2,1)S(1)} collective-permute-done((bf16[16,1792]{1,0:T(8,128)(2,1)S(1)}, bf16[16,1792]{1,0:T(8,128)(2,1)S(1)}, u32[]{:S(2)}, u32[]{:S(2)}) %collective-permute-start.26) | collective-permute-done | bytes 57376 | tf_op jit(solution)/shard_map/ppermute | solution.py:272
  66.7 0.7 %shard_map.104 = bf16[16,3584]{1,0:T(8,128)(2,1)} custom-call(f32[16,1792]{1,0:T(8,128)S(1)} %get-tuple-element.87.refs_0_, bf16[16,1792]{1,0:T(8,128)(2,1)S(1)} %collective-permute-done.18.refs_1_, bf16[16,1792]{1,0:T(8,128)(2,1)S(1)} %collective-permute-done.19.refs_2_, bf16[16,1792]{1,0:T(8,128)(2,1)S(1)} %collective-permute-done.20.refs_3_, ...), custom_call_target="tpu_custom_call" | custom-call | tf_op jit(solution)/shard_map/pallas_call | solution.py:37
  (38 shorter events, 8.0 us)
Async XLA Ops:
  1.0 14.7 %collective-permute-start.1 = (bf16[16,3712]{1,0:T(8,128)(2,1)S(1)}, bf16[16,3712]{1,0:T(8,128)(2,1)S(1)}, u32[]{:S(2)}, u32[]{:S(2)}) collective-permute-start(bf16[16,3712]{1,0:T(8,128)(2,1)S(1)} %shard_map.91.refs_0_), channel_id=1, source_target_pairs={{0,1},{1,0},{2,3},{3,2},{4,5},{5,4},{6,7},{7,6},{8,9},{9,8},{10,11... | collective-permute-start | bytes 356360 | tf_op jit(solution)/shard_map/ppermute | solution.py:272
  4.0 11.7 %collective-permute-start = (bf16[16,3712]{1,0:T(8,128)(2,1)S(1)}, bf16[16,3712]{1,0:T(8,128)(2,1)S(1)}, u32[]{:S(2)}, u32[]{:S(2)}) collective-permute-start(bf16[16,3712]{1,0:T(8,128)(2,1)S(1)} %shard_map.91.refs_0_), channel_id=1, source_target_pairs={{0,2},{1,3},{2,0},{3,1},{4,6},{5,7},{6,4},{7,5},{8,10},{9,11},{10,... | collective-permute-start | bytes 356360 | tf_op jit(solution)/shard_map/ppermute | solution.py:272
  5.6 11.7 %collective-permute-start.2 = (bf16[16,3712]{1,0:T(8,128)(2,1)S(1)}, bf16[16,3712]{1,0:T(8,128)(2,1)S(1)}, u32[]{:S(2)}, u32[]{:S(2)}) collective-permute-start(bf16[16,3712]{1,0:T(8,128)(2,1)S(1)} %shard_map.91.refs_0_), channel_id=1, source_target_pairs={{0,4},{1,5},{2,6},{3,7},{4,0},{5,1},{6,2},{7,3},{8,12},{9,13},{10,... | collective-permute-start | bytes 356360 | tf_op jit(solution)/shard_map/ppermute | solution.py:272
  8.2 9.1 %collective-permute-start.3 = (bf16[16,3712]{1,0:T(8,128)(2,1)S(1)}, bf16[16,3712]{1,0:T(8,128)(2,1)S(1)}, u32[]{:S(2)}, u32[]{:S(2)}) collective-permute-start(bf16[16,3712]{1,0:T(8,128)(2,1)S(1)} %shard_map.91.refs_0_), channel_id=1, source_target_pairs={{0,6},{1,7},{2,4},{3,5},{4,2},{5,3},{6,0},{7,1},{8,14},{9,15},{10,... | collective-permute-start | bytes 356360 | tf_op jit(solution)/shard_map/ppermute | solution.py:272
  8.4 9.4 %collective-permute-start.4 = (bf16[16,3712]{1,0:T(8,128)(2,1)S(1)}, bf16[16,3712]{1,0:T(8,128)(2,1)S(1)}, u32[]{:S(2)}, u32[]{:S(2)}) collective-permute-start(bf16[16,3712]{1,0:T(8,128)(2,1)S(1)} %shard_map.91.refs_0_), channel_id=1, source_target_pairs={{0,8},{1,9},{2,10},{3,11},{4,12},{5,13},{6,14},{7,15},{8,0},{9,1},... | collective-permute-start | bytes 356360 | tf_op jit(solution)/shard_map/ppermute | solution.py:272
  17.3 1.3 %collective-permute-start.5 = (bf16[16,3712]{1,0:T(8,128)(2,1)S(1)}, bf16[16,3712]{1,0:T(8,128)(2,1)S(1)}, u32[]{:S(2)}, u32[]{:S(2)}) collective-permute-start(bf16[16,3712]{1,0:T(8,128)(2,1)S(1)} %collective-permute-done.refs_1_), channel_id=1, source_target_pairs={{0,8},{1,9},{2,10},{3,11},{4,12},{5,13},{6,14},{7,15},{8,0},{9,1},... | collective-permute-start | bytes 356360 | tf_op jit(solution)/shard_map/ppermute | solution.py:272
  17.3 1.5 %collective-permute-start.6 = (bf16[16,3712]{1,0:T(8,128)(2,1)S(1)}, bf16[16,3712]{1,0:T(8,128)(2,1)S(1)}, u32[]{:S(2)}, u32[]{:S(2)}) collective-permute-start(bf16[16,3712]{1,0:T(8,128)(2,1)S(1)} %collective-permute-done.2.refs_2_), channel_id=1, source_target_pairs={{0,8},{1,9},{2,10},{3,11},{4,12},{5,13},{6,14},{7,15},{8,0},{9,1},... | collective-permute-start | bytes 356360 | tf_op jit(solution)/shard_map/ppermute | solution.py:272
  17.8 1.3 %collective-permute-start.7 = (bf16[16,3712]{1,0:T(8,128)(2,1)S(1)}, bf16[16,3712]{1,0:T(8,128)(2,1)S(1)}, u32[]{:S(2)}, u32[]{:S(2)}) collective-permute-start(bf16[16,3712]{1,0:T(8,128)(2,1)S(1)} %collective-permute-done.3.refs_3_), channel_id=1, source_target_pairs={{0,8},{1,9},{2,10},{3,11},{4,12},{5,13},{6,14},{7,15},{8,0},{9,1},... | collective-permute-start | bytes 356360 | tf_op jit(solution)/shard_map/ppermute | solution.py:272
  19.9 8.5 %collective-permute-start.11 = (bf16[32,3584]{1,0:T(8,128)(2,1)S(1)}, bf16[32,3584]{1,0:T(8,128)(2,1)S(1)}, u32[]{:S(2)}, u32[]{:S(2)}) collective-permute-start(bf16[32,3584]{1,0:T(8,128)(2,1)S(1)} %get-tuple-element.63), channel_id=1, source_target_pairs={{0,16},{1,17},{2,18},{3,19},{4,20},{5,21},{6,22},{7,23},{8,24},{9,... | collective-permute-start | bytes 688136 | tf_op jit(solution)/shard_map/ppermute | solution.py:272
  21.5 12.3 %collective-permute-start.12 = (bf16[32,3584]{1,0:T(8,128)(2,1)S(1)}, bf16[32,3584]{1,0:T(8,128)(2,1)S(1)}, u32[]{:S(2)}, u32[]{:S(2)}) collective-permute-start(bf16[32,3584]{1,0:T(8,128)(2,1)S(1)} %get-tuple-element.64), channel_id=1, source_target_pairs={{0,1},{1,0},{2,3},{3,2},{4,5},{5,4},{6,7},{7,6},{8,9},{9,8},{10,11... | collective-permute-start | bytes 688136 | tf_op jit(solution)/shard_map/ppermute | solution.py:272
  22.0 11.8 %collective-permute-start.13 = (bf16[32,3584]{1,0:T(8,128)(2,1)S(1)}, bf16[32,3584]{1,0:T(8,128)(2,1)S(1)}, u32[]{:S(2)}, u32[]{:S(2)}) collective-permute-start(bf16[32,3584]{1,0:T(8,128)(2,1)S(1)} %get-tuple-element.65), channel_id=1, source_target_pairs={{0,17},{1,16},{2,19},{3,18},{4,21},{5,20},{6,23},{7,22},{8,25},{9,... | collective-permute-start | bytes 688136 | tf_op jit(solution)/shard_map/ppermute | solution.py:272
  23.4 14.5 %collective-permute-start.8 = (bf16[16,3712]{1,0:T(8,128)(2,1)S(1)}, bf16[16,3712]{1,0:T(8,128)(2,1)S(1)}, u32[]{:S(2)}, u32[]{:S(2)}) collective-permute-start(bf16[16,3712]{1,0:T(8,128)(2,1)S(1)} %collective-permute-done.1.refs_4_), channel_id=1, source_target_pairs={{0,2},{1,3},{2,0},{3,1},{4,6},{5,7},{6,4},{7,5},{8,10},{9,11},{10,... | collective-permute-start | bytes 356360 | tf_op jit(solution)/shard_map/ppermute | solution.py:272
  25.3 13.9 %collective-permute-start.9 = (bf16[16,3712]{1,0:T(8,128)(2,1)S(1)}, bf16[16,3712]{1,0:T(8,128)(2,1)S(1)}, u32[]{:S(2)}, u32[]{:S(2)}) collective-permute-start(bf16[16,3712]{1,0:T(8,128)(2,1)S(1)} %collective-permute-done.1.refs_4_), channel_id=1, source_target_pairs={{0,4},{1,5},{2,6},{3,7},{4,0},{5,1},{6,2},{7,3},{8,12},{9,13},{10,... | collective-permute-start | bytes 356360 | tf_op jit(solution)/shard_map/ppermute | solution.py:272
  28.4 11.2 %collective-permute-start.10 = (bf16[16,3712]{1,0:T(8,128)(2,1)S(1)}, bf16[16,3712]{1,0:T(8,128)(2,1)S(1)}, u32[]{:S(2)}, u32[]{:S(2)}) collective-permute-start(bf16[16,3712]{1,0:T(8,128)(2,1)S(1)} %collective-permute-done.1.refs_4_), channel_id=1, source_target_pairs={{0,6},{1,7},{2,4},{3,5},{4,2},{5,3},{6,0},{7,1},{8,14},{9,15},{10,... | collective-permute-start | bytes 356360 | tf_op jit(solution)/shard_map/ppermute | solution.py:272
  36.5 4.3 %collective-permute-start.14 = (bf16[32,1792]{1,0:T(8,128)(2,1)S(1)}, bf16[32,1792]{1,0:T(8,128)(2,1)S(1)}, u32[]{:S(2)}, u32[]{:S(2)}) collective-permute-start(bf16[32,1792]{1,0:T(8,128)(2,1)S(1)} %get-tuple-element.82), channel_id=1, source_target_pairs={{0,8},{1,9},{2,10},{3,11},{4,12},{5,13},{6,14},{7,15},{8,0},{9,1},... | collective-permute-start | bytes 344072 | tf_op jit(solution)/shard_map/ppermute | solution.py:272
  36.6 6.0 %collective-permute-start.15 = (bf16[32,1792]{1,0:T(8,128)(2,1)S(1)}, bf16[32,1792]{1,0:T(8,128)(2,1)S(1)}, u32[]{:S(2)}, u32[]{:S(2)}) collective-permute-start(bf16[32,1792]{1,0:T(8,128)(2,1)S(1)} %get-tuple-element.83), channel_id=1, source_target_pairs={{0,16},{1,17},{2,18},{3,19},{4,20},{5,21},{6,22},{7,23},{8,24},{9,... | collective-permute-start | bytes 344072 | tf_op jit(solution)/shard_map/ppermute | solution.py:272
  37.9 6.2 %collective-permute-start.16 = (bf16[32,1792]{1,0:T(8,128)(2,1)S(1)}, bf16[32,1792]{1,0:T(8,128)(2,1)S(1)}, u32[]{:S(2)}, u32[]{:S(2)}) collective-permute-start(bf16[32,1792]{1,0:T(8,128)(2,1)S(1)} %get-tuple-element.84), channel_id=1, source_target_pairs={{0,24},{1,25},{2,26},{3,27},{4,28},{5,29},{6,30},{7,31},{8,16},{9,... | collective-permute-start | bytes 344072 | tf_op jit(solution)/shard_map/ppermute | solution.py:272
  39.1 6.1 %collective-permute-start.21 = (bf16[32,1792]{1,0:T(8,128)(2,1)S(1)}, bf16[32,1792]{1,0:T(8,128)(2,1)S(1)}, u32[]{:S(2)}, u32[]{:S(2)}) collective-permute-start(bf16[32,1792]{1,0:T(8,128)(2,1)S(1)} %get-tuple-element.92), channel_id=1, source_target_pairs={{0,8},{1,9},{2,10},{3,11},{4,12},{5,13},{6,14},{7,15},{8,0},{9,1},... | collective-permute-start | bytes 344072 | tf_op jit(solution)/shard_map/ppermute | solution.py:272
  39.6 8.0 %collective-permute-start.22 = (bf16[32,1792]{1,0:T(8,128)(2,1)S(1)}, bf16[32,1792]{1,0:T(8,128)(2,1)S(1)}, u32[]{:S(2)}, u32[]{:S(2)}) collective-permute-start(bf16[32,1792]{1,0:T(8,128)(2,1)S(1)} %get-tuple-element.93), channel_id=1, source_target_pairs={{0,16},{1,17},{2,18},{3,19},{4,20},{5,21},{6,22},{7,23},{8,24},{9,... | collective-permute-start | bytes 344072 | tf_op jit(solution)/shard_map/ppermute | solution.py:272
  40.8 8.3 %collective-permute-start.23 = (bf16[32,1792]{1,0:T(8,128)(2,1)S(1)}, bf16[32,1792]{1,0:T(8,128)(2,1)S(1)}, u32[]{:S(2)}, u32[]{:S(2)}) collective-permute-start(bf16[32,1792]{1,0:T(8,128)(2,1)S(1)} %get-tuple-element.94), channel_id=1, source_target_pairs={{0,24},{1,25},{2,26},{3,27},{4,28},{5,29},{6,30},{7,31},{8,16},{9,... | collective-permute-start | bytes 344072 | tf_op jit(solution)/shard_map/ppermute | solution.py:272
  44.7 8.4 %collective-permute-start.17 = (bf16[64,1792]{1,0:T(8,128)(2,1)S(1)}, bf16[64,1792]{1,0:T(8,128)(2,1)S(1)}, u32[]{:S(2)}, u32[]{:S(2)}) collective-permute-start(bf16[64,1792]{1,0:T(8,128)(2,1)S(1)} %get-tuple-element.86), channel_id=1, source_target_pairs={{0,1},{1,0},{2,3},{3,2},{4,5},{5,4},{6,7},{7,6},{8,9},{9,8},{10,11... | collective-permute-start | bytes 688136 | tf_op jit(solution)/shard_map/ppermute | solution.py:272
  49.6 8.3 %collective-permute-start.24 = (bf16[64,1792]{1,0:T(8,128)(2,1)S(1)}, bf16[64,1792]{1,0:T(8,128)(2,1)S(1)}, u32[]{:S(2)}, u32[]{:S(2)}) collective-permute-start(bf16[64,1792]{1,0:T(8,128)(2,1)S(1)} %get-tuple-element.96), channel_id=1, source_target_pairs={{0,1},{1,0},{2,3},{3,2},{4,5},{5,4},{6,7},{7,6},{8,9},{9,8},{10,11... | collective-permute-start | bytes 688136 | tf_op jit(solution)/shard_map/ppermute | solution.py:272
  53.1 8.2 %collective-permute-start.18 = (bf16[16,1792]{1,0:T(8,128)(2,1)S(1)}, bf16[16,1792]{1,0:T(8,128)(2,1)S(1)}, u32[]{:S(2)}, u32[]{:S(2)}) collective-permute-start(bf16[16,1792]{1,0:T(8,128)(2,1)S(1)} %get-tuple-element.88), channel_id=1, source_target_pairs={{0,6},{1,7},{2,4},{3,5},{4,2},{5,3},{6,0},{7,1},{8,14},{9,15},{10,... | collective-permute-start | bytes 172040 | tf_op jit(solution)/shard_map/ppermute | solution.py:272
  55.7 6.7 %collective-permute-start.19 = (bf16[16,1792]{1,0:T(8,128)(2,1)S(1)}, bf16[16,1792]{1,0:T(8,128)(2,1)S(1)}, u32[]{:S(2)}, u32[]{:S(2)}) collective-permute-start(bf16[16,1792]{1,0:T(8,128)(2,1)S(1)} %get-tuple-element.89), channel_id=1, source_target_pairs={{0,4},{1,5},{2,6},{3,7},{4,0},{5,1},{6,2},{7,3},{8,12},{9,13},{10,... | collective-permute-start | bytes 172040 | tf_op jit(solution)/shard_map/ppermute | solution.py:272
  56.5 5.9 %collective-permute-start.20 = (bf16[16,1792]{1,0:T(8,128)(2,1)S(1)}, bf16[16,1792]{1,0:T(8,128)(2,1)S(1)}, u32[]{:S(2)}, u32[]{:S(2)}) collective-permute-start(bf16[16,1792]{1,0:T(8,128)(2,1)S(1)} %get-tuple-element.90), channel_id=1, source_target_pairs={{0,2},{1,3},{2,0},{3,1},{4,6},{5,7},{6,4},{7,5},{8,10},{9,11},{10,... | collective-permute-start | bytes 172040 | tf_op jit(solution)/shard_map/ppermute | solution.py:272
  58.0 6.2 %collective-permute-start.25 = (bf16[16,1792]{1,0:T(8,128)(2,1)S(1)}, bf16[16,1792]{1,0:T(8,128)(2,1)S(1)}, u32[]{:S(2)}, u32[]{:S(2)}) collective-permute-start(bf16[16,1792]{1,0:T(8,128)(2,1)S(1)} %get-tuple-element.98), channel_id=1, source_target_pairs={{0,6},{1,7},{2,4},{3,5},{4,2},{5,3},{6,0},{7,1},{8,14},{9,15},{10,... | collective-permute-start | bytes 172040 | tf_op jit(solution)/shard_map/ppermute | solution.py:272
  60.5 6.2 %collective-permute-start.26 = (bf16[16,1792]{1,0:T(8,128)(2,1)S(1)}, bf16[16,1792]{1,0:T(8,128)(2,1)S(1)}, u32[]{:S(2)}, u32[]{:S(2)}) collective-permute-start(bf16[16,1792]{1,0:T(8,128)(2,1)S(1)} %get-tuple-element.99), channel_id=1, source_target_pairs={{0,4},{1,5},{2,6},{3,7},{4,0},{5,1},{6,2},{7,3},{8,12},{9,13},{10,... | collective-permute-start | bytes 172040 | tf_op jit(solution)/shard_map/ppermute | solution.py:272
  61.3 5.4 %collective-permute-start.27 = (bf16[16,1792]{1,0:T(8,128)(2,1)S(1)}, bf16[16,1792]{1,0:T(8,128)(2,1)S(1)}, u32[]{:S(2)}, u32[]{:S(2)}) collective-permute-start(bf16[16,1792]{1,0:T(8,128)(2,1)S(1)} %get-tuple-element.100), channel_id=1, source_target_pairs={{0,2},{1,3},{2,0},{3,1},{4,6},{5,7},{6,4},{7,5},{8,10},{9,11},{10,... | collective-permute-start | bytes 172040 | tf_op jit(solution)/shard_map/ppermute | solution.py:272

commit v4 on v3

--- a/solution.py
+++ b/solution.py
@@ -37,11 +37,17 @@
     return pl.pallas_call(kernel, out_shape=out_shape, compiler_params=PARAMS, **more)(*args)
 
 
-def prefetch_kernel(*refs):
-    count = (len(refs) - 2) // 2
+def columns(ref, at, width):
+    return ref if ref.shape[1] == width else ref.at[:, pl.ds(at * width, width)]
+
+
+def prefetch_kernel(cuts, *refs):
     token_ref, sem = refs[-2:]
+    count = len(cuts)
+    outs = refs[-2 - count:-2]
     copies = [
-        pltpu.make_async_copy(refs[at], refs[count + at], sem.at[at]) for at in range(count)
+        pltpu.make_async_copy(columns(refs[at], cut, outs[at].shape[1]), outs[at], sem.at[at])
+        for at, cut in enumerate(cuts)
     ]
     for copy in copies:
         copy.start()
@@ -62,13 +68,19 @@
     return lax.optimization_barrier((array, *others))[0]
 
 
-def prefetch(*arrays):
+def prefetch(*arrays, half=None, order=None):
+    shapes = [array.shape for array in arrays]
+    if half is not None:
+        arrays += (half,)
+        shapes.append((half.shape[0], half.shape[1] // OUT_CUTS))
     arrays = [far(array) for array in arrays]
-    return call(
-        prefetch_kernel,
-        [pltpu.VMEM(array.shape, array.dtype) for array in arrays] + [pltpu.VMEM((8, LANES), F32)],
+    orders = [] if order is None else [order]
+    return call(
+        functools.partial(prefetch_kernel, [0] * len(arrays)),
+        [pltpu.VMEM(shape, BF16) for shape in shapes] + [pltpu.VMEM((8, LANES), F32)],
         *arrays,
-        in_specs=[ANYWHERE] * len(arrays),
+        *orders,
+        in_specs=[ANYWHERE] * (len(arrays) + len(orders)),
         out_specs=[IN_VMEM] * (len(arrays) + 1),
         scratch_shapes=[pltpu.SemaphoreType.DMA((len(arrays),))],
     )
@@ -153,29 +165,44 @@
 
 
 def hidden_kernel(width, blocks, *refs):
-    pieces = refs[:blocks]
-    gate_ref, up_ref, _, out_ref = refs[blocks:]
+    pieces, (gate_ref, up_ref, _), refs = refs[:blocks], refs[blocks:blocks + 3], refs[blocks + 3:]
+    copies = []
+    if len(refs) > 1:
+        source, refs, sem = refs[0], refs[1:-1], refs[-1]
+        copies = [
+            pltpu.make_async_copy(columns(source, at, target.shape[1]), target, sem.at[at - 1])
+            for at, target in enumerate(refs[1:], 1)
+        ]
+    for copy in copies:
+        copy.start()
     rows = jnp.concatenate([piece[:, :width] for piece in pieces], axis=0)
     gate = dot(rows, gate_ref[...])
     up = dot(rows, up_ref[...])
-    out_ref[...] = (gate / (1.0 + jnp.exp(-gate)) * up).astype(BF16)
-
-
-def hidden(pieces, gate, up, loaded):
-    shape = (sum(piece.shape[0] for piece in pieces), gate.shape[1])
+    refs[0][...] = (gate / (1.0 + jnp.exp(-gate)) * up).astype(BF16)
+    for copy in copies:
+        copy.wait()
+
+
+def hidden(pieces, gate, up, loaded, *later):
+    shapes = [(sum(piece.shape[0] for piece in pieces), gate.shape[1])]
+    for array in later:
+        shapes += [(array.shape[0], array.shape[1] // OUT_CUTS)] * (OUT_CUTS - 1)
     return call(
         functools.partial(hidden_kernel, gate.shape[0], len(pieces)),
-        whole(shape, BF16),
+        [pltpu.VMEM(shape, BF16) for shape in shapes],
         *pieces,
         near(gate),
         near(up),
         loaded,
-        in_specs=[IN_VMEM] * (len(pieces) + 2) + [ANYWHERE],
-    )
-
-
-def down_kernel(start, width, chips_x, depth_y, hidden_ref, down_ref, *outs):
-    answer = dot(hidden_ref[...], down_ref[:, start:start + width])
+        *[far(array) for array in later],
+        in_specs=[IN_VMEM] * (len(pieces) + 2) + [ANYWHERE] * (1 + len(later)),
+        out_specs=[IN_VMEM] * len(shapes),
+        scratch_shapes=[pltpu.SemaphoreType.DMA((OUT_CUTS - 1,))] if later else [],
+    )
+
+
+def down_kernel(chips_x, depth_y, hidden_ref, down_ref, *outs):
+    answer = dot(hidden_ref[...], down_ref[...])
     part = outs[0].shape[0] // depth_y
     for at, out in enumerate(outs):
         along_x, core = at // CORES, at % CORES
@@ -183,10 +210,10 @@
         out[...] = jnp.concatenate([answer[first:first + part] for first in firsts], axis=0).astype(BF16)
 
 
-def down(rows, matrix, start, width, outer_count, depth_y):
-    return call(
-        functools.partial(down_kernel, start, width, outer_count // CORES, depth_y),
-        [whole((rows.shape[0] // outer_count, width), BF16)] * outer_count,
+def down(rows, matrix, outer_count, depth_y):
+    return call(
+        functools.partial(down_kernel, outer_count // CORES, depth_y),
+        [whole((rows.shape[0] // outer_count, matrix.shape[1]), BF16)] * outer_count,
         rows,
         near(matrix),
     )
@@ -282,12 +309,14 @@
     for k in reversed(range(1, DEPTH_Z)):
         column[k] = swap(sent, along_z(k))
     beside = [swap(sent, k) for k in range(1, depth_y)]
-    other = [swap(sent, along_outer(1))]
-    *expert_weights, loaded = prefetch(expert_gate[0], expert_up[0], expert_down[0])
+    gate, up, first_down, loaded = prefetch(
+        expert_gate[0], expert_up[0], half=expert_down[0], order=sent
+    )
+    column[DEPTH_Z - 1], loaded = lax.optimization_barrier((column[DEPTH_Z - 1], loaded))
     *beside, loaded = lax.optimization_barrier((*beside, loaded))
-    for k in range(1, DEPTH_Z):
-        column[k], loaded = lax.optimization_barrier((column[k], loaded))
-        other.append(swap(column[k], along_outer(1)))
+    other = [None] * DEPTH_Z
+    for k in reversed(range(DEPTH_Z)):
+        other[k] = swap(column[k], along_outer(1))
     at_hand = column + other
 
     groups = depth_y * chips_x
@@ -313,7 +342,8 @@
         segment += [swap(block, along_z(k)) for k in range(1, DEPTH_Z)]
     *shared_weights, loaded = prefetch(shared_gate, shared_up, shared_down)
     *arrived, loaded = lax.optimization_barrier((*arrived, loaded))
-    expert_hidden = hidden(arrived, *expert_weights[:2], loaded)
+    expert_hidden, *down_weights = hidden(arrived, gate, up, loaded, expert_down[0])
+    down_weights = [first_down] + down_weights
     high, low = call(
         functools.partial(
             table_kernel, model_width, rows, capacity, inner_count, outer_count, len(segment)
@@ -322,13 +352,13 @@
         *segment,
         in_specs=[IN_VMEM] * len(segment),
     )
-    shared_hidden = hidden(segment, *shared_weights[:2], loaded)
+    (shared_hidden,) = hidden(segment, *shared_weights[:2], loaded)
 
     out_width = model_width // OUT_CUTS
     finals = []
     for at in range(OUT_CUTS):
         start = at * out_width
-        blocks = down(expert_hidden, expert_weights[2], start, out_width, outer_count, depth_y)
+        blocks = down(expert_hidden, down_weights[at], outer_count, depth_y)
         answers = [blocks[0]] + [None] * (outer_count - 1)
         for k in reversed(range(1, outer_count)):
             answers[k] = swap(blocks[k], along_outer(k))

time: 67.5 us -> 65.7 us (0.973)
  waiting for transfers between devices: 18.3 us -> 14.3 us
  starting transfers between devices: 30.9 us -> 34 us
  Pallas kernels: 18.1 us -> 17 us
    ppermute x28, waiting for transfers between devices: 18.3 us -> 14.3 us  [swap(): lax.ppermute(array, BOTH, [(at, at ^ distance) for at in range(device_cou...]
    ppermute x28, starting transfers between devices: 30.9 us -> 34 us  [swap(): lax.ppermute(array, BOTH, [(at, at ^ distance) for at in range(device_cou...]
    pallas_call x14, Pallas kernels: 18.1 us -> 17 us  [call(): pl.pallas_call(kernel, out_shape=out_shape, compiler_params=PARAMS, **more)]
  transfers between devices with their start and end apart: 28 -> 28, of which waited for: 14 -> 13; matrix products, arithmetic and copies ran while one was open for 0% -> 0% of each run, Pallas kernels for 23% -> 22%
where the time goes in v4:
time: 65.7 us; the launch traced here: 65.5 us
  starting transfers between devices  34 us (52%)
  Pallas kernels  17 us (26%)
  waiting for transfers between devices  14.3 us (22%)
    ppermute x28, starting transfers between devices, swap(): lax.ppermute(array, BOTH, [(at, at ^ distance) for at in range(device_cou...  34 us
    pallas_call x14, Pallas kernels, call(): pl.pallas_call(kernel, out_shape=out_shape, compiler_params=PARAMS, **more)  17 us
    ppermute x28, waiting for transfers between devices, swap(): lax.ppermute(array, BOTH, [(at, at ^ distance) for at in range(device_cou...  14.3 us
  transfers between devices with their start and end apart: 28, of which 13 were waited for; matrix products, arithmetic and copies ran while one was open for 0% of the time, Pallas kernels for 22%

profile of v4, /device:TPU:0, one launch (start us, length us, event | category | flops | bytes accessed | tf_op | source)
XLA Modules:
  0.0 65.5 jit_solution(2391643277679782693)
XLA Ops:
  0.0 1.0 %shard_map.91.refs_3_.refs_0_ = bf16[16,3712]{1,0:T(8,128)(2,1)S(1)} custom-call(bf16[16,3584]{1,0:T(8,128)(2,1)} %tokens_ref.1, s32[8,16]{1,0:T(8,128)} %bitcast.9, s32[8,16]{1,0:T(8,128)} %bitcast.10), custom_call_target="tpu_custom_call" | custom-call | tf_op jit(solution)/shard_map/pallas_call | solution.py:37
  1.0 5.1 %collective-permute-start.2 = (bf16[16,3712]{1,0:T(8,128)(2,1)S(1)}, bf16[16,3712]{1,0:T(8,128)(2,1)S(1)}, u32[]{:S(2)}, u32[]{:S(2)}) collective-permute-start(bf16[16,3712]{1,0:T(8,128)(2,1)S(1)} %shard_map.91.refs_3_.refs_0_), channel_id=1, source_target_pairs={{0,6},{1,7},{2,4},{3,5},{4,2},{5,3},{6,0},{7,1},{8,14},{9,15},{10,... | collective-permute-start | bytes 356360 | tf_op jit(solution)/shard_map/ppermute | solution.py:299
  6.7 1.7 %collective-permute-start.3 = (bf16[16,3712]{1,0:T(8,128)(2,1)S(1)}, bf16[16,3712]{1,0:T(8,128)(2,1)S(1)}, u32[]{:S(2)}, u32[]{:S(2)}) collective-permute-start(bf16[16,3712]{1,0:T(8,128)(2,1)S(1)} %shard_map.91.refs_3_.refs_0_), channel_id=1, source_target_pairs={{0,1},{1,0},{2,3},{3,2},{4,5},{5,4},{6,7},{7,6},{8,9},{9,8},{10,11... | collective-permute-start | bytes 356360 | tf_op jit(solution)/shard_map/ppermute | solution.py:299
  8.4 6.2 %shard_map.92 = (bf16[3584,1024]{1,0:T(8,128)(2,1)S(1)}, bf16[3584,1024]{1,0:T(8,128)(2,1)S(1)}, bf16[1024,1792]{1,0:T(8,128)(2,1)S(1)}, f32[8,128]{1,0:T(8,128)S(1)}) custom-call(bf16[3584,1024]{1,0:T(8,128)(2,1)} %bitcast.7, bf16[3584,1024]{1,0:T(8,128)(2,1)} %bitcast.8, bf16[1024,3584]{1,0:T(8,128)(2,1)} %bitcast.5, ...), custom_call_target="tpu_custom_call" | custom-call | tf_op jit(solution)/shard_map/pallas_call | solution.py:37
  15.2 0.9 %collective-permute-done.1.refs_2_ = bf16[16,3712]{1,0:T(8,128)(2,1)S(1)} collective-permute-done((bf16[16,3712]{1,0:T(8,128)(2,1)S(1)}, bf16[16,3712]{1,0:T(8,128)(2,1)S(1)}, u32[]{:S(2)}, u32[]{:S(2)}) %collective-permute-start.1) | collective-permute-done | bytes 118816 | tf_op jit(solution)/shard_map/ppermute | solution.py:299
  16.6 0.8 %collective-permute-done.6.refs_6_ = bf16[16,3712]{1,0:T(8,128)(2,1)S(1)} collective-permute-done((bf16[16,3712]{1,0:T(8,128)(2,1)S(1)}, bf16[16,3712]{1,0:T(8,128)(2,1)S(1)}, u32[]{:S(2)}, u32[]{:S(2)}) %collective-permute-start.6) | collective-permute-done | bytes 118816 | tf_op jit(solution)/shard_map/ppermute | solution.py:299
  17.6 0.7 %shard_map.93 = (bf16[32,3584]{1,0:T(8,128)(2,1)S(1)}, bf16[32,3584]{1,0:T(8,128)(2,1)S(1)}, bf16[32,3584]{1,0:T(8,128)(2,1)S(1)}, bf16[32,3584]{1,0:T(8,128)(2,1)S(1)}) custom-call(bf16[16,3712]{1,0:T(8,128)(2,1)S(1)} %shard_map.91.refs_3_.refs_0_, bf16[16,3712]{1,0:T(8,128)(2,1)S(1)} %collective-permute-done.refs_1_, ...), custom_call_target="tpu_custom_call" | custom-call | tf_op jit(solution)/shard_map/pallas_call | solution.py:37
  18.3 1.6 %collective-permute-start.11 = (bf16[32,3584]{1,0:T(8,128)(2,1)S(1)}, bf16[32,3584]{1,0:T(8,128)(2,1)S(1)}, u32[]{:S(2)}, u32[]{:S(2)}) collective-permute-start(bf16[32,3584]{1,0:T(8,128)(2,1)S(1)} %get-tuple-element.57), channel_id=1, source_target_pairs={{0,16},{1,17},{2,18},{3,19},{4,20},{5,21},{6,22},{7,23},{8,24},{9,... | collective-permute-start | bytes 688136 | tf_op jit(solution)/shard_map/ppermute | solution.py:299
  19.9 1.5 %collective-permute-start.12 = (bf16[32,3584]{1,0:T(8,128)(2,1)S(1)}, bf16[32,3584]{1,0:T(8,128)(2,1)S(1)}, u32[]{:S(2)}, u32[]{:S(2)}) collective-permute-start(bf16[32,3584]{1,0:T(8,128)(2,1)S(1)} %get-tuple-element.58), channel_id=1, source_target_pairs={{0,1},{1,0},{2,3},{3,2},{4,5},{5,4},{6,7},{7,6},{8,9},{9,8},{10,11... | collective-permute-start | bytes 688136 | tf_op jit(solution)/shard_map/ppermute | solution.py:299
  22.3 2.9 %collective-permute-start.9 = (bf16[16,3712]{1,0:T(8,128)(2,1)S(1)}, bf16[16,3712]{1,0:T(8,128)(2,1)S(1)}, u32[]{:S(2)}, u32[]{:S(2)}) collective-permute-start(bf16[16,3712]{1,0:T(8,128)(2,1)S(1)} %collective-permute-done.3.refs_4_), channel_id=1, source_target_pairs={{0,4},{1,5},{2,6},{3,7},{4,0},{5,1},{6,2},{7,3},{8,12},{9,13},{10,... | collective-permute-start | bytes 356360 | tf_op jit(solution)/shard_map/ppermute | solution.py:299
  25.2 1.6 %collective-permute-done.11.refs_1_ = bf16[32,3584]{1,0:T(8,128)(2,1)S(1)} collective-permute-done((bf16[32,3584]{1,0:T(8,128)(2,1)S(1)}, bf16[32,3584]{1,0:T(8,128)(2,1)S(1)}, u32[]{:S(2)}, u32[]{:S(2)}) %collective-permute-start.11) | collective-permute-done | bytes 229408 | tf_op jit(solution)/shard_map/ppermute | solution.py:299
  26.8 2.7 %collective-permute-start.10 = (bf16[16,3712]{1,0:T(8,128)(2,1)S(1)}, bf16[16,3712]{1,0:T(8,128)(2,1)S(1)}, u32[]{:S(2)}, u32[]{:S(2)}) collective-permute-start(bf16[16,3712]{1,0:T(8,128)(2,1)S(1)} %collective-permute-done.3.refs_4_), channel_id=1, source_target_pairs={{0,6},{1,7},{2,4},{3,5},{4,2},{5,3},{6,0},{7,1},{8,14},{9,15},{10,... | collective-permute-start | bytes 356360 | tf_op jit(solution)/shard_map/ppermute | solution.py:299
  29.6 2.6 %shard_map.94 = (bf16[3584,256]{1,0:T(8,128)(2,1)S(1)}, bf16[3584,256]{1,0:T(8,128)(2,1)S(1)}, bf16[256,3584]{1,0:T(8,128)(2,1)S(1)}, f32[8,128]{1,0:T(8,128)S(1)}) custom-call(bf16[3584,256]{1,0:T(8,128)(2,1)} %refs_0_.1, bf16[3584,256]{1,0:T(8,128)(2,1)} %refs_1_.1, bf16[256,3584]{1,0:T(8,128)(2,1)} %refs_2_.1), custom_call_target="tpu_custom_call" | custom-call | tf_op jit(solution)/shard_map/pallas_call | solution.py:37
  32.4 2.1 %shard_map.97 = (bf16[128,1024]{1,0:T(8,128)(2,1)S(1)}, bf16[1024,1792]{1,0:T(8,128)(2,1)S(1)}) custom-call(bf16[32,3584]{1,0:T(8,128)(2,1)S(1)} %get-tuple-element.68.refs_0_, bf16[32,3584]{1,0:T(8,128)(2,1)S(1)} %collective-permute-done.11.refs_1_, bf16[32,3584]{1,0:T(8,128)(2,1)S(1)} %collective-permute-done.12.refs_2_, ...), custom_call_target="tpu_custom_call" | custom-call | tf_op jit(solution)/shard_map/pallas_call | solution.py:37
  34.5 0.7 shard_map.98
  35.3 1.4 %collective-permute-start.15 = (bf16[32,1792]{1,0:T(8,128)(2,1)S(1)}, bf16[32,1792]{1,0:T(8,128)(2,1)S(1)}, u32[]{:S(2)}, u32[]{:S(2)}) collective-permute-start(bf16[32,1792]{1,0:T(8,128)(2,1)S(1)} %get-tuple-element.78), channel_id=1, source_target_pairs={{0,16},{1,17},{2,18},{3,19},{4,20},{5,21},{6,22},{7,23},{8,24},{9,... | collective-permute-start | bytes 344072 | tf_op jit(solution)/shard_map/ppermute | solution.py:299
  37.1 0.6 shard_map.101
  38.2 1.3 %collective-permute-start.22 = (bf16[32,1792]{1,0:T(8,128)(2,1)S(1)}, bf16[32,1792]{1,0:T(8,128)(2,1)S(1)}, u32[]{:S(2)}, u32[]{:S(2)}) collective-permute-start(bf16[32,1792]{1,0:T(8,128)(2,1)S(1)} %get-tuple-element.89), channel_id=1, source_target_pairs={{0,16},{1,17},{2,18},{3,19},{4,20},{5,21},{6,22},{7,23},{8,24},{9,... | collective-permute-start | bytes 344072 | tf_op jit(solution)/shard_map/ppermute | solution.py:299
  40.3 0.7 %shard_map.95.hidden_ref = bf16[128,256]{1,0:T(8,128)(2,1)S(1)} custom-call(bf16[16,3712]{1,0:T(8,128)(2,1)S(1)} %shard_map.91.refs_3_.refs_0_, bf16[16,3712]{1,0:T(8,128)(2,1)S(1)} %collective-permute-done.refs_1_, bf16[16,3712]{1,0:T(8,128)(2,1)S(1)} %collective-permute-done.1.refs_2_, bf16[16,3712]{1,0:T(8,128)(2,1)S(1)} %collective-permute-done.2.refs_3_, ...), custom_call_target="tpu_custom_call" | custom-call | tf_op jit(solution)/shard_map/pallas_call | solution.py:37
  41.3 1.6 %collective-permute-done.16.refs_3_ = bf16[32,1792]{1,0:T(8,128)(2,1)S(1)} collective-permute-done((bf16[32,1792]{1,0:T(8,128)(2,1)S(1)}, bf16[32,1792]{1,0:T(8,128)(2,1)S(1)}, u32[]{:S(2)}, u32[]{:S(2)}) %collective-permute-start.16) | collective-permute-done | bytes 114720 | tf_op jit(solution)/shard_map/ppermute | solution.py:299
  43.3 1.6 %collective-permute-start.17 = (bf16[64,1792]{1,0:T(8,128)(2,1)S(1)}, bf16[64,1792]{1,0:T(8,128)(2,1)S(1)}, u32[]{:S(2)}, u32[]{:S(2)}) collective-permute-start(bf16[64,1792]{1,0:T(8,128)(2,1)S(1)} %get-tuple-element.81), channel_id=1, source_target_pairs={{0,1},{1,0},{2,3},{3,2},{4,5},{5,4},{6,7},{7,6},{8,9},{9,8},{10,11... | collective-permute-start | bytes 688136 | tf_op jit(solution)/shard_map/ppermute | solution.py:299
  44.9 1.3 %collective-permute-done.22.refs_2_ = bf16[32,1792]{1,0:T(8,128)(2,1)S(1)} collective-permute-done((bf16[32,1792]{1,0:T(8,128)(2,1)S(1)}, bf16[32,1792]{1,0:T(8,128)(2,1)S(1)}, u32[]{:S(2)}, u32[]{:S(2)}) %collective-permute-start.22) | collective-permute-done | bytes 114720 | tf_op jit(solution)/shard_map/ppermute | solution.py:299
  46.2 1.6 %collective-permute-done.23.refs_3_ = bf16[32,1792]{1,0:T(8,128)(2,1)S(1)} collective-permute-done((bf16[32,1792]{1,0:T(8,128)(2,1)S(1)}, bf16[32,1792]{1,0:T(8,128)(2,1)S(1)}, u32[]{:S(2)}, u32[]{:S(2)}) %collective-permute-start.23) | collective-permute-done | bytes 114720 | tf_op jit(solution)/shard_map/ppermute | solution.py:299
  48.2 1.6 %collective-permute-start.24 = (bf16[64,1792]{1,0:T(8,128)(2,1)S(1)}, bf16[64,1792]{1,0:T(8,128)(2,1)S(1)}, u32[]{:S(2)}, u32[]{:S(2)}) collective-permute-start(bf16[64,1792]{1,0:T(8,128)(2,1)S(1)} %get-tuple-element.92), channel_id=1, source_target_pairs={{0,1},{1,0},{2,3},{3,2},{4,5},{5,4},{6,7},{7,6},{8,9},{9,8},{10,11... | collective-permute-start | bytes 688136 | tf_op jit(solution)/shard_map/ppermute | solution.py:299
  49.8 1.9 %collective-permute-done.17.refs_0_ = bf16[64,1792]{1,0:T(8,128)(2,1)S(1)} collective-permute-done((bf16[64,1792]{1,0:T(8,128)(2,1)S(1)}, bf16[64,1792]{1,0:T(8,128)(2,1)S(1)}, u32[]{:S(2)}, u32[]{:S(2)}) %collective-permute-start.17) | collective-permute-done | bytes 229408 | tf_op jit(solution)/shard_map/ppermute | solution.py:299
  51.8 2.8 %collective-permute-start.18 = (bf16[16,1792]{1,0:T(8,128)(2,1)S(1)}, bf16[16,1792]{1,0:T(8,128)(2,1)S(1)}, u32[]{:S(2)}, u32[]{:S(2)}) collective-permute-start(bf16[16,1792]{1,0:T(8,128)(2,1)S(1)} %get-tuple-element.83), channel_id=1, source_target_pairs={{0,6},{1,7},{2,4},{3,5},{4,2},{5,3},{6,0},{7,1},{8,14},{9,15},{10,... | collective-permute-start | bytes 172040 | tf_op jit(solution)/shard_map/ppermute | solution.py:299
  54.6 1.6 %collective-permute-start.20 = (bf16[16,1792]{1,0:T(8,128)(2,1)S(1)}, bf16[16,1792]{1,0:T(8,128)(2,1)S(1)}, u32[]{:S(2)}, u32[]{:S(2)}) collective-permute-start(bf16[16,1792]{1,0:T(8,128)(2,1)S(1)} %get-tuple-element.85), channel_id=1, source_target_pairs={{0,2},{1,3},{2,0},{3,1},{4,6},{5,7},{6,4},{7,5},{8,10},{9,11},{10,... | collective-permute-start | bytes 172040 | tf_op jit(solution)/shard_map/ppermute | solution.py:299
  56.6 2.8 %collective-permute-start.25 = (bf16[16,1792]{1,0:T(8,128)(2,1)S(1)}, bf16[16,1792]{1,0:T(8,128)(2,1)S(1)}, u32[]{:S(2)}, u32[]{:S(2)}) collective-permute-start(bf16[16,1792]{1,0:T(8,128)(2,1)S(1)} %get-tuple-element.94), channel_id=1, source_target_pairs={{0,6},{1,7},{2,4},{3,5},{4,2},{5,3},{6,0},{7,1},{8,14},{9,15},{10,... | collective-permute-start | bytes 172040 | tf_op jit(solution)/shard_map/ppermute | solution.py:299
  59.4 1.6 %collective-permute-start.27 = (bf16[16,1792]{1,0:T(8,128)(2,1)S(1)}, bf16[16,1792]{1,0:T(8,128)(2,1)S(1)}, u32[]{:S(2)}, u32[]{:S(2)}) collective-permute-start(bf16[16,1792]{1,0:T(8,128)(2,1)S(1)} %get-tuple-element.96), channel_id=1, source_target_pairs={{0,2},{1,3},{2,0},{3,1},{4,6},{5,7},{6,4},{7,5},{8,10},{9,11},{10,... | collective-permute-start | bytes 172040 | tf_op jit(solution)/shard_map/ppermute | solution.py:299
  61.1 2.0 %collective-permute-done.25.refs_5_ = bf16[16,1792]{1,0:T(8,128)(2,1)S(1)} collective-permute-done((bf16[16,1792]{1,0:T(8,128)(2,1)S(1)}, bf16[16,1792]{1,0:T(8,128)(2,1)S(1)}, u32[]{:S(2)}, u32[]{:S(2)}) %collective-permute-start.25) | collective-permute-done | bytes 57376 | tf_op jit(solution)/shard_map/ppermute | solution.py:299
  63.0 1.8 %collective-permute-done.26.refs_6_ = bf16[16,1792]{1,0:T(8,128)(2,1)S(1)} collective-permute-done((bf16[16,1792]{1,0:T(8,128)(2,1)S(1)}, bf16[16,1792]{1,0:T(8,128)(2,1)S(1)}, u32[]{:S(2)}, u32[]{:S(2)}) %collective-permute-start.26) | collective-permute-done | bytes 57376 | tf_op jit(solution)/shard_map/ppermute | solution.py:299
  64.8 0.7 %shard_map.104 = bf16[16,3584]{1,0:T(8,128)(2,1)} custom-call(f32[16,1792]{1,0:T(8,128)S(1)} %get-tuple-element.82.refs_0_, bf16[16,1792]{1,0:T(8,128)(2,1)S(1)} %collective-permute-done.18.refs_1_, bf16[16,1792]{1,0:T(8,128)(2,1)S(1)} %collective-permute-done.19.refs_2_, bf16[16,1792]{1,0:T(8,128)(2,1)S(1)} %collective-permute-done.20.refs_3_, ...), custom_call_target="tpu_custom_call" | custom-call | tf_op jit(solution)/shard_map/pallas_call | solution.py:37
  (38 shorter events, 6.4 us)
Async XLA Ops:
  1.0 13.7 %collective-permute-start.2 = (bf16[16,3712]{1,0:T(8,128)(2,1)S(1)}, bf16[16,3712]{1,0:T(8,128)(2,1)S(1)}, u32[]{:S(2)}, u32[]{:S(2)}) collective-permute-start(bf16[16,3712]{1,0:T(8,128)(2,1)S(1)} %shard_map.91.refs_3_.refs_0_), channel_id=1, source_target_pairs={{0,6},{1,7},{2,4},{3,5},{4,2},{5,3},{6,0},{7,1},{8,14},{9,15},{10,... | collective-permute-start | bytes 356360 | tf_op jit(solution)/shard_map/ppermute | solution.py:299
  6.1 8.6 %collective-permute-start = (bf16[16,3712]{1,0:T(8,128)(2,1)S(1)}, bf16[16,3712]{1,0:T(8,128)(2,1)S(1)}, u32[]{:S(2)}, u32[]{:S(2)}) collective-permute-start(bf16[16,3712]{1,0:T(8,128)(2,1)S(1)} %shard_map.91.refs_3_.refs_0_), channel_id=1, source_target_pairs={{0,2},{1,3},{2,0},{3,1},{4,6},{5,7},{6,4},{7,5},{8,10},{9,11},{10,... | collective-permute-start | bytes 356360 | tf_op jit(solution)/shard_map/ppermute | solution.py:299
  6.1 10.0 %collective-permute-start.1 = (bf16[16,3712]{1,0:T(8,128)(2,1)S(1)}, bf16[16,3712]{1,0:T(8,128)(2,1)S(1)}, u32[]{:S(2)}, u32[]{:S(2)}) collective-permute-start(bf16[16,3712]{1,0:T(8,128)(2,1)S(1)} %shard_map.91.refs_3_.refs_0_), channel_id=1, source_target_pairs={{0,4},{1,5},{2,6},{3,7},{4,0},{5,1},{6,2},{7,3},{8,12},{9,13},{10,... | collective-permute-start | bytes 356360 | tf_op jit(solution)/shard_map/ppermute | solution.py:299
  6.7 9.9 %collective-permute-start.3 = (bf16[16,3712]{1,0:T(8,128)(2,1)S(1)}, bf16[16,3712]{1,0:T(8,128)(2,1)S(1)}, u32[]{:S(2)}, u32[]{:S(2)}) collective-permute-start(bf16[16,3712]{1,0:T(8,128)(2,1)S(1)} %shard_map.91.refs_3_.refs_0_), channel_id=1, source_target_pairs={{0,1},{1,0},{2,3},{3,2},{4,5},{5,4},{6,7},{7,6},{8,9},{9,8},{10,11... | collective-permute-start | bytes 356360 | tf_op jit(solution)/shard_map/ppermute | solution.py:299
  8.4 8.2 %collective-permute-start.4 = (bf16[16,3712]{1,0:T(8,128)(2,1)S(1)}, bf16[16,3712]{1,0:T(8,128)(2,1)S(1)}, u32[]{:S(2)}, u32[]{:S(2)}) collective-permute-start(bf16[16,3712]{1,0:T(8,128)(2,1)S(1)} %shard_map.91.refs_3_.refs_0_), channel_id=1, source_target_pairs={{0,8},{1,9},{2,10},{3,11},{4,12},{5,13},{6,14},{7,15},{8,0},{9,1},... | collective-permute-start | bytes 356360 | tf_op jit(solution)/shard_map/ppermute | solution.py:299
  14.7 2.0 %collective-permute-start.5 = (bf16[16,3712]{1,0:T(8,128)(2,1)S(1)}, bf16[16,3712]{1,0:T(8,128)(2,1)S(1)}, u32[]{:S(2)}, u32[]{:S(2)}) collective-permute-start(bf16[16,3712]{1,0:T(8,128)(2,1)S(1)} %collective-permute-done.refs_1_), channel_id=1, source_target_pairs={{0,8},{1,9},{2,10},{3,11},{4,12},{5,13},{6,14},{7,15},{8,0},{9,1},... | collective-permute-start | bytes 356360 | tf_op jit(solution)/shard_map/ppermute | solution.py:299
  16.1 1.3 %collective-permute-start.6 = (bf16[16,3712]{1,0:T(8,128)(2,1)S(1)}, bf16[16,3712]{1,0:T(8,128)(2,1)S(1)}, u32[]{:S(2)}, u32[]{:S(2)}) collective-permute-start(bf16[16,3712]{1,0:T(8,128)(2,1)S(1)} %collective-permute-done.1.refs_2_), channel_id=1, source_target_pairs={{0,8},{1,9},{2,10},{3,11},{4,12},{5,13},{6,14},{7,15},{8,0},{9,1},... | collective-permute-start | bytes 356360 | tf_op jit(solution)/shard_map/ppermute | solution.py:299
  16.1 1.5 %collective-permute-start.7 = (bf16[16,3712]{1,0:T(8,128)(2,1)S(1)}, bf16[16,3712]{1,0:T(8,128)(2,1)S(1)}, u32[]{:S(2)}, u32[]{:S(2)}) collective-permute-start(bf16[16,3712]{1,0:T(8,128)(2,1)S(1)} %collective-permute-done.2.refs_3_), channel_id=1, source_target_pairs={{0,8},{1,9},{2,10},{3,11},{4,12},{5,13},{6,14},{7,15},{8,0},{9,1},... | collective-permute-start | bytes 356360 | tf_op jit(solution)/shard_map/ppermute | solution.py:299
  18.3 8.5 %collective-permute-start.11 = (bf16[32,3584]{1,0:T(8,128)(2,1)S(1)}, bf16[32,3584]{1,0:T(8,128)(2,1)S(1)}, u32[]{:S(2)}, u32[]{:S(2)}) collective-permute-start(bf16[32,3584]{1,0:T(8,128)(2,1)S(1)} %get-tuple-element.57), channel_id=1, source_target_pairs={{0,16},{1,17},{2,18},{3,19},{4,20},{5,21},{6,22},{7,23},{8,24},{9,... | collective-permute-start | bytes 688136 | tf_op jit(solution)/shard_map/ppermute | solution.py:299
  19.9 12.5 %collective-permute-start.12 = (bf16[32,3584]{1,0:T(8,128)(2,1)S(1)}, bf16[32,3584]{1,0:T(8,128)(2,1)S(1)}, u32[]{:S(2)}, u32[]{:S(2)}) collective-permute-start(bf16[32,3584]{1,0:T(8,128)(2,1)S(1)} %get-tuple-element.58), channel_id=1, source_target_pairs={{0,1},{1,0},{2,3},{3,2},{4,5},{5,4},{6,7},{7,6},{8,9},{9,8},{10,11... | collective-permute-start | bytes 688136 | tf_op jit(solution)/shard_map/ppermute | solution.py:299
  21.4 11.0 %collective-permute-start.13 = (bf16[32,3584]{1,0:T(8,128)(2,1)S(1)}, bf16[32,3584]{1,0:T(8,128)(2,1)S(1)}, u32[]{:S(2)}, u32[]{:S(2)}) collective-permute-start(bf16[32,3584]{1,0:T(8,128)(2,1)S(1)} %get-tuple-element.59), channel_id=1, source_target_pairs={{0,17},{1,16},{2,19},{3,18},{4,21},{5,20},{6,23},{7,22},{8,25},{9,... | collective-permute-start | bytes 688136 | tf_op jit(solution)/shard_map/ppermute | solution.py:299
  21.9 14.7 %collective-permute-start.8 = (bf16[16,3712]{1,0:T(8,128)(2,1)S(1)}, bf16[16,3712]{1,0:T(8,128)(2,1)S(1)}, u32[]{:S(2)}, u32[]{:S(2)}) collective-permute-start(bf16[16,3712]{1,0:T(8,128)(2,1)S(1)} %collective-permute-done.3.refs_4_), channel_id=1, source_target_pairs={{0,2},{1,3},{2,0},{3,1},{4,6},{5,7},{6,4},{7,5},{8,10},{9,11},{10,... | collective-permute-start | bytes 356360 | tf_op jit(solution)/shard_map/ppermute | solution.py:299
  22.3 15.5 %collective-permute-start.9 = (bf16[16,3712]{1,0:T(8,128)(2,1)S(1)}, bf16[16,3712]{1,0:T(8,128)(2,1)S(1)}, u32[]{:S(2)}, u32[]{:S(2)}) collective-permute-start(bf16[16,3712]{1,0:T(8,128)(2,1)S(1)} %collective-permute-done.3.refs_4_), channel_id=1, source_target_pairs={{0,4},{1,5},{2,6},{3,7},{4,0},{5,1},{6,2},{7,3},{8,12},{9,13},{10,... | collective-permute-start | bytes 356360 | tf_op jit(solution)/shard_map/ppermute | solution.py:299
  26.8 11.4 %collective-permute-start.10 = (bf16[16,3712]{1,0:T(8,128)(2,1)S(1)}, bf16[16,3712]{1,0:T(8,128)(2,1)S(1)}, u32[]{:S(2)}, u32[]{:S(2)}) collective-permute-start(bf16[16,3712]{1,0:T(8,128)(2,1)S(1)} %collective-permute-done.3.refs_4_), channel_id=1, source_target_pairs={{0,6},{1,7},{2,4},{3,5},{4,2},{5,3},{6,0},{7,1},{8,14},{9,15},{10,... | collective-permute-start | bytes 356360 | tf_op jit(solution)/shard_map/ppermute | solution.py:299
  35.2 4.4 %collective-permute-start.14 = (bf16[32,1792]{1,0:T(8,128)(2,1)S(1)}, bf16[32,1792]{1,0:T(8,128)(2,1)S(1)}, u32[]{:S(2)}, u32[]{:S(2)}) collective-permute-start(bf16[32,1792]{1,0:T(8,128)(2,1)S(1)} %get-tuple-element.77), channel_id=1, source_target_pairs={{0,8},{1,9},{2,10},{3,11},{4,12},{5,13},{6,14},{7,15},{8,0},{9,1},... | collective-permute-start | bytes 344072 | tf_op jit(solution)/shard_map/ppermute | solution.py:299
  35.3 6.0 %collective-permute-start.15 = (bf16[32,1792]{1,0:T(8,128)(2,1)S(1)}, bf16[32,1792]{1,0:T(8,128)(2,1)S(1)}, u32[]{:S(2)}, u32[]{:S(2)}) collective-permute-start(bf16[32,1792]{1,0:T(8,128)(2,1)S(1)} %get-tuple-element.78), channel_id=1, source_target_pairs={{0,16},{1,17},{2,18},{3,19},{4,20},{5,21},{6,22},{7,23},{8,24},{9,... | collective-permute-start | bytes 344072 | tf_op jit(solution)/shard_map/ppermute | solution.py:299
  36.7 6.2 %collective-permute-start.16 = (bf16[32,1792]{1,0:T(8,128)(2,1)S(1)}, bf16[32,1792]{1,0:T(8,128)(2,1)S(1)}, u32[]{:S(2)}, u32[]{:S(2)}) collective-permute-start(bf16[32,1792]{1,0:T(8,128)(2,1)S(1)} %get-tuple-element.79), channel_id=1, source_target_pairs={{0,24},{1,25},{2,26},{3,27},{4,28},{5,29},{6,30},{7,31},{8,16},{9,... | collective-permute-start | bytes 344072 | tf_op jit(solution)/shard_map/ppermute | solution.py:299
  37.8 7.1 %collective-permute-start.21 = (bf16[32,1792]{1,0:T(8,128)(2,1)S(1)}, bf16[32,1792]{1,0:T(8,128)(2,1)S(1)}, u32[]{:S(2)}, u32[]{:S(2)}) collective-permute-start(bf16[32,1792]{1,0:T(8,128)(2,1)S(1)} %get-tuple-element.88), channel_id=1, source_target_pairs={{0,8},{1,9},{2,10},{3,11},{4,12},{5,13},{6,14},{7,15},{8,0},{9,1},... | collective-permute-start | bytes 344072 | tf_op jit(solution)/shard_map/ppermute | solution.py:299
  38.2 8.0 %collective-permute-start.22 = (bf16[32,1792]{1,0:T(8,128)(2,1)S(1)}, bf16[32,1792]{1,0:T(8,128)(2,1)S(1)}, u32[]{:S(2)}, u32[]{:S(2)}) collective-permute-start(bf16[32,1792]{1,0:T(8,128)(2,1)S(1)} %get-tuple-element.89), channel_id=1, source_target_pairs={{0,16},{1,17},{2,18},{3,19},{4,20},{5,21},{6,22},{7,23},{8,24},{9,... | collective-permute-start | bytes 344072 | tf_op jit(solution)/shard_map/ppermute | solution.py:299
  39.5 8.2 %collective-permute-start.23 = (bf16[32,1792]{1,0:T(8,128)(2,1)S(1)}, bf16[32,1792]{1,0:T(8,128)(2,1)S(1)}, u32[]{:S(2)}, u32[]{:S(2)}) collective-permute-start(bf16[32,1792]{1,0:T(8,128)(2,1)S(1)} %get-tuple-element.90), channel_id=1, source_target_pairs={{0,24},{1,25},{2,26},{3,27},{4,28},{5,29},{6,30},{7,31},{8,16},{9,... | collective-permute-start | bytes 344072 | tf_op jit(solution)/shard_map/ppermute | solution.py:299
  43.3 8.4 %collective-permute-start.17 = (bf16[64,1792]{1,0:T(8,128)(2,1)S(1)}, bf16[64,1792]{1,0:T(8,128)(2,1)S(1)}, u32[]{:S(2)}, u32[]{:S(2)}) collective-permute-start(bf16[64,1792]{1,0:T(8,128)(2,1)S(1)} %get-tuple-element.81), channel_id=1, source_target_pairs={{0,1},{1,0},{2,3},{3,2},{4,5},{5,4},{6,7},{7,6},{8,9},{9,8},{10,11... | collective-permute-start | bytes 688136 | tf_op jit(solution)/shard_map/ppermute | solution.py:299
  48.2 8.3 %collective-permute-start.24 = (bf16[64,1792]{1,0:T(8,128)(2,1)S(1)}, bf16[64,1792]{1,0:T(8,128)(2,1)S(1)}, u32[]{:S(2)}, u32[]{:S(2)}) collective-permute-start(bf16[64,1792]{1,0:T(8,128)(2,1)S(1)} %get-tuple-element.92), channel_id=1, source_target_pairs={{0,1},{1,0},{2,3},{3,2},{4,5},{5,4},{6,7},{7,6},{8,9},{9,8},{10,11... | collective-permute-start | bytes 688136 | tf_op jit(solution)/shard_map/ppermute | solution.py:299
  51.8 7.6 %collective-permute-start.18 = (bf16[16,1792]{1,0:T(8,128)(2,1)S(1)}, bf16[16,1792]{1,0:T(8,128)(2,1)S(1)}, u32[]{:S(2)}, u32[]{:S(2)}) collective-permute-start(bf16[16,1792]{1,0:T(8,128)(2,1)S(1)} %get-tuple-element.83), channel_id=1, source_target_pairs={{0,6},{1,7},{2,4},{3,5},{4,2},{5,3},{6,0},{7,1},{8,14},{9,15},{10,... | collective-permute-start | bytes 172040 | tf_op jit(solution)/shard_map/ppermute | solution.py:299
  54.6 6.5 %collective-permute-start.19 = (bf16[16,1792]{1,0:T(8,128)(2,1)S(1)}, bf16[16,1792]{1,0:T(8,128)(2,1)S(1)}, u32[]{:S(2)}, u32[]{:S(2)}) collective-permute-start(bf16[16,1792]{1,0:T(8,128)(2,1)S(1)} %get-tuple-element.84), channel_id=1, source_target_pairs={{0,4},{1,5},{2,6},{3,7},{4,0},{5,1},{6,2},{7,3},{8,12},{9,13},{10,... | collective-permute-start | bytes 172040 | tf_op jit(solution)/shard_map/ppermute | solution.py:299
  54.6 6.5 %collective-permute-start.20 = (bf16[16,1792]{1,0:T(8,128)(2,1)S(1)}, bf16[16,1792]{1,0:T(8,128)(2,1)S(1)}, u32[]{:S(2)}, u32[]{:S(2)}) collective-permute-start(bf16[16,1792]{1,0:T(8,128)(2,1)S(1)} %get-tuple-element.85), channel_id=1, source_target_pairs={{0,2},{1,3},{2,0},{3,1},{4,6},{5,7},{6,4},{7,5},{8,10},{9,11},{10,... | collective-permute-start | bytes 172040 | tf_op jit(solution)/shard_map/ppermute | solution.py:299
  56.6 6.4 %collective-permute-start.25 = (bf16[16,1792]{1,0:T(8,128)(2,1)S(1)}, bf16[16,1792]{1,0:T(8,128)(2,1)S(1)}, u32[]{:S(2)}, u32[]{:S(2)}) collective-permute-start(bf16[16,1792]{1,0:T(8,128)(2,1)S(1)} %get-tuple-element.94), channel_id=1, source_target_pairs={{0,6},{1,7},{2,4},{3,5},{4,2},{5,3},{6,0},{7,1},{8,14},{9,15},{10,... | collective-permute-start | bytes 172040 | tf_op jit(solution)/shard_map/ppermute | solution.py:299
  59.4 5.4 %collective-permute-start.26 = (bf16[16,1792]{1,0:T(8,128)(2,1)S(1)}, bf16[16,1792]{1,0:T(8,128)(2,1)S(1)}, u32[]{:S(2)}, u32[]{:S(2)}) collective-permute-start(bf16[16,1792]{1,0:T(8,128)(2,1)S(1)} %get-tuple-element.95), channel_id=1, source_target_pairs={{0,4},{1,5},{2,6},{3,7},{4,0},{5,1},{6,2},{7,3},{8,12},{9,13},{10,... | collective-permute-start | bytes 172040 | tf_op jit(solution)/shard_map/ppermute | solution.py:299
  59.4 5.4 %collective-permute-start.27 = (bf16[16,1792]{1,0:T(8,128)(2,1)S(1)}, bf16[16,1792]{1,0:T(8,128)(2,1)S(1)}, u32[]{:S(2)}, u32[]{:S(2)}) collective-permute-start(bf16[16,1792]{1,0:T(8,128)(2,1)S(1)} %get-tuple-element.96), channel_id=1, source_target_pairs={{0,2},{1,3},{2,0},{3,1},{4,6},{5,7},{6,4},{7,5},{8,10},{9,11},{10,... | collective-permute-start | bytes 172040 | tf_op jit(solution)/shard_map/ppermute | solution.py:299

commit v5 on v4

--- a/solution.py
+++ b/solution.py
@@ -12,6 +12,9 @@
 LANES = 128
 CORES = 2
 DEPTH_Z = 4
+FIRST_Z = 2
+WAY_BACK = (3, 2, 1)
+WAY_SHARED = (2, 1, 3)
 OUT_CUTS = 2
 BOTH = ("outer", "inner")
 BF16 = jnp.bfloat16
@@ -232,27 +235,34 @@
     low_ref[...] = (weight - high.astype(F32)).astype(BF16)
 
 
-def combine_kernel(blocks, start, width, hidden_ref, down_ref, high_ref, low_ref, *refs):
+def shared_kernel(hidden_ref, down_ref, *outs):
+    width = outs[0].shape[1]
+    for at, out in enumerate(outs):
+        out[...] = dot(hidden_ref[...], down_ref[:, at * width:(at + 1) * width])
+
+
+def combine_kernel(blocks, base_ref, high_ref, low_ref, *refs):
     answers, keep_ref, outs = refs[:blocks], refs[blocks], refs[blocks + 1:]
+    answers = [answers[0], answers[-1], *answers[1:-1]]
     rows = jnp.concatenate([answer[...] for answer in answers], axis=0)
-    total = dot(hidden_ref[...], down_ref[:, start:start + width])
-    total = total + dot(high_ref[...], rows) + dot(low_ref[...], rows)
+    total = base_ref[...] + dot(high_ref[...], rows) + dot(low_ref[...], rows)
     each = keep_ref.shape[0]
     keep_ref[...] = total[:each]
     for at, out in enumerate(outs):
         out[...] = total[(at + 1) * each:(at + 2) * each].astype(BF16)
 
 
-def combine(shared_hidden, shared_down, high, low, answers, start, width, sends):
-    each = shared_hidden.shape[0] // (sends + 1)
-    return call(
-        functools.partial(combine_kernel, len(answers), start, width),
+def combine(base, high, low, answers, sends):
+    each, width = base.shape[0] // (sends + 1), base.shape[1]
+    return call(
+        functools.partial(combine_kernel, len(answers)),
         [whole((each, width), F32)] + [whole((each, width), BF16)] * sends,
-        shared_hidden,
-        near(shared_down),
+        base,
         high,
         low,
-        *answers,
+        answers[0],
+        *answers[2:],
+        answers[1],
     )
 
 
@@ -309,10 +319,8 @@
     for k in reversed(range(1, DEPTH_Z)):
         column[k] = swap(sent, along_z(k))
     beside = [swap(sent, k) for k in range(1, depth_y)]
-    gate, up, first_down, loaded = prefetch(
-        expert_gate[0], expert_up[0], half=expert_down[0], order=sent
-    )
-    column[DEPTH_Z - 1], loaded = lax.optimization_barrier((column[DEPTH_Z - 1], loaded))
+    gate, up, loaded = prefetch(expert_gate[0], expert_up[0], order=sent)
+    column[FIRST_Z], loaded = lax.optimization_barrier((column[FIRST_Z], loaded))
     *beside, loaded = lax.optimization_barrier((*beside, loaded))
     other = [None] * DEPTH_Z
     for k in reversed(range(DEPTH_Z)):
@@ -339,9 +347,17 @@
     for block in beside:
         block = after(block, *blocks)
         segment.append(block)
-        segment += [swap(block, along_z(k)) for k in range(1, DEPTH_Z)]
-    *shared_weights, loaded = prefetch(shared_gate, shared_up, shared_down)
-    *arrived, loaded = lax.optimization_barrier((*arrived, loaded))
+        moved = {k: swap(block, along_z(k)) for k in WAY_SHARED}
+        for k, block in zip(WAY_SHARED, lax.optimization_barrier(tuple(moved.values()))):
+            moved[k] = block
+        segment += [moved[k] for k in range(1, DEPTH_Z)]
+    *shared_weights, first_down, loaded = prefetch(
+        shared_gate, shared_up, shared_down, half=expert_down[0]
+    )
+    way = sorted(range(groups), key=lambda at: (at % chips_x > 0, at // chips_x > 0, at))
+    *coming, loaded = lax.optimization_barrier((*[arrived[at] for at in way], loaded))
+    for at, block in zip(way, coming):
+        arrived[at] = block
     expert_hidden, *down_weights = hidden(arrived, gate, up, loaded, expert_down[0])
     down_weights = [first_down] + down_weights
     high, low = call(
@@ -354,17 +370,21 @@
     )
     (shared_hidden,) = hidden(segment, *shared_weights[:2], loaded)
 
+    bases = call(
+        shared_kernel,
+        [whole((rows * inner_count, model_width // OUT_CUTS), F32)] * OUT_CUTS,
+        shared_hidden,
+        near(shared_weights[2]),
+    )
+
     out_width = model_width // OUT_CUTS
     finals = []
     for at in range(OUT_CUTS):
-        start = at * out_width
         blocks = down(expert_hidden, down_weights[at], outer_count, depth_y)
         answers = [blocks[0]] + [None] * (outer_count - 1)
         for k in reversed(range(1, outer_count)):
             answers[k] = swap(blocks[k], along_outer(k))
-        kept, *leaving = combine(
-            shared_hidden, shared_weights[2], high, low, answers, start, out_width, depth_y - 1
-        )
+        kept, *leaving = combine(bases[at], high, low, answers, depth_y - 1)
         coming = [swap(block, k + 1) for k, block in enumerate(leaving)]
         kept, *leaving = call(
             functools.partial(add_kernel, depth_y - 1),
@@ -372,7 +392,7 @@
             kept,
             *coming,
         )
-        coming = [swap(leaving[k - 1], along_z(k)) for k in reversed(range(1, DEPTH_Z))]
+        coming = [swap(leaving[k - 1], along_z(k)) for k in WAY_BACK]
         finals += [kept] + coming
     return call(
         functools.partial(finish_kernel, DEPTH_Z, out_width), whole((rows, model_width), BF16), *finals

time: 65.7 us -> 64.3 us (0.979)
  waiting for transfers between devices: 14.3 us -> 12.9 us
    ppermute x28, waiting for transfers between devices: 14.3 us -> 12.9 us  [swap(): lax.ppermute(array, BOTH, [(at, at ^ distance) for at in range(device_cou...]
    pallas_call x14 -> x15, Pallas kernels: 17 us -> 17.3 us  [call(): pl.pallas_call(kernel, out_shape=out_shape, compiler_params=PARAMS, **more)]
  transfers between devices with their start and end apart: 28 -> 28, of which waited for: 13 -> 12; matrix products, arithmetic and copies ran while one was open for 0% -> 0% of each run, Pallas kernels for 22% -> 23%
where the time goes in v5:
time: 64.3 us; the launch traced here: 64 us
  starting transfers between devices  33.7 us (52%)
  Pallas kernels  17.3 us (27%)
  waiting for transfers between devices  12.9 us (20%)
    ppermute x28, starting transfers between devices, swap(): lax.ppermute(array, BOTH, [(at, at ^ distance) for at in range(device_cou...  33.7 us
    pallas_call x15, Pallas kernels, call(): pl.pallas_call(kernel, out_shape=out_shape, compiler_params=PARAMS, **more)  17.3 us
    ppermute x28, waiting for transfers between devices, swap(): lax.ppermute(array, BOTH, [(at, at ^ distance) for at in range(device_cou...  12.9 us
  transfers between devices with their start and end apart: 28, of which 12 were waited for; matrix products, arithmetic and copies ran while one was open for 0% of the time, Pallas kernels for 23%

profile of v5, /device:TPU:0, one launch (start us, length us, event | category | flops | bytes accessed | tf_op | source)
XLA Modules:
  0.0 64.0 jit_solution(382747853804857610)
XLA Ops:
  0.0 1.0 %shard_map.91.refs_2_.refs_0_ = bf16[16,3712]{1,0:T(8,128)(2,1)S(1)} custom-call(bf16[16,3584]{1,0:T(8,128)(2,1)} %tokens_ref.1, s32[8,16]{1,0:T(8,128)} %bitcast.9, s32[8,16]{1,0:T(8,128)} %bitcast.10), custom_call_target="tpu_custom_call" | custom-call | tf_op jit(solution)/shard_map/pallas_call | solution.py:40
  1.0 4.1 %collective-permute-start.1 = (bf16[16,3712]{1,0:T(8,128)(2,1)S(1)}, bf16[16,3712]{1,0:T(8,128)(2,1)S(1)}, u32[]{:S(2)}, u32[]{:S(2)}) collective-permute-start(bf16[16,3712]{1,0:T(8,128)(2,1)S(1)} %shard_map.91.refs_2_.refs_0_), channel_id=1, source_target_pairs={{0,4},{1,5},{2,6},{3,7},{4,0},{5,1},{6,2},{7,3},{8,12},{9,13},{10,... | collective-permute-start | bytes 356360 | tf_op jit(solution)/shard_map/ppermute | solution.py:309
  5.1 1.6 %collective-permute-start = (bf16[16,3712]{1,0:T(8,128)(2,1)S(1)}, bf16[16,3712]{1,0:T(8,128)(2,1)S(1)}, u32[]{:S(2)}, u32[]{:S(2)}) collective-permute-start(bf16[16,3712]{1,0:T(8,128)(2,1)S(1)} %shard_map.91.refs_2_.refs_0_), channel_id=1, source_target_pairs={{0,2},{1,3},{2,0},{3,1},{4,6},{5,7},{6,4},{7,5},{8,10},{9,11},{10,... | collective-permute-start | bytes 356360 | tf_op jit(solution)/shard_map/ppermute | solution.py:309
  6.6 1.7 %collective-permute-start.3 = (bf16[16,3712]{1,0:T(8,128)(2,1)S(1)}, bf16[16,3712]{1,0:T(8,128)(2,1)S(1)}, u32[]{:S(2)}, u32[]{:S(2)}) collective-permute-start(bf16[16,3712]{1,0:T(8,128)(2,1)S(1)} %shard_map.91.refs_2_.refs_0_), channel_id=1, source_target_pairs={{0,1},{1,0},{2,3},{3,2},{4,5},{5,4},{6,7},{7,6},{8,9},{9,8},{10,11... | collective-permute-start | bytes 356360 | tf_op jit(solution)/shard_map/ppermute | solution.py:309
  8.4 5.2 %shard_map.92 = (bf16[3584,1024]{1,0:T(8,128)(2,1)S(1)}, bf16[3584,1024]{1,0:T(8,128)(2,1)S(1)}, f32[8,128]{1,0:T(8,128)S(1)}) custom-call(bf16[3584,1024]{1,0:T(8,128)(2,1)} %bitcast.7, bf16[3584,1024]{1,0:T(8,128)(2,1)} %bitcast.8, bf16[16,3712]{1,0:T(8,128)(2,1)S(1)} %shard_map.91.refs_2_.refs_0_), custom_call_target="tpu_custom_call" | custom-call | tf_op jit(solution)/shard_map/pallas_call | solution.py:40
  14.7 0.8 %collective-permute-done.5.refs_5_ = bf16[16,3712]{1,0:T(8,128)(2,1)S(1)} collective-permute-done((bf16[16,3712]{1,0:T(8,128)(2,1)S(1)}, bf16[16,3712]{1,0:T(8,128)(2,1)S(1)}, u32[]{:S(2)}, u32[]{:S(2)}) %collective-permute-start.5) | collective-permute-done | bytes 118816 | tf_op jit(solution)/shard_map/ppermute | solution.py:309
  15.9 0.7 %shard_map.93 = (bf16[32,3584]{1,0:T(8,128)(2,1)S(1)}, bf16[32,3584]{1,0:T(8,128)(2,1)S(1)}, bf16[32,3584]{1,0:T(8,128)(2,1)S(1)}, bf16[32,3584]{1,0:T(8,128)(2,1)S(1)}) custom-call(bf16[16,3712]{1,0:T(8,128)(2,1)S(1)} %shard_map.91.refs_2_.refs_0_, bf16[16,3712]{1,0:T(8,128)(2,1)S(1)} %collective-permute-done.refs_1_, ...), custom_call_target="tpu_custom_call" | custom-call | tf_op jit(solution)/shard_map/pallas_call | solution.py:40
  16.6 2.1 %collective-permute-start.11 = (bf16[32,3584]{1,0:T(8,128)(2,1)S(1)}, bf16[32,3584]{1,0:T(8,128)(2,1)S(1)}, u32[]{:S(2)}, u32[]{:S(2)}) collective-permute-start(bf16[32,3584]{1,0:T(8,128)(2,1)S(1)} %get-tuple-element.63), channel_id=1, source_target_pairs={{0,1},{1,0},{2,3},{3,2},{4,5},{5,4},{6,7},{7,6},{8,9},{9,8},{10,11... | collective-permute-start | bytes 688136 | tf_op jit(solution)/shard_map/ppermute | solution.py:309
  18.8 1.5 %collective-permute-start.12 = (bf16[32,3584]{1,0:T(8,128)(2,1)S(1)}, bf16[32,3584]{1,0:T(8,128)(2,1)S(1)}, u32[]{:S(2)}, u32[]{:S(2)}) collective-permute-start(bf16[32,3584]{1,0:T(8,128)(2,1)S(1)} %get-tuple-element.62), channel_id=1, source_target_pairs={{0,16},{1,17},{2,18},{3,19},{4,20},{5,21},{6,22},{7,23},{8,24},{9,... | collective-permute-start | bytes 688136 | tf_op jit(solution)/shard_map/ppermute | solution.py:309
  20.3 3.9 %collective-permute-start.8 = (bf16[16,3712]{1,0:T(8,128)(2,1)S(1)}, bf16[16,3712]{1,0:T(8,128)(2,1)S(1)}, u32[]{:S(2)}, u32[]{:S(2)}) collective-permute-start(bf16[16,3712]{1,0:T(8,128)(2,1)S(1)} %collective-permute-done.3.refs_4_), channel_id=1, source_target_pairs={{0,4},{1,5},{2,6},{3,7},{4,0},{5,1},{6,2},{7,3},{8,12},{9,13},{10,... | collective-permute-start | bytes 356360 | tf_op jit(solution)/shard_map/ppermute | solution.py:309
  24.7 3.3 %collective-permute-start.10 = (bf16[16,3712]{1,0:T(8,128)(2,1)S(1)}, bf16[16,3712]{1,0:T(8,128)(2,1)S(1)}, u32[]{:S(2)}, u32[]{:S(2)}) collective-permute-start(bf16[16,3712]{1,0:T(8,128)(2,1)S(1)} %collective-permute-done.3.refs_4_), channel_id=1, source_target_pairs={{0,6},{1,7},{2,4},{3,5},{4,2},{5,3},{6,0},{7,1},{8,14},{9,15},{10,... | collective-permute-start | bytes 356360 | tf_op jit(solution)/shard_map/ppermute | solution.py:309
  27.9 3.7 %shard_map.94 = (bf16[3584,256]{1,0:T(8,128)(2,1)S(1)}, bf16[3584,256]{1,0:T(8,128)(2,1)S(1)}, bf16[256,3584]{1,0:T(8,128)(2,1)S(1)}, bf16[1024,1792]{1,0:T(8,128)(2,1)S(1)}, f32[8,128]{1,0:T(8,128)S(1)}) custom-call(bf16[3584,256]{1,0:T(8,128)(2,1)} %refs_0_.1, bf16[3584,256]{1,0:T(8,128)(2,1)} %refs_1_.1, bf16[256,3584]{1,0:T(8,128)(2,1)} %refs_2_.1, ...), custom_call_target="tpu_custom_call" | custom-call | tf_op jit(solution)/shard_map/pallas_call | solution.py:40
  31.7 2.1 %shard_map.98 = (bf16[128,1024]{1,0:T(8,128)(2,1)S(1)}, bf16[1024,1792]{1,0:T(8,128)(2,1)S(1)}) custom-call(bf16[32,3584]{1,0:T(8,128)(2,1)S(1)} %get-tuple-element.77.refs_0_, bf16[32,3584]{1,0:T(8,128)(2,1)S(1)} %collective-permute-done.12.refs_1_, bf16[32,3584]{1,0:T(8,128)(2,1)S(1)} %collective-permute-done.11.refs_2_, ...), custom_call_target="tpu_custom_call" | custom-call | tf_op jit(solution)/shard_map/pallas_call | solution.py:40
  33.8 0.7 %shard_map.99 = (bf16[32,1792]{1,0:T(8,128)(2,1)S(1)}, bf16[32,1792]{1,0:T(8,128)(2,1)S(1)}, bf16[32,1792]{1,0:T(8,128)(2,1)S(1)}, bf16[32,1792]{1,0:T(8,128)(2,1)S(1)}) custom-call(bf16[128,1024]{1,0:T(8,128)(2,1)S(1)} %get-tuple-element.83.hidden_ref, bf16[1024,1792]{1,0:T(8,128)(2,1)S(1)} %get-tuple-element.84.down_ref), custom_call_target="tpu_custom_call" | custom-call | tf_op jit(solution)/shard_map/pallas_call | solution.py:40
  34.5 1.6 %collective-permute-start.14 = (bf16[32,1792]{1,0:T(8,128)(2,1)S(1)}, bf16[32,1792]{1,0:T(8,128)(2,1)S(1)}, u32[]{:S(2)}, u32[]{:S(2)}) collective-permute-start(bf16[32,1792]{1,0:T(8,128)(2,1)S(1)} %get-tuple-element.86), channel_id=1, source_target_pairs={{0,16},{1,17},{2,18},{3,19},{4,20},{5,21},{6,22},{7,23},{8,24},{9,... | collective-permute-start | bytes 344072 | tf_op jit(solution)/shard_map/ppermute | solution.py:309
  36.7 0.7 %shard_map.102 = (bf16[32,1792]{1,0:T(8,128)(2,1)S(1)}, bf16[32,1792]{1,0:T(8,128)(2,1)S(1)}, bf16[32,1792]{1,0:T(8,128)(2,1)S(1)}, bf16[32,1792]{1,0:T(8,128)(2,1)S(1)}) custom-call(bf16[128,1024]{1,0:T(8,128)(2,1)S(1)} %get-tuple-element.83.hidden_ref, bf16[1024,1792]{1,0:T(8,128)(2,1)S(1)} %get-tuple-element.96.down_ref), custom_call_target="tpu_custom_call" | custom-call | tf_op jit(solution)/shard_map/pallas_call | solution.py:40
  37.4 1.6 %collective-permute-start.21 = (bf16[32,1792]{1,0:T(8,128)(2,1)S(1)}, bf16[32,1792]{1,0:T(8,128)(2,1)S(1)}, u32[]{:S(2)}, u32[]{:S(2)}) collective-permute-start(bf16[32,1792]{1,0:T(8,128)(2,1)S(1)} %get-tuple-element.98), channel_id=1, source_target_pairs={{0,16},{1,17},{2,18},{3,19},{4,20},{5,21},{6,22},{7,23},{8,24},{9,... | collective-permute-start | bytes 344072 | tf_op jit(solution)/shard_map/ppermute | solution.py:309
  38.9 0.7 %collective-permute-done.14.refs_1_ = bf16[32,1792]{1,0:T(8,128)(2,1)S(1)} collective-permute-done((bf16[32,1792]{1,0:T(8,128)(2,1)S(1)}, bf16[32,1792]{1,0:T(8,128)(2,1)S(1)}, u32[]{:S(2)}, u32[]{:S(2)}) %collective-permute-start.14) | collective-permute-done | bytes 114720 | tf_op jit(solution)/shard_map/ppermute | solution.py:309
  40.2 0.7 %shard_map.95.hidden_ref = bf16[128,256]{1,0:T(8,128)(2,1)S(1)} custom-call(bf16[16,3712]{1,0:T(8,128)(2,1)S(1)} %shard_map.91.refs_2_.refs_0_, bf16[16,3712]{1,0:T(8,128)(2,1)S(1)} %collective-permute-done.refs_1_, bf16[16,3712]{1,0:T(8,128)(2,1)S(1)} %collective-permute-done.1.refs_2_, bf16[16,3712]{1,0:T(8,128)(2,1)S(1)} %collective-permute-done.2.refs_3_, ...), custom_call_target="tpu_custom_call" | custom-call | tf_op jit(solution)/shard_map/pallas_call | solution.py:40
  41.3 0.7 %collective-permute-done.15.refs_2_ = bf16[32,1792]{1,0:T(8,128)(2,1)S(1)} collective-permute-done((bf16[32,1792]{1,0:T(8,128)(2,1)S(1)}, bf16[32,1792]{1,0:T(8,128)(2,1)S(1)}, u32[]{:S(2)}, u32[]{:S(2)}) %collective-permute-start.15) | collective-permute-done | bytes 114720 | tf_op jit(solution)/shard_map/ppermute | solution.py:309
  42.4 1.0 %collective-permute-start.17 = (bf16[64,1792]{1,0:T(8,128)(2,1)S(1)}, bf16[64,1792]{1,0:T(8,128)(2,1)S(1)}, u32[]{:S(2)}, u32[]{:S(2)}) collective-permute-start(bf16[64,1792]{1,0:T(8,128)(2,1)S(1)} %get-tuple-element.90), channel_id=1, source_target_pairs={{0,1},{1,0},{2,3},{3,2},{4,5},{5,4},{6,7},{7,6},{8,9},{9,8},{10,11... | collective-permute-start | bytes 688136 | tf_op jit(solution)/shard_map/ppermute | solution.py:309
  43.4 1.1 %collective-permute-done.21.refs_1_ = bf16[32,1792]{1,0:T(8,128)(2,1)S(1)} collective-permute-done((bf16[32,1792]{1,0:T(8,128)(2,1)S(1)}, bf16[32,1792]{1,0:T(8,128)(2,1)S(1)}, u32[]{:S(2)}, u32[]{:S(2)}) %collective-permute-start.21) | collective-permute-done | bytes 114720 | tf_op jit(solution)/shard_map/ppermute | solution.py:309
  44.6 1.8 %collective-permute-done.22.refs_2_ = bf16[32,1792]{1,0:T(8,128)(2,1)S(1)} collective-permute-done((bf16[32,1792]{1,0:T(8,128)(2,1)S(1)}, bf16[32,1792]{1,0:T(8,128)(2,1)S(1)}, u32[]{:S(2)}, u32[]{:S(2)}) %collective-permute-start.22) | collective-permute-done | bytes 114720 | tf_op jit(solution)/shard_map/ppermute | solution.py:309
  46.8 1.0 %collective-permute-start.24 = (bf16[64,1792]{1,0:T(8,128)(2,1)S(1)}, bf16[64,1792]{1,0:T(8,128)(2,1)S(1)}, u32[]{:S(2)}, u32[]{:S(2)}) collective-permute-start(bf16[64,1792]{1,0:T(8,128)(2,1)S(1)} %get-tuple-element.102), channel_id=1, source_target_pairs={{0,1},{1,0},{2,3},{3,2},{4,5},{5,4},{6,7},{7,6},{8,9},{9,8},{10,11... | collective-permute-start | bytes 688136 | tf_op jit(solution)/shard_map/ppermute | solution.py:309
  47.8 2.1 %collective-permute-done.17.refs_0_ = bf16[64,1792]{1,0:T(8,128)(2,1)S(1)} collective-permute-done((bf16[64,1792]{1,0:T(8,128)(2,1)S(1)}, bf16[64,1792]{1,0:T(8,128)(2,1)S(1)}, u32[]{:S(2)}, u32[]{:S(2)}) %collective-permute-start.17) | collective-permute-done | bytes 229408 | tf_op jit(solution)/shard_map/ppermute | solution.py:309
  49.9 2.4 %collective-permute-start.18 = (bf16[16,1792]{1,0:T(8,128)(2,1)S(1)}, bf16[16,1792]{1,0:T(8,128)(2,1)S(1)}, u32[]{:S(2)}, u32[]{:S(2)}) collective-permute-start(bf16[16,1792]{1,0:T(8,128)(2,1)S(1)} %get-tuple-element.92), channel_id=1, source_target_pairs={{0,6},{1,7},{2,4},{3,5},{4,2},{5,3},{6,0},{7,1},{8,14},{9,15},{10,... | collective-permute-start | bytes 172040 | tf_op jit(solution)/shard_map/ppermute | solution.py:309
  52.9 1.5 %collective-permute-start.20 = (bf16[16,1792]{1,0:T(8,128)(2,1)S(1)}, bf16[16,1792]{1,0:T(8,128)(2,1)S(1)}, u32[]{:S(2)}, u32[]{:S(2)}) collective-permute-start(bf16[16,1792]{1,0:T(8,128)(2,1)S(1)} %get-tuple-element.94), channel_id=1, source_target_pairs={{0,2},{1,3},{2,0},{3,1},{4,6},{5,7},{6,4},{7,5},{8,10},{9,11},{10,... | collective-permute-start | bytes 172040 | tf_op jit(solution)/shard_map/ppermute | solution.py:309
  54.9 2.4 %collective-permute-start.25 = (bf16[16,1792]{1,0:T(8,128)(2,1)S(1)}, bf16[16,1792]{1,0:T(8,128)(2,1)S(1)}, u32[]{:S(2)}, u32[]{:S(2)}) collective-permute-start(bf16[16,1792]{1,0:T(8,128)(2,1)S(1)} %get-tuple-element.104), channel_id=1, source_target_pairs={{0,6},{1,7},{2,4},{3,5},{4,2},{5,3},{6,0},{7,1},{8,14},{9,15},{10,... | collective-permute-start | bytes 172040 | tf_op jit(solution)/shard_map/ppermute | solution.py:309
  57.8 1.5 %collective-permute-start.27 = (bf16[16,1792]{1,0:T(8,128)(2,1)S(1)}, bf16[16,1792]{1,0:T(8,128)(2,1)S(1)}, u32[]{:S(2)}, u32[]{:S(2)}) collective-permute-start(bf16[16,1792]{1,0:T(8,128)(2,1)S(1)} %get-tuple-element.106), channel_id=1, source_target_pairs={{0,2},{1,3},{2,0},{3,1},{4,6},{5,7},{6,4},{7,5},{8,10},{9,11},{10,... | collective-permute-start | bytes 172040 | tf_op jit(solution)/shard_map/ppermute | solution.py:309
  59.3 2.0 %collective-permute-done.25.refs_5_ = bf16[16,1792]{1,0:T(8,128)(2,1)S(1)} collective-permute-done((bf16[16,1792]{1,0:T(8,128)(2,1)S(1)}, bf16[16,1792]{1,0:T(8,128)(2,1)S(1)}, u32[]{:S(2)}, u32[]{:S(2)}) %collective-permute-start.25) | collective-permute-done | bytes 57376 | tf_op jit(solution)/shard_map/ppermute | solution.py:309
  61.3 2.0 %collective-permute-done.26.refs_6_ = bf16[16,1792]{1,0:T(8,128)(2,1)S(1)} collective-permute-done((bf16[16,1792]{1,0:T(8,128)(2,1)S(1)}, bf16[16,1792]{1,0:T(8,128)(2,1)S(1)}, u32[]{:S(2)}, u32[]{:S(2)}) %collective-permute-start.26) | collective-permute-done | bytes 57376 | tf_op jit(solution)/shard_map/ppermute | solution.py:309
  63.3 0.7 %shard_map.105 = bf16[16,3584]{1,0:T(8,128)(2,1)} custom-call(f32[16,1792]{1,0:T(8,128)S(1)} %get-tuple-element.91.refs_0_, bf16[16,1792]{1,0:T(8,128)(2,1)S(1)} %collective-permute-done.18.refs_1_, bf16[16,1792]{1,0:T(8,128)(2,1)S(1)} %collective-permute-done.19.refs_2_, bf16[16,1792]{1,0:T(8,128)(2,1)S(1)} %collective-permute-done.20.refs_3_, ...), custom_call_target="tpu_custom_call" | custom-call | tf_op jit(solution)/shard_map/pallas_call | solution.py:40
  (39 shorter events, 5.9 us)
Async XLA Ops:
  1.0 12.6 %collective-permute-start.1 = (bf16[16,3712]{1,0:T(8,128)(2,1)S(1)}, bf16[16,3712]{1,0:T(8,128)(2,1)S(1)}, u32[]{:S(2)}, u32[]{:S(2)}) collective-permute-start(bf16[16,3712]{1,0:T(8,128)(2,1)S(1)} %shard_map.91.refs_2_.refs_0_), channel_id=1, source_target_pairs={{0,4},{1,5},{2,6},{3,7},{4,0},{5,1},{6,2},{7,3},{8,12},{9,13},{10,... | collective-permute-start | bytes 356360 | tf_op jit(solution)/shard_map/ppermute | solution.py:309
  5.1 9.1 %collective-permute-start = (bf16[16,3712]{1,0:T(8,128)(2,1)S(1)}, bf16[16,3712]{1,0:T(8,128)(2,1)S(1)}, u32[]{:S(2)}, u32[]{:S(2)}) collective-permute-start(bf16[16,3712]{1,0:T(8,128)(2,1)S(1)} %shard_map.91.refs_2_.refs_0_), channel_id=1, source_target_pairs={{0,2},{1,3},{2,0},{3,1},{4,6},{5,7},{6,4},{7,5},{8,10},{9,11},{10,... | collective-permute-start | bytes 356360 | tf_op jit(solution)/shard_map/ppermute | solution.py:309
  6.6 7.9 %collective-permute-start.2 = (bf16[16,3712]{1,0:T(8,128)(2,1)S(1)}, bf16[16,3712]{1,0:T(8,128)(2,1)S(1)}, u32[]{:S(2)}, u32[]{:S(2)}) collective-permute-start(bf16[16,3712]{1,0:T(8,128)(2,1)S(1)} %shard_map.91.refs_2_.refs_0_), channel_id=1, source_target_pairs={{0,6},{1,7},{2,4},{3,5},{4,2},{5,3},{6,0},{7,1},{8,14},{9,15},{10,... | collective-permute-start | bytes 356360 | tf_op jit(solution)/shard_map/ppermute | solution.py:309
  6.6 8.0 %collective-permute-start.3 = (bf16[16,3712]{1,0:T(8,128)(2,1)S(1)}, bf16[16,3712]{1,0:T(8,128)(2,1)S(1)}, u32[]{:S(2)}, u32[]{:S(2)}) collective-permute-start(bf16[16,3712]{1,0:T(8,128)(2,1)S(1)} %shard_map.91.refs_2_.refs_0_), channel_id=1, source_target_pairs={{0,1},{1,0},{2,3},{3,2},{4,5},{5,4},{6,7},{7,6},{8,9},{9,8},{10,11... | collective-permute-start | bytes 356360 | tf_op jit(solution)/shard_map/ppermute | solution.py:309
  8.4 6.3 %collective-permute-start.4 = (bf16[16,3712]{1,0:T(8,128)(2,1)S(1)}, bf16[16,3712]{1,0:T(8,128)(2,1)S(1)}, u32[]{:S(2)}, u32[]{:S(2)}) collective-permute-start(bf16[16,3712]{1,0:T(8,128)(2,1)S(1)} %shard_map.91.refs_2_.refs_0_), channel_id=1, source_target_pairs={{0,8},{1,9},{2,10},{3,11},{4,12},{5,13},{6,14},{7,15},{8,0},{9,1},... | collective-permute-start | bytes 356360 | tf_op jit(solution)/shard_map/ppermute | solution.py:309
  13.6 1.9 %collective-permute-start.6 = (bf16[16,3712]{1,0:T(8,128)(2,1)S(1)}, bf16[16,3712]{1,0:T(8,128)(2,1)S(1)}, u32[]{:S(2)}, u32[]{:S(2)}) collective-permute-start(bf16[16,3712]{1,0:T(8,128)(2,1)S(1)} %collective-permute-done.1.refs_2_), channel_id=1, source_target_pairs={{0,8},{1,9},{2,10},{3,11},{4,12},{5,13},{6,14},{7,15},{8,0},{9,1},... | collective-permute-start | bytes 356360 | tf_op jit(solution)/shard_map/ppermute | solution.py:309
  14.2 1.3 %collective-permute-start.5 = (bf16[16,3712]{1,0:T(8,128)(2,1)S(1)}, bf16[16,3712]{1,0:T(8,128)(2,1)S(1)}, u32[]{:S(2)}, u32[]{:S(2)}) collective-permute-start(bf16[16,3712]{1,0:T(8,128)(2,1)S(1)} %collective-permute-done.refs_1_), channel_id=1, source_target_pairs={{0,8},{1,9},{2,10},{3,11},{4,12},{5,13},{6,14},{7,15},{8,0},{9,1},... | collective-permute-start | bytes 356360 | tf_op jit(solution)/shard_map/ppermute | solution.py:309
  14.6 1.3 %collective-permute-start.7 = (bf16[16,3712]{1,0:T(8,128)(2,1)S(1)}, bf16[16,3712]{1,0:T(8,128)(2,1)S(1)}, u32[]{:S(2)}, u32[]{:S(2)}) collective-permute-start(bf16[16,3712]{1,0:T(8,128)(2,1)S(1)} %collective-permute-done.2.refs_3_), channel_id=1, source_target_pairs={{0,8},{1,9},{2,10},{3,11},{4,12},{5,13},{6,14},{7,15},{8,0},{9,1},... | collective-permute-start | bytes 356360 | tf_op jit(solution)/shard_map/ppermute | solution.py:309
  16.6 8.0 %collective-permute-start.11 = (bf16[32,3584]{1,0:T(8,128)(2,1)S(1)}, bf16[32,3584]{1,0:T(8,128)(2,1)S(1)}, u32[]{:S(2)}, u32[]{:S(2)}) collective-permute-start(bf16[32,3584]{1,0:T(8,128)(2,1)S(1)} %get-tuple-element.63), channel_id=1, source_target_pairs={{0,1},{1,0},{2,3},{3,2},{4,5},{5,4},{6,7},{7,6},{8,9},{9,8},{10,11... | collective-permute-start | bytes 688136 | tf_op jit(solution)/shard_map/ppermute | solution.py:309
  18.8 12.9 %collective-permute-start.12 = (bf16[32,3584]{1,0:T(8,128)(2,1)S(1)}, bf16[32,3584]{1,0:T(8,128)(2,1)S(1)}, u32[]{:S(2)}, u32[]{:S(2)}) collective-permute-start(bf16[32,3584]{1,0:T(8,128)(2,1)S(1)} %get-tuple-element.62), channel_id=1, source_target_pairs={{0,16},{1,17},{2,18},{3,19},{4,20},{5,21},{6,22},{7,23},{8,24},{9,... | collective-permute-start | bytes 688136 | tf_op jit(solution)/shard_map/ppermute | solution.py:309
  20.2 11.5 %collective-permute-start.13 = (bf16[32,3584]{1,0:T(8,128)(2,1)S(1)}, bf16[32,3584]{1,0:T(8,128)(2,1)S(1)}, u32[]{:S(2)}, u32[]{:S(2)}) collective-permute-start(bf16[32,3584]{1,0:T(8,128)(2,1)S(1)} %get-tuple-element.64), channel_id=1, source_target_pairs={{0,17},{1,16},{2,19},{3,18},{4,21},{5,20},{6,23},{7,22},{8,25},{9,... | collective-permute-start | bytes 688136 | tf_op jit(solution)/shard_map/ppermute | solution.py:309
  20.3 15.8 %collective-permute-start.8 = (bf16[16,3712]{1,0:T(8,128)(2,1)S(1)}, bf16[16,3712]{1,0:T(8,128)(2,1)S(1)}, u32[]{:S(2)}, u32[]{:S(2)}) collective-permute-start(bf16[16,3712]{1,0:T(8,128)(2,1)S(1)} %collective-permute-done.3.refs_4_), channel_id=1, source_target_pairs={{0,4},{1,5},{2,6},{3,7},{4,0},{5,1},{6,2},{7,3},{8,12},{9,13},{10,... | collective-permute-start | bytes 356360 | tf_op jit(solution)/shard_map/ppermute | solution.py:309
  24.2 13.1 %collective-permute-start.9 = (bf16[16,3712]{1,0:T(8,128)(2,1)S(1)}, bf16[16,3712]{1,0:T(8,128)(2,1)S(1)}, u32[]{:S(2)}, u32[]{:S(2)}) collective-permute-start(bf16[16,3712]{1,0:T(8,128)(2,1)S(1)} %collective-permute-done.3.refs_4_), channel_id=1, source_target_pairs={{0,2},{1,3},{2,0},{3,1},{4,6},{5,7},{6,4},{7,5},{8,10},{9,11},{10,... | collective-permute-start | bytes 356360 | tf_op jit(solution)/shard_map/ppermute | solution.py:309
  24.7 14.2 %collective-permute-start.10 = (bf16[16,3712]{1,0:T(8,128)(2,1)S(1)}, bf16[16,3712]{1,0:T(8,128)(2,1)S(1)}, u32[]{:S(2)}, u32[]{:S(2)}) collective-permute-start(bf16[16,3712]{1,0:T(8,128)(2,1)S(1)} %collective-permute-done.3.refs_4_), channel_id=1, source_target_pairs={{0,6},{1,7},{2,4},{3,5},{4,2},{5,3},{6,0},{7,1},{8,14},{9,15},{10,... | collective-permute-start | bytes 356360 | tf_op jit(solution)/shard_map/ppermute | solution.py:309
  34.5 5.2 %collective-permute-start.14 = (bf16[32,1792]{1,0:T(8,128)(2,1)S(1)}, bf16[32,1792]{1,0:T(8,128)(2,1)S(1)}, u32[]{:S(2)}, u32[]{:S(2)}) collective-permute-start(bf16[32,1792]{1,0:T(8,128)(2,1)S(1)} %get-tuple-element.86), channel_id=1, source_target_pairs={{0,16},{1,17},{2,18},{3,19},{4,20},{5,21},{6,22},{7,23},{8,24},{9,... | collective-permute-start | bytes 344072 | tf_op jit(solution)/shard_map/ppermute | solution.py:309
  36.0 6.0 %collective-permute-start.15 = (bf16[32,1792]{1,0:T(8,128)(2,1)S(1)}, bf16[32,1792]{1,0:T(8,128)(2,1)S(1)}, u32[]{:S(2)}, u32[]{:S(2)}) collective-permute-start(bf16[32,1792]{1,0:T(8,128)(2,1)S(1)} %get-tuple-element.87), channel_id=1, source_target_pairs={{0,24},{1,25},{2,26},{3,27},{4,28},{5,29},{6,30},{7,31},{8,16},{9,... | collective-permute-start | bytes 344072 | tf_op jit(solution)/shard_map/ppermute | solution.py:309
  36.0 6.0 %collective-permute-start.16 = (bf16[32,1792]{1,0:T(8,128)(2,1)S(1)}, bf16[32,1792]{1,0:T(8,128)(2,1)S(1)}, u32[]{:S(2)}, u32[]{:S(2)}) collective-permute-start(bf16[32,1792]{1,0:T(8,128)(2,1)S(1)} %get-tuple-element.88), channel_id=1, source_target_pairs={{0,8},{1,9},{2,10},{3,11},{4,12},{5,13},{6,14},{7,15},{8,0},{9,1},... | collective-permute-start | bytes 344072 | tf_op jit(solution)/shard_map/ppermute | solution.py:309
  37.4 7.2 %collective-permute-start.21 = (bf16[32,1792]{1,0:T(8,128)(2,1)S(1)}, bf16[32,1792]{1,0:T(8,128)(2,1)S(1)}, u32[]{:S(2)}, u32[]{:S(2)}) collective-permute-start(bf16[32,1792]{1,0:T(8,128)(2,1)S(1)} %get-tuple-element.98), channel_id=1, source_target_pairs={{0,16},{1,17},{2,18},{3,19},{4,20},{5,21},{6,22},{7,23},{8,24},{9,... | collective-permute-start | bytes 344072 | tf_op jit(solution)/shard_map/ppermute | solution.py:309
  38.9 7.5 %collective-permute-start.22 = (bf16[32,1792]{1,0:T(8,128)(2,1)S(1)}, bf16[32,1792]{1,0:T(8,128)(2,1)S(1)}, u32[]{:S(2)}, u32[]{:S(2)}) collective-permute-start(bf16[32,1792]{1,0:T(8,128)(2,1)S(1)} %get-tuple-element.99), channel_id=1, source_target_pairs={{0,24},{1,25},{2,26},{3,27},{4,28},{5,29},{6,30},{7,31},{8,16},{9,... | collective-permute-start | bytes 344072 | tf_op jit(solution)/shard_map/ppermute | solution.py:309
  39.7 6.7 %collective-permute-start.23 = (bf16[32,1792]{1,0:T(8,128)(2,1)S(1)}, bf16[32,1792]{1,0:T(8,128)(2,1)S(1)}, u32[]{:S(2)}, u32[]{:S(2)}) collective-permute-start(bf16[32,1792]{1,0:T(8,128)(2,1)S(1)} %get-tuple-element.100), channel_id=1, source_target_pairs={{0,8},{1,9},{2,10},{3,11},{4,12},{5,13},{6,14},{7,15},{8,0},{9,1},... | collective-permute-start | bytes 344072 | tf_op jit(solution)/shard_map/ppermute | solution.py:309
  42.4 7.5 %collective-permute-start.17 = (bf16[64,1792]{1,0:T(8,128)(2,1)S(1)}, bf16[64,1792]{1,0:T(8,128)(2,1)S(1)}, u32[]{:S(2)}, u32[]{:S(2)}) collective-permute-start(bf16[64,1792]{1,0:T(8,128)(2,1)S(1)} %get-tuple-element.90), channel_id=1, source_target_pairs={{0,1},{1,0},{2,3},{3,2},{4,5},{5,4},{6,7},{7,6},{8,9},{9,8},{10,11... | collective-permute-start | bytes 688136 | tf_op jit(solution)/shard_map/ppermute | solution.py:309
  46.8 8.0 %collective-permute-start.24 = (bf16[64,1792]{1,0:T(8,128)(2,1)S(1)}, bf16[64,1792]{1,0:T(8,128)(2,1)S(1)}, u32[]{:S(2)}, u32[]{:S(2)}) collective-permute-start(bf16[64,1792]{1,0:T(8,128)(2,1)S(1)} %get-tuple-element.102), channel_id=1, source_target_pairs={{0,1},{1,0},{2,3},{3,2},{4,5},{5,4},{6,7},{7,6},{8,9},{9,8},{10,11... | collective-permute-start | bytes 688136 | tf_op jit(solution)/shard_map/ppermute | solution.py:309
  49.9 7.9 %collective-permute-start.18 = (bf16[16,1792]{1,0:T(8,128)(2,1)S(1)}, bf16[16,1792]{1,0:T(8,128)(2,1)S(1)}, u32[]{:S(2)}, u32[]{:S(2)}) collective-permute-start(bf16[16,1792]{1,0:T(8,128)(2,1)S(1)} %get-tuple-element.92), channel_id=1, source_target_pairs={{0,6},{1,7},{2,4},{3,5},{4,2},{5,3},{6,0},{7,1},{8,14},{9,15},{10,... | collective-permute-start | bytes 172040 | tf_op jit(solution)/shard_map/ppermute | solution.py:309
  52.4 7.0 %collective-permute-start.19 = (bf16[16,1792]{1,0:T(8,128)(2,1)S(1)}, bf16[16,1792]{1,0:T(8,128)(2,1)S(1)}, u32[]{:S(2)}, u32[]{:S(2)}) collective-permute-start(bf16[16,1792]{1,0:T(8,128)(2,1)S(1)} %get-tuple-element.93), channel_id=1, source_target_pairs={{0,4},{1,5},{2,6},{3,7},{4,0},{5,1},{6,2},{7,3},{8,12},{9,13},{10,... | collective-permute-start | bytes 172040 | tf_op jit(solution)/shard_map/ppermute | solution.py:309
  52.9 6.5 %collective-permute-start.20 = (bf16[16,1792]{1,0:T(8,128)(2,1)S(1)}, bf16[16,1792]{1,0:T(8,128)(2,1)S(1)}, u32[]{:S(2)}, u32[]{:S(2)}) collective-permute-start(bf16[16,1792]{1,0:T(8,128)(2,1)S(1)} %get-tuple-element.94), channel_id=1, source_target_pairs={{0,2},{1,3},{2,0},{3,1},{4,6},{5,7},{6,4},{7,5},{8,10},{9,11},{10,... | collective-permute-start | bytes 172040 | tf_op jit(solution)/shard_map/ppermute | solution.py:309
  54.9 6.4 %collective-permute-start.25 = (bf16[16,1792]{1,0:T(8,128)(2,1)S(1)}, bf16[16,1792]{1,0:T(8,128)(2,1)S(1)}, u32[]{:S(2)}, u32[]{:S(2)}) collective-permute-start(bf16[16,1792]{1,0:T(8,128)(2,1)S(1)} %get-tuple-element.104), channel_id=1, source_target_pairs={{0,6},{1,7},{2,4},{3,5},{4,2},{5,3},{6,0},{7,1},{8,14},{9,15},{10,... | collective-permute-start | bytes 172040 | tf_op jit(solution)/shard_map/ppermute | solution.py:309
  57.3 6.0 %collective-permute-start.26 = (bf16[16,1792]{1,0:T(8,128)(2,1)S(1)}, bf16[16,1792]{1,0:T(8,128)(2,1)S(1)}, u32[]{:S(2)}, u32[]{:S(2)}) collective-permute-start(bf16[16,1792]{1,0:T(8,128)(2,1)S(1)} %get-tuple-element.105), channel_id=1, source_target_pairs={{0,4},{1,5},{2,6},{3,7},{4,0},{5,1},{6,2},{7,3},{8,12},{9,13},{10,... | collective-permute-start | bytes 172040 | tf_op jit(solution)/shard_map/ppermute | solution.py:309
  57.8 5.5 %collective-permute-start.27 = (bf16[16,1792]{1,0:T(8,128)(2,1)S(1)}, bf16[16,1792]{1,0:T(8,128)(2,1)S(1)}, u32[]{:S(2)}, u32[]{:S(2)}) collective-permute-start(bf16[16,1792]{1,0:T(8,128)(2,1)S(1)} %get-tuple-element.106), channel_id=1, source_target_pairs={{0,2},{1,3},{2,0},{3,1},{4,6},{5,7},{6,4},{7,5},{8,10},{9,11},{10,... | collective-permute-start | bytes 172040 | tf_op jit(solution)/shard_map/ppermute | solution.py:309

commit v6 on v5

--- a/solution.py
+++ b/solution.py
@@ -149,8 +149,7 @@
     return hit, weight
 
 
-def select_kernel(width, block_rows, capacity, inner_count, chips_x, blocks, *refs):
-    pieces, outs = refs[:blocks], refs[blocks + 1:]
+def chosen_rows(width, block_rows, capacity, inner_count, chips_x, groups, pieces):
     outer_at, inner_at = lax.axis_index("outer"), lax.axis_index("inner")
 
     def expert_of(group):
@@ -159,12 +158,22 @@
         return (outer_at ^ (along_x * CORES)) * inner_count + (inner_at ^ along_y)
 
     meta = jnp.concatenate([piece[:, width:] for piece in pieces], axis=0).astype(F32)
-    hit, _ = routing(meta, block_rows, capacity, len(outs), expert_of)
+    hit, _ = routing(meta, block_rows, capacity, groups, expert_of)
     rows = jnp.concatenate([piece[:, :width] for piece in pieces], axis=0)
-    chosen = dot_first(jnp.where(hit, 1.0, 0.0).astype(BF16), rows).astype(BF16)
-    each = outs[0].shape[0]
+    return dot_first(jnp.where(hit, 1.0, 0.0).astype(BF16), rows)
+
+
+def own_kernel(sizes, *refs):
+    refs[-1][...] = chosen_rows(*sizes, refs[:-1])
+
+
+def select_kernel(sizes, blocks, *refs):
+    own_ref, pieces, outs = refs[0], refs[1:1 + blocks], refs[2 + blocks:]
+    others = chosen_rows(*sizes, pieces)
+    part = others.shape[0] // len(outs)
     for at, out in enumerate(outs):
-        out[...] = chosen[at * each:(at + 1) * each]
+        chosen = slice(at * part, (at + 1) * part)
+        out[...] = jnp.concatenate([own_ref[chosen], others[chosen]], axis=0).astype(BF16)
 
 
 def hidden_kernel(width, blocks, *refs):
@@ -325,17 +334,20 @@
     other = [None] * DEPTH_Z
     for k in reversed(range(DEPTH_Z)):
         other[k] = swap(column[k], along_outer(1))
-    at_hand = column + other
 
     groups = depth_y * chips_x
+    part = DEPTH_Z * capacity
+    sizes = (model_width, rows, capacity, inner_count, chips_x, groups)
+    own_rows = call(
+        functools.partial(own_kernel, sizes), whole((groups * part, model_width), F32), *column
+    )
     blocks = call(
-        functools.partial(
-            select_kernel, model_width, rows, capacity, inner_count, chips_x, len(at_hand)
-        ),
-        [whole((CORES * DEPTH_Z * capacity, model_width), BF16)] * groups,
-        *at_hand,
+        functools.partial(select_kernel, sizes, DEPTH_Z),
+        [whole((CORES * part, model_width), BF16)] * groups,
+        own_rows,
+        *other,
         loaded,
-        in_specs=[IN_VMEM] * len(at_hand) + [ANYWHERE],
+        in_specs=[IN_VMEM] * (1 + DEPTH_Z) + [ANYWHERE],
         out_specs=[IN_VMEM] * groups,
     )
     arrived = [blocks[0]] + [None] * (groups - 1)

time: 64.3 us -> 64.2 us (level)
    pallas_call x15 -> x16, Pallas kernels: 17.3 us -> 17.6 us  [call(): pl.pallas_call(kernel, out_shape=out_shape, compiler_params=PARAMS, **more)]
  transfers between devices with their start and end apart: 28 -> 28, of which waited for: 12 -> 12; matrix products, arithmetic and copies ran while one was open for 0% -> 0% of each run, Pallas kernels for 23% -> 24%
where the time goes in v6:
time: 64.2 us; the launch traced here: 63.8 us
  starting transfers between devices  33.7 us (52%)
  Pallas kernels  17.6 us (27%)
  waiting for transfers between devices  12.3 us (19%)
    ppermute x28, starting transfers between devices, swap(): lax.ppermute(array, BOTH, [(at, at ^ distance) for at in range(device_cou...  33.7 us
    pallas_call x16, Pallas kernels, call(): pl.pallas_call(kernel, out_shape=out_shape, compiler_params=PARAMS, **more)  17.6 us
    ppermute x28, waiting for transfers between devices, swap(): lax.ppermute(array, BOTH, [(at, at ^ distance) for at in range(device_cou...  12.3 us
  transfers between devices with their start and end apart: 28, of which 12 were waited for; matrix products, arithmetic and copies ran while one was open for 0% of the time, Pallas kernels for 24%

profile of v6, /device:TPU:0, one launch (start us, length us, event | category | flops | bytes accessed | tf_op | source)
XLA Modules:
  0.0 63.8 jit_solution(9401570978020621114)
XLA Ops:
  0.0 1.0 %shard_map.91.refs_2_.refs_0_ = bf16[16,3712]{1,0:T(8,128)(2,1)S(1)} custom-call(bf16[16,3584]{1,0:T(8,128)(2,1)} %tokens_ref.1, s32[8,16]{1,0:T(8,128)} %bitcast.9, s32[8,16]{1,0:T(8,128)} %bitcast.10), custom_call_target="tpu_custom_call" | custom-call | tf_op jit(solution)/shard_map/pallas_call | solution.py:40
  1.0 4.1 %collective-permute-start.1 = (bf16[16,3712]{1,0:T(8,128)(2,1)S(1)}, bf16[16,3712]{1,0:T(8,128)(2,1)S(1)}, u32[]{:S(2)}, u32[]{:S(2)}) collective-permute-start(bf16[16,3712]{1,0:T(8,128)(2,1)S(1)} %shard_map.91.refs_2_.refs_0_), channel_id=1, source_target_pairs={{0,4},{1,5},{2,6},{3,7},{4,0},{5,1},{6,2},{7,3},{8,12},{9,13},{10,... | collective-permute-start | bytes 356360 | tf_op jit(solution)/shard_map/ppermute | solution.py:318
  5.1 1.6 %collective-permute-start = (bf16[16,3712]{1,0:T(8,128)(2,1)S(1)}, bf16[16,3712]{1,0:T(8,128)(2,1)S(1)}, u32[]{:S(2)}, u32[]{:S(2)}) collective-permute-start(bf16[16,3712]{1,0:T(8,128)(2,1)S(1)} %shard_map.91.refs_2_.refs_0_), channel_id=1, source_target_pairs={{0,2},{1,3},{2,0},{3,1},{4,6},{5,7},{6,4},{7,5},{8,10},{9,11},{10,... | collective-permute-start | bytes 356360 | tf_op jit(solution)/shard_map/ppermute | solution.py:318
  6.6 1.7 %collective-permute-start.3 = (bf16[16,3712]{1,0:T(8,128)(2,1)S(1)}, bf16[16,3712]{1,0:T(8,128)(2,1)S(1)}, u32[]{:S(2)}, u32[]{:S(2)}) collective-permute-start(bf16[16,3712]{1,0:T(8,128)(2,1)S(1)} %shard_map.91.refs_2_.refs_0_), channel_id=1, source_target_pairs={{0,1},{1,0},{2,3},{3,2},{4,5},{5,4},{6,7},{7,6},{8,9},{9,8},{10,11... | collective-permute-start | bytes 356360 | tf_op jit(solution)/shard_map/ppermute | solution.py:318
  8.4 5.2 %shard_map.92 = (bf16[3584,1024]{1,0:T(8,128)(2,1)S(1)}, bf16[3584,1024]{1,0:T(8,128)(2,1)S(1)}, f32[8,128]{1,0:T(8,128)S(1)}) custom-call(bf16[3584,1024]{1,0:T(8,128)(2,1)} %bitcast.7, bf16[3584,1024]{1,0:T(8,128)(2,1)} %bitcast.8, bf16[16,3712]{1,0:T(8,128)(2,1)S(1)} %shard_map.91.refs_2_.refs_0_), custom_call_target="tpu_custom_call" | custom-call | tf_op jit(solution)/shard_map/pallas_call | solution.py:40
  13.6 0.6 collective-permute-start.6
  16.5 2.1 %collective-permute-start.11 = (bf16[32,3584]{1,0:T(8,128)(2,1)S(1)}, bf16[32,3584]{1,0:T(8,128)(2,1)S(1)}, u32[]{:S(2)}, u32[]{:S(2)}) collective-permute-start(bf16[32,3584]{1,0:T(8,128)(2,1)S(1)} %get-tuple-element.63), channel_id=1, source_target_pairs={{0,1},{1,0},{2,3},{3,2},{4,5},{5,4},{6,7},{7,6},{8,9},{9,8},{10,11... | collective-permute-start | bytes 688136 | tf_op jit(solution)/shard_map/ppermute | solution.py:318
  18.6 1.5 %collective-permute-start.12 = (bf16[32,3584]{1,0:T(8,128)(2,1)S(1)}, bf16[32,3584]{1,0:T(8,128)(2,1)S(1)}, u32[]{:S(2)}, u32[]{:S(2)}) collective-permute-start(bf16[32,3584]{1,0:T(8,128)(2,1)S(1)} %get-tuple-element.62), channel_id=1, source_target_pairs={{0,16},{1,17},{2,18},{3,19},{4,20},{5,21},{6,22},{7,23},{8,24},{9,... | collective-permute-start | bytes 688136 | tf_op jit(solution)/shard_map/ppermute | solution.py:318
  20.1 3.9 %collective-permute-start.8 = (bf16[16,3712]{1,0:T(8,128)(2,1)S(1)}, bf16[16,3712]{1,0:T(8,128)(2,1)S(1)}, u32[]{:S(2)}, u32[]{:S(2)}) collective-permute-start(bf16[16,3712]{1,0:T(8,128)(2,1)S(1)} %collective-permute-done.3.refs_4_), channel_id=1, source_target_pairs={{0,4},{1,5},{2,6},{3,7},{4,0},{5,1},{6,2},{7,3},{8,12},{9,13},{10,... | collective-permute-start | bytes 356360 | tf_op jit(solution)/shard_map/ppermute | solution.py:318
  24.5 3.3 %collective-permute-start.10 = (bf16[16,3712]{1,0:T(8,128)(2,1)S(1)}, bf16[16,3712]{1,0:T(8,128)(2,1)S(1)}, u32[]{:S(2)}, u32[]{:S(2)}) collective-permute-start(bf16[16,3712]{1,0:T(8,128)(2,1)S(1)} %collective-permute-done.3.refs_4_), channel_id=1, source_target_pairs={{0,6},{1,7},{2,4},{3,5},{4,2},{5,3},{6,0},{7,1},{8,14},{9,15},{10,... | collective-permute-start | bytes 356360 | tf_op jit(solution)/shard_map/ppermute | solution.py:318
  27.8 3.7 %shard_map.95 = (bf16[3584,256]{1,0:T(8,128)(2,1)S(1)}, bf16[3584,256]{1,0:T(8,128)(2,1)S(1)}, bf16[256,3584]{1,0:T(8,128)(2,1)S(1)}, bf16[1024,1792]{1,0:T(8,128)(2,1)S(1)}, f32[8,128]{1,0:T(8,128)S(1)}) custom-call(bf16[3584,256]{1,0:T(8,128)(2,1)} %refs_0_.1, bf16[3584,256]{1,0:T(8,128)(2,1)} %refs_1_.1, bf16[256,3584]{1,0:T(8,128)(2,1)} %refs_2_.1, ...), custom_call_target="tpu_custom_call" | custom-call | tf_op jit(solution)/shard_map/pallas_call | solution.py:40
  31.5 2.1 %shard_map.99 = (bf16[128,1024]{1,0:T(8,128)(2,1)S(1)}, bf16[1024,1792]{1,0:T(8,128)(2,1)S(1)}) custom-call(bf16[32,3584]{1,0:T(8,128)(2,1)S(1)} %get-tuple-element.77.refs_0_, bf16[32,3584]{1,0:T(8,128)(2,1)S(1)} %collective-permute-done.12.refs_1_, bf16[32,3584]{1,0:T(8,128)(2,1)S(1)} %collective-permute-done.11.refs_2_, ...), custom_call_target="tpu_custom_call" | custom-call | tf_op jit(solution)/shard_map/pallas_call | solution.py:40
  33.6 0.7 %shard_map.100 = (bf16[32,1792]{1,0:T(8,128)(2,1)S(1)}, bf16[32,1792]{1,0:T(8,128)(2,1)S(1)}, bf16[32,1792]{1,0:T(8,128)(2,1)S(1)}, bf16[32,1792]{1,0:T(8,128)(2,1)S(1)}) custom-call(bf16[128,1024]{1,0:T(8,128)(2,1)S(1)} %get-tuple-element.83.hidden_ref, bf16[1024,1792]{1,0:T(8,128)(2,1)S(1)} %get-tuple-element.84.down_ref), custom_call_target="tpu_custom_call" | custom-call | tf_op jit(solution)/shard_map/pallas_call | solution.py:40
  34.3 1.6 %collective-permute-start.14 = (bf16[32,1792]{1,0:T(8,128)(2,1)S(1)}, bf16[32,1792]{1,0:T(8,128)(2,1)S(1)}, u32[]{:S(2)}, u32[]{:S(2)}) collective-permute-start(bf16[32,1792]{1,0:T(8,128)(2,1)S(1)} %get-tuple-element.86), channel_id=1, source_target_pairs={{0,16},{1,17},{2,18},{3,19},{4,20},{5,21},{6,22},{7,23},{8,24},{9,... | collective-permute-start | bytes 344072 | tf_op jit(solution)/shard_map/ppermute | solution.py:318
  35.9 0.6 collective-permute-start.16
  36.5 0.7 %shard_map.103 = (bf16[32,1792]{1,0:T(8,128)(2,1)S(1)}, bf16[32,1792]{1,0:T(8,128)(2,1)S(1)}, bf16[32,1792]{1,0:T(8,128)(2,1)S(1)}, bf16[32,1792]{1,0:T(8,128)(2,1)S(1)}) custom-call(bf16[128,1024]{1,0:T(8,128)(2,1)S(1)} %get-tuple-element.83.hidden_ref, bf16[1024,1792]{1,0:T(8,128)(2,1)S(1)} %get-tuple-element.96.down_ref), custom_call_target="tpu_custom_call" | custom-call | tf_op jit(solution)/shard_map/pallas_call | solution.py:40
  37.2 1.6 %collective-permute-start.21 = (bf16[32,1792]{1,0:T(8,128)(2,1)S(1)}, bf16[32,1792]{1,0:T(8,128)(2,1)S(1)}, u32[]{:S(2)}, u32[]{:S(2)}) collective-permute-start(bf16[32,1792]{1,0:T(8,128)(2,1)S(1)} %get-tuple-element.98), channel_id=1, source_target_pairs={{0,16},{1,17},{2,18},{3,19},{4,20},{5,21},{6,22},{7,23},{8,24},{9,... | collective-permute-start | bytes 344072 | tf_op jit(solution)/shard_map/ppermute | solution.py:318
  38.8 0.7 %collective-permute-done.14.refs_1_ = bf16[32,1792]{1,0:T(8,128)(2,1)S(1)} collective-permute-done((bf16[32,1792]{1,0:T(8,128)(2,1)S(1)}, bf16[32,1792]{1,0:T(8,128)(2,1)S(1)}, u32[]{:S(2)}, u32[]{:S(2)}) %collective-permute-start.14) | collective-permute-done | bytes 114720 | tf_op jit(solution)/shard_map/ppermute | solution.py:318
  40.0 0.7 %shard_map.96.hidden_ref = bf16[128,256]{1,0:T(8,128)(2,1)S(1)} custom-call(bf16[16,3712]{1,0:T(8,128)(2,1)S(1)} %shard_map.91.refs_2_.refs_0_, bf16[16,3712]{1,0:T(8,128)(2,1)S(1)} %collective-permute-done.refs_1_, bf16[16,3712]{1,0:T(8,128)(2,1)S(1)} %collective-permute-done.1.refs_2_, bf16[16,3712]{1,0:T(8,128)(2,1)S(1)} %collective-permute-done.2.refs_3_, ...), custom_call_target="tpu_custom_call" | custom-call | tf_op jit(solution)/shard_map/pallas_call | solution.py:40
  41.1 0.7 %collective-permute-done.15.refs_2_ = bf16[32,1792]{1,0:T(8,128)(2,1)S(1)} collective-permute-done((bf16[32,1792]{1,0:T(8,128)(2,1)S(1)}, bf16[32,1792]{1,0:T(8,128)(2,1)S(1)}, u32[]{:S(2)}, u32[]{:S(2)}) %collective-permute-start.15) | collective-permute-done | bytes 114720 | tf_op jit(solution)/shard_map/ppermute | solution.py:318
  42.3 1.0 %collective-permute-start.17 = (bf16[64,1792]{1,0:T(8,128)(2,1)S(1)}, bf16[64,1792]{1,0:T(8,128)(2,1)S(1)}, u32[]{:S(2)}, u32[]{:S(2)}) collective-permute-start(bf16[64,1792]{1,0:T(8,128)(2,1)S(1)} %get-tuple-element.90), channel_id=1, source_target_pairs={{0,1},{1,0},{2,3},{3,2},{4,5},{5,4},{6,7},{7,6},{8,9},{9,8},{10,11... | collective-permute-start | bytes 688136 | tf_op jit(solution)/shard_map/ppermute | solution.py:318
  43.3 1.1 %collective-permute-done.21.refs_1_ = bf16[32,1792]{1,0:T(8,128)(2,1)S(1)} collective-permute-done((bf16[32,1792]{1,0:T(8,128)(2,1)S(1)}, bf16[32,1792]{1,0:T(8,128)(2,1)S(1)}, u32[]{:S(2)}, u32[]{:S(2)}) %collective-permute-start.21) | collective-permute-done | bytes 114720 | tf_op jit(solution)/shard_map/ppermute | solution.py:318
  44.4 1.8 %collective-permute-done.22.refs_2_ = bf16[32,1792]{1,0:T(8,128)(2,1)S(1)} collective-permute-done((bf16[32,1792]{1,0:T(8,128)(2,1)S(1)}, bf16[32,1792]{1,0:T(8,128)(2,1)S(1)}, u32[]{:S(2)}, u32[]{:S(2)}) %collective-permute-start.22) | collective-permute-done | bytes 114720 | tf_op jit(solution)/shard_map/ppermute | solution.py:318
  46.6 1.0 %collective-permute-start.24 = (bf16[64,1792]{1,0:T(8,128)(2,1)S(1)}, bf16[64,1792]{1,0:T(8,128)(2,1)S(1)}, u32[]{:S(2)}, u32[]{:S(2)}) collective-permute-start(bf16[64,1792]{1,0:T(8,128)(2,1)S(1)} %get-tuple-element.102), channel_id=1, source_target_pairs={{0,1},{1,0},{2,3},{3,2},{4,5},{5,4},{6,7},{7,6},{8,9},{9,8},{10,11... | collective-permute-start | bytes 688136 | tf_op jit(solution)/shard_map/ppermute | solution.py:318
  47.6 2.1 %collective-permute-done.17.refs_0_ = bf16[64,1792]{1,0:T(8,128)(2,1)S(1)} collective-permute-done((bf16[64,1792]{1,0:T(8,128)(2,1)S(1)}, bf16[64,1792]{1,0:T(8,128)(2,1)S(1)}, u32[]{:S(2)}, u32[]{:S(2)}) %collective-permute-start.17) | collective-permute-done | bytes 229408 | tf_op jit(solution)/shard_map/ppermute | solution.py:318
  49.8 2.4 %collective-permute-start.18 = (bf16[16,1792]{1,0:T(8,128)(2,1)S(1)}, bf16[16,1792]{1,0:T(8,128)(2,1)S(1)}, u32[]{:S(2)}, u32[]{:S(2)}) collective-permute-start(bf16[16,1792]{1,0:T(8,128)(2,1)S(1)} %get-tuple-element.92), channel_id=1, source_target_pairs={{0,6},{1,7},{2,4},{3,5},{4,2},{5,3},{6,0},{7,1},{8,14},{9,15},{10,... | collective-permute-start | bytes 172040 | tf_op jit(solution)/shard_map/ppermute | solution.py:318
  52.7 1.5 %collective-permute-start.20 = (bf16[16,1792]{1,0:T(8,128)(2,1)S(1)}, bf16[16,1792]{1,0:T(8,128)(2,1)S(1)}, u32[]{:S(2)}, u32[]{:S(2)}) collective-permute-start(bf16[16,1792]{1,0:T(8,128)(2,1)S(1)} %get-tuple-element.94), channel_id=1, source_target_pairs={{0,2},{1,3},{2,0},{3,1},{4,6},{5,7},{6,4},{7,5},{8,10},{9,11},{10,... | collective-permute-start | bytes 172040 | tf_op jit(solution)/shard_map/ppermute | solution.py:318
  54.7 2.4 %collective-permute-start.25 = (bf16[16,1792]{1,0:T(8,128)(2,1)S(1)}, bf16[16,1792]{1,0:T(8,128)(2,1)S(1)}, u32[]{:S(2)}, u32[]{:S(2)}) collective-permute-start(bf16[16,1792]{1,0:T(8,128)(2,1)S(1)} %get-tuple-element.104), channel_id=1, source_target_pairs={{0,6},{1,7},{2,4},{3,5},{4,2},{5,3},{6,0},{7,1},{8,14},{9,15},{10,... | collective-permute-start | bytes 172040 | tf_op jit(solution)/shard_map/ppermute | solution.py:318
  57.6 1.5 %collective-permute-start.27 = (bf16[16,1792]{1,0:T(8,128)(2,1)S(1)}, bf16[16,1792]{1,0:T(8,128)(2,1)S(1)}, u32[]{:S(2)}, u32[]{:S(2)}) collective-permute-start(bf16[16,1792]{1,0:T(8,128)(2,1)S(1)} %get-tuple-element.106), channel_id=1, source_target_pairs={{0,2},{1,3},{2,0},{3,1},{4,6},{5,7},{6,4},{7,5},{8,10},{9,11},{10,... | collective-permute-start | bytes 172040 | tf_op jit(solution)/shard_map/ppermute | solution.py:318
  59.2 2.0 %collective-permute-done.25.refs_5_ = bf16[16,1792]{1,0:T(8,128)(2,1)S(1)} collective-permute-done((bf16[16,1792]{1,0:T(8,128)(2,1)S(1)}, bf16[16,1792]{1,0:T(8,128)(2,1)S(1)}, u32[]{:S(2)}, u32[]{:S(2)}) %collective-permute-start.25) | collective-permute-done | bytes 57376 | tf_op jit(solution)/shard_map/ppermute | solution.py:318
  61.2 1.9 %collective-permute-done.26.refs_6_ = bf16[16,1792]{1,0:T(8,128)(2,1)S(1)} collective-permute-done((bf16[16,1792]{1,0:T(8,128)(2,1)S(1)}, bf16[16,1792]{1,0:T(8,128)(2,1)S(1)}, u32[]{:S(2)}, u32[]{:S(2)}) %collective-permute-start.26) | collective-permute-done | bytes 57376 | tf_op jit(solution)/shard_map/ppermute | solution.py:318
  63.1 0.7 %shard_map.106 = bf16[16,3584]{1,0:T(8,128)(2,1)} custom-call(f32[16,1792]{1,0:T(8,128)S(1)} %get-tuple-element.91.refs_0_, bf16[16,1792]{1,0:T(8,128)(2,1)S(1)} %collective-permute-done.18.refs_1_, bf16[16,1792]{1,0:T(8,128)(2,1)S(1)} %collective-permute-done.19.refs_2_, bf16[16,1792]{1,0:T(8,128)(2,1)S(1)} %collective-permute-done.20.refs_3_, ...), custom_call_target="tpu_custom_call" | custom-call | tf_op jit(solution)/shard_map/pallas_call | solution.py:40
  (40 shorter events, 6.1 us)
Async XLA Ops:
  1.0 12.6 %collective-permute-start.1 = (bf16[16,3712]{1,0:T(8,128)(2,1)S(1)}, bf16[16,3712]{1,0:T(8,128)(2,1)S(1)}, u32[]{:S(2)}, u32[]{:S(2)}) collective-permute-start(bf16[16,3712]{1,0:T(8,128)(2,1)S(1)} %shard_map.91.refs_2_.refs_0_), channel_id=1, source_target_pairs={{0,4},{1,5},{2,6},{3,7},{4,0},{5,1},{6,2},{7,3},{8,12},{9,13},{10,... | collective-permute-start | bytes 356360 | tf_op jit(solution)/shard_map/ppermute | solution.py:318
  5.1 9.1 %collective-permute-start = (bf16[16,3712]{1,0:T(8,128)(2,1)S(1)}, bf16[16,3712]{1,0:T(8,128)(2,1)S(1)}, u32[]{:S(2)}, u32[]{:S(2)}) collective-permute-start(bf16[16,3712]{1,0:T(8,128)(2,1)S(1)} %shard_map.91.refs_2_.refs_0_), channel_id=1, source_target_pairs={{0,2},{1,3},{2,0},{3,1},{4,6},{5,7},{6,4},{7,5},{8,10},{9,11},{10,... | collective-permute-start | bytes 356360 | tf_op jit(solution)/shard_map/ppermute | solution.py:318
  6.6 7.9 %collective-permute-start.2 = (bf16[16,3712]{1,0:T(8,128)(2,1)S(1)}, bf16[16,3712]{1,0:T(8,128)(2,1)S(1)}, u32[]{:S(2)}, u32[]{:S(2)}) collective-permute-start(bf16[16,3712]{1,0:T(8,128)(2,1)S(1)} %shard_map.91.refs_2_.refs_0_), channel_id=1, source_target_pairs={{0,6},{1,7},{2,4},{3,5},{4,2},{5,3},{6,0},{7,1},{8,14},{9,15},{10,... | collective-permute-start | bytes 356360 | tf_op jit(solution)/shard_map/ppermute | solution.py:318
  6.6 8.0 %collective-permute-start.3 = (bf16[16,3712]{1,0:T(8,128)(2,1)S(1)}, bf16[16,3712]{1,0:T(8,128)(2,1)S(1)}, u32[]{:S(2)}, u32[]{:S(2)}) collective-permute-start(bf16[16,3712]{1,0:T(8,128)(2,1)S(1)} %shard_map.91.refs_2_.refs_0_), channel_id=1, source_target_pairs={{0,1},{1,0},{2,3},{3,2},{4,5},{5,4},{6,7},{7,6},{8,9},{9,8},{10,11... | collective-permute-start | bytes 356360 | tf_op jit(solution)/shard_map/ppermute | solution.py:318
  8.4 6.9 %collective-permute-start.4 = (bf16[16,3712]{1,0:T(8,128)(2,1)S(1)}, bf16[16,3712]{1,0:T(8,128)(2,1)S(1)}, u32[]{:S(2)}, u32[]{:S(2)}) collective-permute-start(bf16[16,3712]{1,0:T(8,128)(2,1)S(1)} %shard_map.91.refs_2_.refs_0_), channel_id=1, source_target_pairs={{0,8},{1,9},{2,10},{3,11},{4,12},{5,13},{6,14},{7,15},{8,0},{9,1},... | collective-permute-start | bytes 356360 | tf_op jit(solution)/shard_map/ppermute | solution.py:318
  13.6 1.9 %collective-permute-start.6 = (bf16[16,3712]{1,0:T(8,128)(2,1)S(1)}, bf16[16,3712]{1,0:T(8,128)(2,1)S(1)}, u32[]{:S(2)}, u32[]{:S(2)}) collective-permute-start(bf16[16,3712]{1,0:T(8,128)(2,1)S(1)} %collective-permute-done.1.refs_2_), channel_id=1, source_target_pairs={{0,8},{1,9},{2,10},{3,11},{4,12},{5,13},{6,14},{7,15},{8,0},{9,1},... | collective-permute-start | bytes 356360 | tf_op jit(solution)/shard_map/ppermute | solution.py:318
  14.2 1.3 %collective-permute-start.5 = (bf16[16,3712]{1,0:T(8,128)(2,1)S(1)}, bf16[16,3712]{1,0:T(8,128)(2,1)S(1)}, u32[]{:S(2)}, u32[]{:S(2)}) collective-permute-start(bf16[16,3712]{1,0:T(8,128)(2,1)S(1)} %collective-permute-done.refs_1_), channel_id=1, source_target_pairs={{0,8},{1,9},{2,10},{3,11},{4,12},{5,13},{6,14},{7,15},{8,0},{9,1},... | collective-permute-start | bytes 356360 | tf_op jit(solution)/shard_map/ppermute | solution.py:318
  14.6 1.3 %collective-permute-start.7 = (bf16[16,3712]{1,0:T(8,128)(2,1)S(1)}, bf16[16,3712]{1,0:T(8,128)(2,1)S(1)}, u32[]{:S(2)}, u32[]{:S(2)}) collective-permute-start(bf16[16,3712]{1,0:T(8,128)(2,1)S(1)} %collective-permute-done.2.refs_3_), channel_id=1, source_target_pairs={{0,8},{1,9},{2,10},{3,11},{4,12},{5,13},{6,14},{7,15},{8,0},{9,1},... | collective-permute-start | bytes 356360 | tf_op jit(solution)/shard_map/ppermute | solution.py:318
  16.5 8.0 %collective-permute-start.11 = (bf16[32,3584]{1,0:T(8,128)(2,1)S(1)}, bf16[32,3584]{1,0:T(8,128)(2,1)S(1)}, u32[]{:S(2)}, u32[]{:S(2)}) collective-permute-start(bf16[32,3584]{1,0:T(8,128)(2,1)S(1)} %get-tuple-element.63), channel_id=1, source_target_pairs={{0,1},{1,0},{2,3},{3,2},{4,5},{5,4},{6,7},{7,6},{8,9},{9,8},{10,11... | collective-permute-start | bytes 688136 | tf_op jit(solution)/shard_map/ppermute | solution.py:318
  18.6 12.9 %collective-permute-start.12 = (bf16[32,3584]{1,0:T(8,128)(2,1)S(1)}, bf16[32,3584]{1,0:T(8,128)(2,1)S(1)}, u32[]{:S(2)}, u32[]{:S(2)}) collective-permute-start(bf16[32,3584]{1,0:T(8,128)(2,1)S(1)} %get-tuple-element.62), channel_id=1, source_target_pairs={{0,16},{1,17},{2,18},{3,19},{4,20},{5,21},{6,22},{7,23},{8,24},{9,... | collective-permute-start | bytes 688136 | tf_op jit(solution)/shard_map/ppermute | solution.py:318
  20.1 11.5 %collective-permute-start.13 = (bf16[32,3584]{1,0:T(8,128)(2,1)S(1)}, bf16[32,3584]{1,0:T(8,128)(2,1)S(1)}, u32[]{:S(2)}, u32[]{:S(2)}) collective-permute-start(bf16[32,3584]{1,0:T(8,128)(2,1)S(1)} %get-tuple-element.64), channel_id=1, source_target_pairs={{0,17},{1,16},{2,19},{3,18},{4,21},{5,20},{6,23},{7,22},{8,25},{9,... | collective-permute-start | bytes 688136 | tf_op jit(solution)/shard_map/ppermute | solution.py:318
  20.1 15.8 %collective-permute-start.8 = (bf16[16,3712]{1,0:T(8,128)(2,1)S(1)}, bf16[16,3712]{1,0:T(8,128)(2,1)S(1)}, u32[]{:S(2)}, u32[]{:S(2)}) collective-permute-start(bf16[16,3712]{1,0:T(8,128)(2,1)S(1)} %collective-permute-done.3.refs_4_), channel_id=1, source_target_pairs={{0,4},{1,5},{2,6},{3,7},{4,0},{5,1},{6,2},{7,3},{8,12},{9,13},{10,... | collective-permute-start | bytes 356360 | tf_op jit(solution)/shard_map/ppermute | solution.py:318
  24.0 13.1 %collective-permute-start.9 = (bf16[16,3712]{1,0:T(8,128)(2,1)S(1)}, bf16[16,3712]{1,0:T(8,128)(2,1)S(1)}, u32[]{:S(2)}, u32[]{:S(2)}) collective-permute-start(bf16[16,3712]{1,0:T(8,128)(2,1)S(1)} %collective-permute-done.3.refs_4_), channel_id=1, source_target_pairs={{0,2},{1,3},{2,0},{3,1},{4,6},{5,7},{6,4},{7,5},{8,10},{9,11},{10,... | collective-permute-start | bytes 356360 | tf_op jit(solution)/shard_map/ppermute | solution.py:318
  24.5 14.3 %collective-permute-start.10 = (bf16[16,3712]{1,0:T(8,128)(2,1)S(1)}, bf16[16,3712]{1,0:T(8,128)(2,1)S(1)}, u32[]{:S(2)}, u32[]{:S(2)}) collective-permute-start(bf16[16,3712]{1,0:T(8,128)(2,1)S(1)} %collective-permute-done.3.refs_4_), channel_id=1, source_target_pairs={{0,6},{1,7},{2,4},{3,5},{4,2},{5,3},{6,0},{7,1},{8,14},{9,15},{10,... | collective-permute-start | bytes 356360 | tf_op jit(solution)/shard_map/ppermute | solution.py:318
  34.3 5.2 %collective-permute-start.14 = (bf16[32,1792]{1,0:T(8,128)(2,1)S(1)}, bf16[32,1792]{1,0:T(8,128)(2,1)S(1)}, u32[]{:S(2)}, u32[]{:S(2)}) collective-permute-start(bf16[32,1792]{1,0:T(8,128)(2,1)S(1)} %get-tuple-element.86), channel_id=1, source_target_pairs={{0,16},{1,17},{2,18},{3,19},{4,20},{5,21},{6,22},{7,23},{8,24},{9,... | collective-permute-start | bytes 344072 | tf_op jit(solution)/shard_map/ppermute | solution.py:318
  35.9 6.0 %collective-permute-start.15 = (bf16[32,1792]{1,0:T(8,128)(2,1)S(1)}, bf16[32,1792]{1,0:T(8,128)(2,1)S(1)}, u32[]{:S(2)}, u32[]{:S(2)}) collective-permute-start(bf16[32,1792]{1,0:T(8,128)(2,1)S(1)} %get-tuple-element.87), channel_id=1, source_target_pairs={{0,24},{1,25},{2,26},{3,27},{4,28},{5,29},{6,30},{7,31},{8,16},{9,... | collective-permute-start | bytes 344072 | tf_op jit(solution)/shard_map/ppermute | solution.py:318
  35.9 6.0 %collective-permute-start.16 = (bf16[32,1792]{1,0:T(8,128)(2,1)S(1)}, bf16[32,1792]{1,0:T(8,128)(2,1)S(1)}, u32[]{:S(2)}, u32[]{:S(2)}) collective-permute-start(bf16[32,1792]{1,0:T(8,128)(2,1)S(1)} %get-tuple-element.88), channel_id=1, source_target_pairs={{0,8},{1,9},{2,10},{3,11},{4,12},{5,13},{6,14},{7,15},{8,0},{9,1},... | collective-permute-start | bytes 344072 | tf_op jit(solution)/shard_map/ppermute | solution.py:318
  37.2 7.2 %collective-permute-start.21 = (bf16[32,1792]{1,0:T(8,128)(2,1)S(1)}, bf16[32,1792]{1,0:T(8,128)(2,1)S(1)}, u32[]{:S(2)}, u32[]{:S(2)}) collective-permute-start(bf16[32,1792]{1,0:T(8,128)(2,1)S(1)} %get-tuple-element.98), channel_id=1, source_target_pairs={{0,16},{1,17},{2,18},{3,19},{4,20},{5,21},{6,22},{7,23},{8,24},{9,... | collective-permute-start | bytes 344072 | tf_op jit(solution)/shard_map/ppermute | solution.py:318
  38.8 7.5 %collective-permute-start.22 = (bf16[32,1792]{1,0:T(8,128)(2,1)S(1)}, bf16[32,1792]{1,0:T(8,128)(2,1)S(1)}, u32[]{:S(2)}, u32[]{:S(2)}) collective-permute-start(bf16[32,1792]{1,0:T(8,128)(2,1)S(1)} %get-tuple-element.99), channel_id=1, source_target_pairs={{0,24},{1,25},{2,26},{3,27},{4,28},{5,29},{6,30},{7,31},{8,16},{9,... | collective-permute-start | bytes 344072 | tf_op jit(solution)/shard_map/ppermute | solution.py:318
  39.5 6.8 %collective-permute-start.23 = (bf16[32,1792]{1,0:T(8,128)(2,1)S(1)}, bf16[32,1792]{1,0:T(8,128)(2,1)S(1)}, u32[]{:S(2)}, u32[]{:S(2)}) collective-permute-start(bf16[32,1792]{1,0:T(8,128)(2,1)S(1)} %get-tuple-element.100), channel_id=1, source_target_pairs={{0,8},{1,9},{2,10},{3,11},{4,12},{5,13},{6,14},{7,15},{8,0},{9,1},... | collective-permute-start | bytes 344072 | tf_op jit(solution)/shard_map/ppermute | solution.py:318
  42.3 7.4 %collective-permute-start.17 = (bf16[64,1792]{1,0:T(8,128)(2,1)S(1)}, bf16[64,1792]{1,0:T(8,128)(2,1)S(1)}, u32[]{:S(2)}, u32[]{:S(2)}) collective-permute-start(bf16[64,1792]{1,0:T(8,128)(2,1)S(1)} %get-tuple-element.90), channel_id=1, source_target_pairs={{0,1},{1,0},{2,3},{3,2},{4,5},{5,4},{6,7},{7,6},{8,9},{9,8},{10,11... | collective-permute-start | bytes 688136 | tf_op jit(solution)/shard_map/ppermute | solution.py:318
  46.6 8.0 %collective-permute-start.24 = (bf16[64,1792]{1,0:T(8,128)(2,1)S(1)}, bf16[64,1792]{1,0:T(8,128)(2,1)S(1)}, u32[]{:S(2)}, u32[]{:S(2)}) collective-permute-start(bf16[64,1792]{1,0:T(8,128)(2,1)S(1)} %get-tuple-element.102), channel_id=1, source_target_pairs={{0,1},{1,0},{2,3},{3,2},{4,5},{5,4},{6,7},{7,6},{8,9},{9,8},{10,11... | collective-permute-start | bytes 688136 | tf_op jit(solution)/shard_map/ppermute | solution.py:318
  49.8 7.9 %collective-permute-start.18 = (bf16[16,1792]{1,0:T(8,128)(2,1)S(1)}, bf16[16,1792]{1,0:T(8,128)(2,1)S(1)}, u32[]{:S(2)}, u32[]{:S(2)}) collective-permute-start(bf16[16,1792]{1,0:T(8,128)(2,1)S(1)} %get-tuple-element.92), channel_id=1, source_target_pairs={{0,6},{1,7},{2,4},{3,5},{4,2},{5,3},{6,0},{7,1},{8,14},{9,15},{10,... | collective-permute-start | bytes 172040 | tf_op jit(solution)/shard_map/ppermute | solution.py:318
  52.2 7.0 %collective-permute-start.19 = (bf16[16,1792]{1,0:T(8,128)(2,1)S(1)}, bf16[16,1792]{1,0:T(8,128)(2,1)S(1)}, u32[]{:S(2)}, u32[]{:S(2)}) collective-permute-start(bf16[16,1792]{1,0:T(8,128)(2,1)S(1)} %get-tuple-element.93), channel_id=1, source_target_pairs={{0,4},{1,5},{2,6},{3,7},{4,0},{5,1},{6,2},{7,3},{8,12},{9,13},{10,... | collective-permute-start | bytes 172040 | tf_op jit(solution)/shard_map/ppermute | solution.py:318
  52.7 6.4 %collective-permute-start.20 = (bf16[16,1792]{1,0:T(8,128)(2,1)S(1)}, bf16[16,1792]{1,0:T(8,128)(2,1)S(1)}, u32[]{:S(2)}, u32[]{:S(2)}) collective-permute-start(bf16[16,1792]{1,0:T(8,128)(2,1)S(1)} %get-tuple-element.94), channel_id=1, source_target_pairs={{0,2},{1,3},{2,0},{3,1},{4,6},{5,7},{6,4},{7,5},{8,10},{9,11},{10,... | collective-permute-start | bytes 172040 | tf_op jit(solution)/shard_map/ppermute | solution.py:318
  54.7 6.5 %collective-permute-start.25 = (bf16[16,1792]{1,0:T(8,128)(2,1)S(1)}, bf16[16,1792]{1,0:T(8,128)(2,1)S(1)}, u32[]{:S(2)}, u32[]{:S(2)}) collective-permute-start(bf16[16,1792]{1,0:T(8,128)(2,1)S(1)} %get-tuple-element.104), channel_id=1, source_target_pairs={{0,6},{1,7},{2,4},{3,5},{4,2},{5,3},{6,0},{7,1},{8,14},{9,15},{10,... | collective-permute-start | bytes 172040 | tf_op jit(solution)/shard_map/ppermute | solution.py:318
  57.1 6.0 %collective-permute-start.26 = (bf16[16,1792]{1,0:T(8,128)(2,1)S(1)}, bf16[16,1792]{1,0:T(8,128)(2,1)S(1)}, u32[]{:S(2)}, u32[]{:S(2)}) collective-permute-start(bf16[16,1792]{1,0:T(8,128)(2,1)S(1)} %get-tuple-element.105), channel_id=1, source_target_pairs={{0,4},{1,5},{2,6},{3,7},{4,0},{5,1},{6,2},{7,3},{8,12},{9,13},{10,... | collective-permute-start | bytes 172040 | tf_op jit(solution)/shard_map/ppermute | solution.py:318
  57.6 5.5 %collective-permute-start.27 = (bf16[16,1792]{1,0:T(8,128)(2,1)S(1)}, bf16[16,1792]{1,0:T(8,128)(2,1)S(1)}, u32[]{:S(2)}, u32[]{:S(2)}) collective-permute-start(bf16[16,1792]{1,0:T(8,128)(2,1)S(1)} %get-tuple-element.106), channel_id=1, source_target_pairs={{0,2},{1,3},{2,0},{3,1},{4,6},{5,7},{6,4},{7,5},{8,10},{9,11},{10,... | collective-permute-start | bytes 172040 | tf_op jit(solution)/shard_map/ppermute | solution.py:318
